TPU v7x, 512 devices: a whole 4x8x8 slice. The times are simulated.
512 devices in a mesh: seq: 64 (over z, x, core), chan: 8 (over y).
Axes of the slice: x: 4, y: 8, z: 8, core: 2. Of those that a mesh axis runs over, the one named last changes fastest.
Arguments:
- gate_input: bfloat16 [4096, 4096], P('seq', 'chan'), may hold values from -6 to 6
- key_input: bfloat16 [4096, 4096], P('seq', 'chan'), may hold values from -6 to 6
- value_input: bfloat16 [4096, 4096], P('seq', 'chan'), may hold values from -6 to 6
- decay_rate: float32 [16, 4096], P(None, 'chan'), may hold values from 0.00024414062 to 0.1
- residue: float32 [16, 4096], P(None, 'chan'), may hold values from -1.5 to 1.5
- skip_gain: float32 [4096], P('chan'), may hold values from -3 to 3
- out_weight: bfloat16 [4096, 4096], P('chan', 'seq'), may hold values from -0.25 to 0.25
Outputs:
- mixed: bfloat16 [4096, 4096], P('seq', 'chan')
All inputs are finite; a program needn't handle non-finite values.
Results may differ from a plain program's by a relative error of at most 0.014.
Values may be sent and summed in bfloat16 or wider, within the bound.
No kernel may reach another device: no remote copies, remote signals or barrier semaphores. Data moves between devices by JAX's collectives and lax.ppermute only.
A program may use at most 64 MiB of HBM per device.

v0:
```python
import math

import jax
import jax.numpy as jnp
from jax import lax
from jax.sharding import Mesh
from jax.sharding import PartitionSpec as P

SEQ = ("seq_0", "seq_1", "seq_2")


def laid_out(blocks, dim):
    blocks = jnp.moveaxis(blocks, 0, dim)
    lengths = blocks.shape
    return blocks.reshape(*lengths[:dim], lengths[dim] * lengths[dim + 1], *lengths[dim + 2 :])


def gather_in_order(x, axes, order):
    blocks = x
    for k in order:
        blocks = lax.all_gather(blocks, axes[k])
    done = order[::-1]
    back = [done.index(k) for k in range(len(axes))]
    blocks = blocks.transpose(*back, *range(len(axes), blocks.ndim))
    return blocks.reshape(-1, *x.shape)


def gather_axes(x, axes, order, dim):
    return laid_out(gather_in_order(x, axes, order), dim)


def split_up(x, dim, size):
    lengths = x.shape
    blocks = x.reshape(*lengths[:dim], size, lengths[dim] // size, *lengths[dim + 1 :])
    return jnp.moveaxis(blocks, dim, 0)


def sent_and_summed(x, axis, dim):
    size = lax.axis_size(axis)
    blocks = lax.all_to_all(split_up(x, dim, size), axis, 0, 0, tiled=True)
    return jnp.sum(blocks.astype(jnp.float32), axis=0)


def phase_table(row_ids, col_ids, modulus, direction):
    turns = row_ids[:, None] * col_ids[None, :] % modulus
    angle = direction * 2.0 * math.pi / modulus * turns.astype(jnp.float32)
    return (jnp.cos(angle), jnp.sin(angle))


def complex_mix(pattern, table, real_part, imag_part):

    def contract(left, right):
        return jnp.einsum(pattern, left, right, precision=lax.Precision.HIGHEST)

    return (
        contract(table[0], real_part) - contract(table[1], imag_part),
        contract(table[0], imag_part) + contract(table[1], real_part),
    )


def complex_times(left_real, left_imag, right_real, right_imag):
    return (
        left_real * right_real - left_imag * right_imag,
        left_real * right_imag + left_imag * right_real,
    )


def transposed_conv(signal, decay_rate, amplitude):
    devices = lax.axis_size(SEQ)
    seq_index = lax.axis_index(SEQ)
    row_count, col_count = signal.shape
    own_cols = col_count // devices
    total_rows = row_count * devices
    padded_len = 2 * total_rows
    outer = 2 * devices
    columns = lax.all_to_all(signal, SEQ, split_axis=1, concat_axis=0, tiled=True)
    rates = lax.dynamic_slice_in_dim(decay_rate, seq_index * own_cols, own_cols, 1)
    amps = lax.dynamic_slice_in_dim(amplitude, seq_index * own_cols, own_cols, 1)
    positions = jnp.arange(total_rows, dtype=jnp.int32).astype(jnp.float32)

    def add_mode(mode_index, totals):
        return totals + amps[mode_index][None, :] * jnp.exp(
            -rates[mode_index][None, :] * positions[:, None]
        )

    response = lax.fori_loop(
        0, rates.shape[0], add_mode, jnp.zeros((total_rows, own_cols), jnp.float32)
    )
    stacked = jnp.concatenate([columns, response], axis=1)
    shaped = stacked.reshape(row_count // 2, outer, 2 * own_cols)
    half_ids = jnp.arange(row_count // 2, dtype=jnp.int32)
    inner_ids = jnp.arange(row_count, dtype=jnp.int32)
    outer_ids = jnp.arange(outer, dtype=jnp.int32)
    first_table = phase_table(inner_ids, half_ids, row_count, -1.0)
    step_real = jnp.einsum("kn,nac->kac", first_table[0], shaped, precision=lax.Precision.HIGHEST)
    step_imag = jnp.einsum("kn,nac->kac", first_table[1], shaped, precision=lax.Precision.HIGHEST)
    twiddle = phase_table(inner_ids, outer_ids, padded_len, -1.0)
    step_real, step_imag = complex_times(
        step_real, step_imag, twiddle[0][:, :, None], twiddle[1][:, :, None]
    )
    spec_real, spec_imag = complex_mix(
        "ja,kac->kjc", phase_table(outer_ids, outer_ids, outer, -1.0), step_real, step_imag
    )
    prod_real, prod_imag = complex_times(
        spec_real[..., :own_cols],
        spec_imag[..., :own_cols],
        spec_real[..., own_cols:],
        spec_imag[..., own_cols:],
    )
    back_real, back_imag = complex_mix(
        "aj,kjc->kac", phase_table(outer_ids, outer_ids, outer, 1.0), prod_real, prod_imag
    )
    twiddle_back = phase_table(inner_ids, outer_ids, padded_len, 1.0)
    back_real, back_imag = complex_times(
        back_real, back_imag, twiddle_back[0][:, :, None], twiddle_back[1][:, :, None]
    )
    last_table = phase_table(half_ids, inner_ids, row_count, 1.0)
    result = jnp.einsum(
        "mk,kac->mac", last_table[0], back_real, precision=lax.Precision.HIGHEST
    ) - jnp.einsum("mk,kac->mac", last_table[1], back_imag, precision=lax.Precision.HIGHEST)
    convolved_cols = result.reshape(total_rows, own_cols) * (1.0 / padded_len)
    return lax.all_to_all(convolved_cols, SEQ, split_axis=0, concat_axis=1, tiled=True)


def body(gate_input, key_input, value_input, decay_rate, residue, skip_gain, out_weight):
    signal = key_input.astype(jnp.float32) * value_input.astype(jnp.float32)
    amplitude = residue * jnp.sqrt(-jnp.expm1(-2.0 * decay_rate))
    convolved = transposed_conv(signal, decay_rate, amplitude)
    gated_rows = (
        gate_input.astype(jnp.float32) * (convolved + skip_gain[None, :] * signal)
    ).astype(jnp.bfloat16)
    partials = jnp.dot(
        gated_rows, gather_axes(out_weight, SEQ, (1, 0, 2), 1), preferred_element_type=jnp.float32
    )
    summed = sent_and_summed(partials.astype(jnp.bfloat16), "chan", 1)
    return summed.astype(jnp.bfloat16)


def solution(mesh):
    finer = Mesh(
        mesh.devices.reshape(8, 4, 2, mesh.shape["chan"]), ("seq_0", "seq_1", "seq_2", "chan")
    )
    return jax.shard_map(
        body,
        mesh=finer,
        in_specs=(
            P(SEQ, "chan"),
            P(SEQ, "chan"),
            P(SEQ, "chan"),
            P(None, "chan"),
            P(None, "chan"),
            P("chan"),
            P("chan", SEQ),
        ),
        out_specs=P(SEQ, "chan"),
        check_vma=False,
    )
```

profile of v0, /device:TPU:1, one launch (start us, length us, event | category | flops | bytes accessed | tf_op | source)
XLA Modules:
  0.0 137.6 jit_solution(7889716281706167657)
XLA Ops:
  6.5 10.7 %all-gather = bf16[2048,64]{0,1:T(8,128)(2,1)S(1)} all-gather(bf16[512,64]{0,1:T(8,128)(2,1)} %param.15), channel_id=2, replica_groups=mesh['seq_0'=8,'seq_1'=4,'seq_2'=2,'chan'=8] {'seq_1'}, dimensions={0}, use_global_device_ids=true | all-gather | bytes 327680 | tf_op jit(solution)/shard_map/all_gather | solution.py:21
  17.3 0.7 copy.87
  18.0 1.0 copy.55
  19.0 1.0 copy.54
  20.0 0.8 reshape.96
  20.8 16.3 %all-to-all-start = ((f32[64,1,512]{2,1,0:T(1,128)}), f32[64,1,512]{2,1,0:T(1,128)S(1)}, u32[]{:S(2)}, u32[]{:S(2)}) async-start(f32[64,1,512]{2,1,0:T(1,128)} %reshape.96), calls=%async_computation | async-start | bytes 262144 | tf_op jit(solution)/shard_map/all_to_all | solution.py:76
  37.2 0.8 constant_dynamic-slice_fusion
  38.0 2.8 %while.14 = (s32[]{:T(128)}, f32[4096,8]{0,1:T(8,128)S(1)}, f32[16,8]{1,0:T(8,128)S(1)}, f32[16,8]{1,0:T(8,128)S(1)}, s32[]{:T(128)}, /*index=5*/s32[]{:T(128)}) while((s32[]{:T(128)}, f32[4096,8]{0,1:T(8,128)S(1)}, f32[16,8]{1,0:T(8,128)S(1)}, f32[16,8]{1,0:T(8,128)S(1)}, s32[]{:T(128)}, /*index=5*/s32[]{:T(128)}) %tuple.41), condition=%wide.region_1.0_spmd.clone, body=%wide.region_0.0_spmd.clone.sunk | while | flops 135179 | bytes 295195 | solution.py:86
  41.0 25.4 %all-gather.6.cloned.1.call-done = bf16[32,512,64]{1,2,0:T(8,128)(2,1)} async-done(((bf16[4,512,64]{1,2,0:T(8,128)(2,1)}), bf16[32,512,64]{1,2,0:T(8,128)(2,1)}) %all-gather.6.cloned.1.call-update) | async-done | bytes 2097168 | tf_op jit(solution)/shard_map/all_gather | solution.py:21
  67.0 0.9 reduce.1
  68.3 0.7 fusion.64
  69.0 0.8 multiply_subtract_fusion
  69.8 1.0 fusion.5
  70.9 1.0 fusion.9
  71.9 1.0 fusion.2
  73.0 1.0 fusion.3
  77.7 0.8 reshape.98
  78.5 11.9 %all-to-all-start.1 = ((f32[64,1,512]{2,1,0:T(1,128)}), f32[64,1,512]{2,1,0:T(1,128)S(1)}, u32[]{:S(2)}, u32[]{:S(2)}) async-start(f32[64,1,512]{2,1,0:T(1,128)} %reshape.98), calls=%async_computation.1 | async-start | bytes 262144 | tf_op jit(solution)/shard_map/all_to_all | solution.py:122
  90.6 11.0 %all-to-all-done.1 = f32[64,1,512]{2,1,0:T(1,128)S(1)} async-done(((f32[64,1,512]{2,1,0:T(1,128)}), f32[64,1,512]{2,1,0:T(1,128)S(1)}, u32[]{:S(2)}, u32[]{:S(2)}) %all-to-all-start.1) | async-done | bytes 131104 | tf_op jit(solution)/shard_map/all_to_all | solution.py:122
  101.6 1.0 reduce.2
  102.7 2.7 %copy.65 = bf16[8,4,2,512,64]{3,4,2,1,0:T(8,128)(2,1)S(1)} copy(bf16[8,4,2,512,64]{3,4,1,0,2:T(8,128)(2,1)} %bitcast.115) | data formatting | bytes 8388608 | tf_op jit(solution)/shard_map/transpose | solution.py:24
  105.4 1.5 %convolution_convert_fusion = bf16[64,4096]{1,0:T(8,128)(2,1)S(1)} fusion(bf16[512,4096]{0,1:T(8,128)(2,1)S(1)} %bitcast.113, bf16[64,512]{0,1:T(8,128)(2,1)S(1)} %copy.53, bf16[64,512]{0,1:T(8,128)(2,1)S(1)} %copy.55, bf16[64,512]{0,1:T(8,128)(2,1)S(1)} %copy.54, f32[512]{0:T(512)S(1)} %copy-done.1, f32[64,8,64]{2,1,0:T(8,128)S(1)} %reshape.99), kind=kOutput, calls=%fused_computation.5 | convolution fusion | flops 268959744 | bytes 5048320 | tf_op jit(solution)/shard_map/dot_general | solution.py:132
  107.0 23.1 %all_to_all.37 = bf16[8,64,512]{2,1,0:T(8,128)(2,1)S(1)} all-to-all(bf16[8,64,512]{2,1,0:T(8,128)(2,1)S(1)} %bitcast.118), channel_id=1, replica_groups=mesh['seq_0'=8,'seq_1'=4,'seq_2'=2,'chan'=8] {'chan'}, dimensions={0} | all-to-all | bytes 1048576 | tf_op jit(solution)/shard_map/all_to_all | solution.py:40
  130.0 0.7 reduce_sum.12
  (81 shorter events, 7.3 us)
Async XLA Ops:
  6.5 59.8 %all-gather.6.cloned.1.call-start = ((), (), s32[]{:S(2)}) async-start(), calls=%async_computation.3 | async-start | bytes 2359296 | tf_op jit(solution)/shard_map/all_gather | solution.py:21
  20.8 45.7 %all-to-all-start = ((f32[64,1,512]{2,1,0:T(1,128)}), f32[64,1,512]{2,1,0:T(1,128)S(1)}, u32[]{:S(2)}, u32[]{:S(2)}) async-start(f32[64,1,512]{2,1,0:T(1,128)} %reshape.96), calls=%async_computation | async-start | bytes 262144 | tf_op jit(solution)/shard_map/all_to_all | solution.py:76
  37.2 65.5 %all-gather.8.cloned.1.call-start = ((), (), s32[]{:S(2)}) async-start(), calls=%async_computation.4 | async-start | bytes 6291456 | tf_op jit(solution)/shard_map/all_gather | solution.py:21
  73.0 17.5 %copy-start = (bf16[64,512]{1,0:T(8,128)(2,1)S(1)}, bf16[64,512]{1,0:T(8,128)(2,1)}, u32[]{:S(2)}) copy-start(bf16[64,512]{1,0:T(8,128)(2,1)} %param.9) | copy-start | bytes 196612
  78.5 23.1 %all-to-all-start.1 = ((f32[64,1,512]{2,1,0:T(1,128)}), f32[64,1,512]{2,1,0:T(1,128)S(1)}, u32[]{:S(2)}, u32[]{:S(2)}) async-start(f32[64,1,512]{2,1,0:T(1,128)} %reshape.98), calls=%async_computation.1 | async-start | bytes 262144 | tf_op jit(solution)/shard_map/all_to_all | solution.py:122
  102.7 2.7 %copy-start.1 = (f32[512]{0:T(512)S(1)}, f32[512]{0:T(512)}, u32[]{:S(2)}) copy-start(f32[512]{0:T(512)} %param.14) | copy-start | bytes 6148
Sparse Core Ops, SparseCore 0:
  18.2 48.1 all-gather.5
  68.4 25.5 all-gather.7
where the time goes:
time: 138 us
  waiting for transfers between devices  36.4 us (26%)
  blocking collectives  33.8 us (24%)
  starting transfers between devices  28.3 us (21%)
  between operations  13.7 us (10%)
  matrix products  10.5 us (8%)
  local copies, waits for them, and re-layouts  8.32 us (6%)
  other arithmetic  5.96 us (4%)
    all_gather x2, waiting for transfers between devices, gather_in_order(): blocks = lax.all_gather(blocks, axes[k])  25.4 us
    all_to_all x1, blocking collectives, sent_and_summed(): blocks = lax.all_to_all(split_up(x, dim, size), axis, 0, 0, tiled=True)  23.1 us
    all_to_all x1, starting transfers between devices, transposed_conv(): lax.all_to_all(signal, SEQ, split_axis=1, concat_axis=0, tiled=True)  16.3 us
    all_to_all x1, starting transfers between devices, transposed_conv(): lax.all_to_all(convolved_cols, SEQ, split_axis=0, concat_axis=1, tiled=True)  11.9 us
    all_to_all x1, waiting for transfers between devices, transposed_conv(): lax.all_to_all(convolved_cols, SEQ, split_axis=0, concat_axis=1, tiled=True)  11 us
    all_gather x1, blocking collectives, gather_in_order(): blocks = lax.all_gather(blocks, axes[k])  10.7 us
    dot_general x8, matrix products, contract(): return jnp.einsum(pattern, left, right, precision=lax.Precision.HIGHEST)  6.67 us
    unnamed x12, local copies, waits for them, and re-layouts  3.91 us
  transfers between devices with their start and end apart: 4, of which 2 were waited for; matrix products, arithmetic and copies ran while one was open for 14% of the time, Pallas kernels for 0%

commit v1 on v0

v1 whole, which is shorter than its diff:
```python
import jax
import jax.numpy as jnp
from jax import lax
from jax.experimental import pallas as pl
from jax.experimental.pallas import tpu as pltpu
from jax.sharding import Mesh
from jax.sharding import PartitionSpec as P

F32 = jnp.float32
BF16 = jnp.bfloat16
SEQ = ("z", "x", "core")
LANES = 128
VMEM = pl.BlockSpec(memory_space=pltpu.VMEM)
SMEM = pl.BlockSpec(memory_space=pltpu.SMEM)
PARAMS = pltpu.CompilerParams(vmem_limit_bytes=48 * 1024 * 1024)


def tile_rows():
    return lax.broadcasted_iota(jnp.int32, (8, LANES), 0).astype(F32)


def own_rows_kernel(key_ref, value_ref, rate_ref, amp_ref, skip_ref, base_ref, state_ref):
    rows, width = key_ref.shape
    modes = rate_ref.shape[0]
    tiles = rows // 8
    copies = state_ref.shape[0]

    def slab(index, carry):
        cols = pl.ds(pl.multiple_of(index * LANES, LANES), LANES)
        signal = key_ref[:, cols].astype(F32) * value_ref[:, cols].astype(F32)
        rate = rate_ref[:, cols]
        amp = amp_ref[:, cols]
        steps = [jnp.exp(-8.0 * j * rate) for j in range(tiles)]
        scaled = [amp * step for step in steps]
        first = tile_rows()
        taps = [jnp.zeros((8, LANES), F32) for _ in range(tiles)]
        states = []
        for m in range(modes):
            ahead = jnp.exp(-rate[m : m + 1] * first)
            behind = jnp.exp(-rate[m : m + 1] * (7.0 - first))
            held = jnp.zeros((8, LANES), F32)
            for j in range(tiles):
                taps[j] = taps[j] + scaled[j][m : m + 1] * ahead
                held = held + steps[tiles - 1 - j][m : m + 1] * signal[8 * j : 8 * j + 8]
            states.append(jnp.sum(held * behind, axis=0, keepdims=True))
        state = jnp.concatenate(states, axis=0)
        for copy in range(copies):
            state_ref[copy, :, cols] = state
        row_ids = lax.broadcasted_iota(jnp.int32, (rows, LANES), 0)
        totals = [
            skip_ref[0:1, cols] * signal[8 * j : 8 * j + 8] for j in range(tiles)
        ]
        for lag in range(8):
            moved = signal
            if lag:
                moved = jnp.where(row_ids >= lag, pltpu.roll(signal, lag, 0), 0.0)
            for j in range(tiles):
                tap = taps[j][lag : lag + 1]
                for i in range(j, tiles):
                    totals[i] = totals[i] + tap * moved[8 * (i - j) : 8 * (i - j) + 8]
        for j in range(tiles):
            base_ref[8 * j : 8 * j + 8, cols] = totals[j]
        return carry

    lax.fori_loop(0, width // LANES, slab, 0)


def row_block_kernel(rows, where_ref, states_ref, rate_ref, before_ref, total_ref):
    own = where_ref[0]
    decay = jnp.exp(-float(rows) * rate_ref[...])
    running = jnp.zeros(rate_ref.shape, F32)
    before = jnp.zeros(rate_ref.shape, F32)
    for j in range(states_ref.shape[0]):
        before = jnp.where(own == j, running, before)
        running = decay * running + states_ref[j]
    before_ref[...] = before
    for copy in range(total_ref.shape[0]):
        total_ref[copy] = running


def gate_kernel(
    rows, where_ref, totals_ref, before_ref, rate_ref, amp_ref, base_ref, gate_ref, gated_ref
):
    own = where_ref[0].astype(F32)
    block = where_ref[1]
    blocks, modes, width = totals_ref.shape
    tiles = rows // 8

    def slab(index, carry):
        cols = pl.ds(pl.multiple_of(index * LANES, LANES), LANES)
        rate = rate_ref[:, cols]
        decay = jnp.exp(-float(rows * 8) * rate)
        running = jnp.zeros((modes, LANES), F32)
        entering = jnp.zeros((modes, LANES), F32)
        for z in range(blocks):
            entering = jnp.where(block == z, running, entering)
            running = decay * running + totals_ref[z, :, cols]
        state = before_ref[:, cols] + jnp.exp(-float(rows) * own * rate) * entering
        state = state * amp_ref[:, cols]
        scaled = [state * jnp.exp(-8.0 * j * rate) for j in range(tiles)]
        first = tile_rows() + 1.0
        totals = [base_ref[8 * j : 8 * j + 8, cols] for j in range(tiles)]
        for m in range(modes):
            ahead = jnp.exp(-rate[m : m + 1] * first)
            for j in range(tiles):
                totals[j] = totals[j] + scaled[j][m : m + 1] * ahead
        result = jnp.concatenate(totals, axis=0)
        gated_ref[:, cols] = (gate_ref[:, cols].astype(F32) * result).astype(BF16)
        return carry

    lax.fori_loop(0, width // LANES, slab, 0)


def project_kernel(gated_ref, weight_ref, out_ref):
    cores, rows, depth = gated_ref.shape
    gated = gated_ref[...].reshape(cores * rows, depth)
    weight = weight_ref[...].reshape(-1, depth)
    part = lax.dot_general(
        gated, weight, (((1,), (1,)), ((), ())), preferred_element_type=F32
    ).astype(BF16)
    out_ref[...] = part.reshape(out_ref.shape)


def sum_kernel(parts_ref, out_ref):
    groups, cores, rows, width = parts_ref.shape
    unit = out_ref.shape[1] // (width // 64 * cores)
    totals = []
    for core in range(cores):
        total = parts_ref[0, core].astype(F32)
        for j in range(1, groups):
            total = total + parts_ref[j, core].astype(F32)
        totals.append(total)
    pieces = []
    for j in range(width // unit):
        for core in range(cores):
            pieces.append(totals[core][:, j * unit : (j + 1) * unit])
    out_ref[...] = jnp.concatenate(pieces, axis=1).astype(BF16)


def exchange(x, axes):
    return lax.all_to_all(x, axes, 0, 0, tiled=True)


def body(gate_input, key_input, value_input, decay_rate, residue, skip_gain, out_weight):
    rows, width = key_input.shape
    modes = decay_rate.shape[0]
    z_size, x_size, y_size = (lax.axis_size(a) for a in ("z", "x", "chan"))
    cores = lax.axis_size("core")
    out_cols = out_weight.shape[1]
    where = jnp.stack([lax.axis_index(("x", "core")), lax.axis_index("z")]).astype(jnp.int32)

    own_weight = jnp.broadcast_to(out_weight.T[None], (z_size, out_cols, width))
    weight_z = exchange(own_weight, "z")
    weight = exchange(jnp.broadcast_to(weight_z[None], (x_size,) + weight_z.shape), "x")
    weight = weight.reshape(x_size, z_size, out_cols, width)

    amplitude = residue * jnp.sqrt(-jnp.expm1(-2.0 * decay_rate))
    base, states = pl.pallas_call(
        own_rows_kernel,
        out_shape=(
            jax.ShapeDtypeStruct((rows, width), F32),
            jax.ShapeDtypeStruct((x_size * cores, modes, width), F32),
        ),
        in_specs=[VMEM] * 5,
        out_specs=(VMEM, VMEM),
        compiler_params=PARAMS,
        name="own_rows",
    )(key_input, value_input, decay_rate, amplitude, skip_gain[None, :])
    states = exchange(states, ("x", "core"))
    before, total = pl.pallas_call(
        lambda *refs: row_block_kernel(rows, *refs),
        out_shape=(
            jax.ShapeDtypeStruct((modes, width), F32),
            jax.ShapeDtypeStruct((z_size, modes, width), F32),
        ),
        in_specs=[SMEM, VMEM, VMEM],
        out_specs=(VMEM, VMEM),
        compiler_params=PARAMS,
        name="row_block",
    )(where, states, decay_rate)
    totals = exchange(total, "z")
    gated = pl.pallas_call(
        lambda *refs: gate_kernel(rows, *refs),
        out_shape=jax.ShapeDtypeStruct((rows, width), BF16),
        in_specs=[SMEM] + [VMEM] * 6,
        out_specs=VMEM,
        compiler_params=PARAMS,
        name="gate",
    )(where, totals, before, decay_rate, amplitude, base, gate_input)
    gated = lax.all_gather(gated, "core")
    parts = pl.pallas_call(
        project_kernel,
        grid=(z_size,),
        out_shape=jax.ShapeDtypeStruct((y_size, cores, rows, x_size * out_cols), BF16),
        in_specs=[
            pl.BlockSpec((cores, rows, width), lambda i: (0, 0, 0)),
            pl.BlockSpec((x_size, 1, out_cols, width), lambda i: (0, i, 0, 0)),
        ],
        out_specs=pl.BlockSpec((1, cores, rows, x_size * out_cols), lambda i: (i, 0, 0, 0)),
        compiler_params=PARAMS,
        name="project",
    )(gated, weight)
    parts = parts.reshape(y_size * cores, rows, x_size * out_cols)
    parts = exchange(parts, ("chan", "core")).reshape(y_size, cores, rows, x_size * out_cols)
    return pl.pallas_call(
        sum_kernel,
        out_shape=jax.ShapeDtypeStruct((rows, width), BF16),
        in_specs=[VMEM],
        out_specs=VMEM,
        compiler_params=PARAMS,
        name="sum_parts",
    )(parts)


def solution(mesh):
    finer = Mesh(
        mesh.devices.reshape(8, 4, 2, mesh.shape["chan"]), ("z", "x", "core", "chan")
    )
    return jax.shard_map(
        body,
        mesh=finer,
        in_specs=(
            P(SEQ, "chan"),
            P(SEQ, "chan"),
            P(SEQ, "chan"),
            P(None, "chan"),
            P(None, "chan"),
            P("chan"),
            P("chan", SEQ),
        ),
        out_specs=P(SEQ, "chan"),
        check_vma=False,
    )
```

time: 138 us -> 117 us (0.85)
  blocking collectives: 33.8 us -> 67.3 us
  starting transfers between devices: 28.3 us -> 13.9 us
  waiting for transfers between devices: 36.4 us -> 22.2 us
  between operations: 13.7 us -> 0.07 us
  matrix products: 10.5 us -> 0 us
  Pallas kernels: 0 us -> 5.96 us
  other arithmetic: 5.96 us -> 0.88 us
  local copies, waits for them, and re-layouts: 8.32 us -> 6.33 us
    all_to_all x1 -> x3, blocking collectives: 23.1 us -> 61.7 us  [exchange(): return lax.all_to_all(x, axes, 0, 0, tiled=True)]
    all_gather x2 -> x0, waiting for transfers between devices: 25.4 us -> none  [gather_in_order(): blocks = lax.all_gather(blocks, axes[k])]
    all_to_all x2, starting transfers between devices: 28.3 us -> 13.9 us  [exchange(): return lax.all_to_all(x, axes, 0, 0, tiled=True)]
    all_to_all x2, waiting for transfers between devices: 11 us -> 22.2 us  [exchange(): return lax.all_to_all(x, axes, 0, 0, tiled=True)]
    dot_general x13 -> x0, matrix products: 10.5 us -> none  [the longest x8 6.67 us: contract(): return jnp.einsum(pattern, left, right, precision=lax.Precision.HIGHEST)]
    pallas_call x0 -> x5, Pallas kernels: none -> 5.96 us  [the longest x1 2 us: body(): pl.pallas_call(project_kernel, grid=(z_size,), out_shape=jax.ShapeDtypeSt...]
    all_gather x1, blocking collectives: 10.7 us -> 5.58 us  [body(): gated = lax.all_gather(gated, 'core')]
    transpose x1 -> x0, local copies, waits for them, and re-layouts: 2.68 us -> none  [gather_in_order(): blocks = blocks.transpose(*back, *range(len(axes), blocks.ndim))]
  transfers between devices with their start and end apart: 4 -> 2, of which waited for: 2 -> 2; matrix products, arithmetic and copies ran while one was open for 14% -> 0% of each run, Pallas kernels for 0% -> 1%
where the time goes in v1:
time: 117 us
  blocking collectives  67.3 us (58%)
  waiting for transfers between devices  22.2 us (19%)
  starting transfers between devices  13.9 us (12%)
  local copies, waits for them, and re-layouts  6.33 us (5%)
  Pallas kernels  5.96 us (5%)
    all_to_all x3, blocking collectives, exchange(): return lax.all_to_all(x, axes, 0, 0, tiled=True)  61.7 us
    all_to_all x2, waiting for transfers between devices, exchange(): return lax.all_to_all(x, axes, 0, 0, tiled=True)  22.2 us
    all_to_all x2, starting transfers between devices, exchange(): return lax.all_to_all(x, axes, 0, 0, tiled=True)  13.9 us
    all_gather x1, blocking collectives, body(): gated = lax.all_gather(gated, 'core')  5.58 us
    unnamed x14, local copies, waits for them, and re-layouts  3.88 us
  transfers between devices with their start and end apart: 2, of which 2 were waited for; matrix products, arithmetic and copies ran while one was open for 0% of the time, Pallas kernels for 1%

profile of v1, /device:TPU:1, one launch (start us, length us, event | category | flops | bytes accessed | tf_op | source)
XLA Modules:
  0.0 116.6 jit_solution(5366861264387080851)
XLA Ops:
  0.0 0.8 sqrt_multiply_fusion.amp_ref.refs_4_
  0.8 0.0 copy-start
  0.8 0.7 copy-done
  1.6 0.8 copy-done.3
  2.4 0.8 copy-done.4
  3.2 0.7 copy-done.6
  3.9 1.7 %own_rows.1 = (f32[64,512]{1,0:T(8,128)S(1)}, f32[8,16,512]{2,1,0:T(8,128)}) custom-call(bf16[64,512]{1,0:T(8,128)(2,1)S(1)} %copy-done.3, bf16[64,512]{1,0:T(8,128)(2,1)S(1)} %copy-done.4, f32[16,512]{1,0:T(8,128)S(1)} %copy-done, f32[16,512]{1,0:T(8,128)S(1)} %sqrt_multiply_fusion.amp_ref.refs_4_, f32[1,512]{1,0:T(1,128)S(1)} %bitcast.10), custom_call_target="tpu_custom_call" | custom-call | tf_op jit(solution)/shard_map/own_rows/pallas_call | solution.py:158
  5.6 10.2 %all-to-all-start = ((f32[8,16,512]{2,1,0:T(8,128)}), f32[8,16,512]{2,1,0:T(8,128)S(1)}, u32[]{:S(2)}, u32[]{:S(2)}) async-start(f32[8,16,512]{2,1,0:T(8,128)} %get-tuple-element.9), calls=%async_computation | async-start | bytes 524288 | tf_op jit(solution)/shard_map/all_to_all | solution.py:141
  15.8 0.1 pad_add_fusion.refs_0_
  15.9 6.4 %all-to-all-done.refs_1_ = f32[8,16,512]{2,1,0:T(8,128)S(1)} async-done(((f32[8,16,512]{2,1,0:T(8,128)}), f32[8,16,512]{2,1,0:T(8,128)S(1)}, u32[]{:S(2)}, u32[]{:S(2)}) %all-to-all-start) | async-done | bytes 262176 | tf_op jit(solution)/shard_map/all_to_all | solution.py:141
  22.3 0.8 copy-done.1
  23.1 0.6 row_block.1
  23.7 15.5 %all_to_all.25.refs_1_ = f32[8,16,512]{2,1,0:T(8,128)S(1)} all-to-all(f32[8,16,512]{2,1,0:T(8,128)S(1)} %get-tuple-element.10), channel_id=1, replica_groups=mesh['z'=8,'x'=4,'core'=2,'chan'=8] {'z'}, dimensions={0} | all-to-all | bytes 524288 | tf_op jit(solution)/shard_map/all_to_all | solution.py:141
  39.2 0.9 broadcast_in_dim.7
  40.1 17.0 %all_to_all.26 = bf16[8,64,512]{2,1,0:T(8,128)(2,1)S(1)} all-to-all(bf16[8,64,512]{2,1,0:T(8,128)(2,1)S(1)} %broadcast_in_dim.7), channel_id=1, replica_groups=mesh['z'=8,'x'=4,'core'=2,'chan'=8] {'z'}, dimensions={0} | all-to-all | bytes 1048576 | tf_op jit(solution)/shard_map/all_to_all | solution.py:141
  57.1 1.6 %broadcast_in_dim.8 = bf16[4,8,64,512]{3,2,1,0:T(8,128)(2,1)} broadcast(bf16[8,64,512]{2,1,0:T(8,128)(2,1)S(1)} %all_to_all.26), dimensions={1,2,3} | broadcast | bytes 2621440 | tf_op jit(solution)/shard_map/broadcast_in_dim | solution.py:154
  58.6 3.7 %all-to-all-start.3 = ((bf16[4,8,64,512]{3,2,1,0:T(8,128)(2,1)}), bf16[4,8,64,512]{3,2,1,0:T(8,128)(2,1)S(1)}, u32[]{:S(2)}, u32[]{:S(2)}) async-start(bf16[4,8,64,512]{3,2,1,0:T(8,128)(2,1)} %broadcast_in_dim.8), calls=%async_computation.3 | async-start | bytes 4194304 | tf_op jit(solution)/shard_map/all_to_all | solution.py:141
  62.4 0.0 copy-done.2
  62.4 0.9 gate.1
  63.3 5.6 %all-gather = bf16[128,512]{1,0:T(8,128)(2,1)S(1)} all-gather(bf16[64,512]{1,0:T(8,128)(2,1)S(1)} %gate.1), channel_id=2, replica_groups=mesh['z'=8,'x'=4,'core'=2,'chan'=8] {'core'}, dimensions={0}, use_global_device_ids=true | all-gather | bytes 196608 | tf_op jit(solution)/shard_map/all_gather | solution.py:190
  68.9 15.8 %all-to-all-done.3.weight_ref = bf16[4,8,64,512]{3,2,1,0:T(8,128)(2,1)S(1)} async-done(((bf16[4,8,64,512]{3,2,1,0:T(8,128)(2,1)}), bf16[4,8,64,512]{3,2,1,0:T(8,128)(2,1)S(1)}, u32[]{:S(2)}, u32[]{:S(2)}) %all-to-all-start.3) | async-done | bytes 2097184 | tf_op jit(solution)/shard_map/all_to_all | solution.py:141
  84.7 2.0 %project.1 = bf16[8,2,64,256]{3,2,1,0:T(8,128)(2,1)S(1)} custom-call(bf16[2,64,512]{2,1,0:T(8,128)(2,1)S(1)} %bitcast.9, bf16[4,8,64,512]{3,2,1,0:T(8,128)(2,1)S(1)} %all-to-all-done.3.weight_ref), custom_call_target="tpu_custom_call" | custom-call | tf_op jit(solution)/shard_map/project/pallas_call | solution.py:191
  86.7 29.2 %all_to_all.27 = bf16[16,64,256]{2,1,0:T(8,128)(2,1)S(1)} all-to-all(bf16[16,64,256]{2,1,0:T(8,128)(2,1)S(1)} %bitcast.8), channel_id=1, replica_groups=mesh['z'=8,'x'=4,'core'=2,'chan'=8] {'chan','core'}, dimensions={0} | all-to-all | bytes 1048576 | tf_op jit(solution)/shard_map/all_to_all | solution.py:141
  115.9 0.8 sum_parts.1
  (7 shorter events, 0.0 us)
Async XLA Ops:
  0.8 0.8 copy-start
  1.6 0.8 copy-start.3
  2.4 0.8 copy-start.4
  3.2 0.7 copy-start.6
  5.6 16.7 %all-to-all-start = ((f32[8,16,512]{2,1,0:T(8,128)}), f32[8,16,512]{2,1,0:T(8,128)S(1)}, u32[]{:S(2)}, u32[]{:S(2)}) async-start(f32[8,16,512]{2,1,0:T(8,128)} %get-tuple-element.9), calls=%async_computation | async-start | bytes 524288 | tf_op jit(solution)/shard_map/all_to_all | solution.py:141
  22.3 0.8 copy-start.1
  58.6 3.8 %copy-start.2 = (f32[16,512]{1,0:T(8,128)S(1)}, f32[16,512]{1,0:T(8,128)}, u32[]{:S(2)}) copy-start(f32[16,512]{1,0:T(8,128)} %refs_3_.1) | copy-start | bytes 98308
  58.6 3.8 %copy-start.5 = (bf16[64,512]{1,0:T(8,128)(2,1)S(1)}, bf16[64,512]{1,0:T(8,128)(2,1)}, u32[]{:S(2)}) copy-start(bf16[64,512]{1,0:T(8,128)(2,1)} %refs_6_.1) | copy-start | bytes 196612
  58.6 26.0 %all-to-all-start.3 = ((bf16[4,8,64,512]{3,2,1,0:T(8,128)(2,1)}), bf16[4,8,64,512]{3,2,1,0:T(8,128)(2,1)S(1)}, u32[]{:S(2)}, u32[]{:S(2)}) async-start(bf16[4,8,64,512]{3,2,1,0:T(8,128)(2,1)} %broadcast_in_dim.8), calls=%async_computation.3 | async-start | bytes 4194304 | tf_op jit(solution)/shard_map/all_to_all | solution.py:141

commit v2 on v1

--- a/solution.py
+++ b/solution.py
@@ -10,6 +10,7 @@
 BF16 = jnp.bfloat16
 SEQ = ("z", "x", "core")
 LANES = 128
+SHIFTS = (0, 1, 3, 2)
 VMEM = pl.BlockSpec(memory_space=pltpu.VMEM)
 SMEM = pl.BlockSpec(memory_space=pltpu.SMEM)
 PARAMS = pltpu.CompilerParams(vmem_limit_bytes=48 * 1024 * 1024)
@@ -19,7 +20,9 @@
     return lax.broadcasted_iota(jnp.int32, (8, LANES), 0).astype(F32)
 
 
-def own_rows_kernel(key_ref, value_ref, rate_ref, amp_ref, skip_ref, base_ref, state_ref):
+def own_rows_kernel(
+    key_ref, value_ref, rate_ref, residue_ref, skip_ref, base_ref, state_ref, amp_ref, copy_ref
+):
     rows, width = key_ref.shape
     modes = rate_ref.shape[0]
     tiles = rows // 8
@@ -29,7 +32,9 @@
         cols = pl.ds(pl.multiple_of(index * LANES, LANES), LANES)
         signal = key_ref[:, cols].astype(F32) * value_ref[:, cols].astype(F32)
         rate = rate_ref[:, cols]
-        amp = amp_ref[:, cols]
+        amp = residue_ref[:, cols] * jnp.sqrt(1.0 - jnp.exp(-2.0 * rate))
+        amp_ref[:, cols] = amp
+        copy_ref[:, cols] = rate
         steps = [jnp.exp(-8.0 * j * rate) for j in range(tiles)]
         scaled = [amp * step for step in steps]
         first = tile_rows()
@@ -111,30 +116,33 @@
     lax.fori_loop(0, width // LANES, slab, 0)
 
 
-def project_kernel(gated_ref, weight_ref, out_ref):
+def project_kernel(gated_ref, *refs):
+    weight_refs, out_ref = refs[:-1], refs[-1]
     cores, rows, depth = gated_ref.shape
     gated = gated_ref[...].reshape(cores * rows, depth)
-    weight = weight_ref[...].reshape(-1, depth)
-    part = lax.dot_general(
-        gated, weight, (((1,), (1,)), ((), ())), preferred_element_type=F32
-    ).astype(BF16)
-    out_ref[...] = part.reshape(out_ref.shape)
-
-
-def sum_kernel(parts_ref, out_ref):
+    for j in range(out_ref.shape[0]):
+        weight = jnp.concatenate([ref[j] for ref in weight_refs], axis=0)
+        part = lax.dot_general(
+            gated, weight, (((1,), (1,)), ((), ())), preferred_element_type=F32
+        ).astype(BF16)
+        out_ref[j] = part.reshape(out_ref.shape[1:])
+
+
+def sum_kernel(where_ref, parts_ref, out_ref):
     groups, cores, rows, width = parts_ref.shape
-    unit = out_ref.shape[1] // (width // 64 * cores)
+    unit = out_ref.shape[1] // (len(SHIFTS) * cores)
+    own_x = where_ref[2]
     totals = []
     for core in range(cores):
         total = parts_ref[0, core].astype(F32)
         for j in range(1, groups):
             total = total + parts_ref[j, core].astype(F32)
         totals.append(total)
-    pieces = []
-    for j in range(width // unit):
-        for core in range(cores):
-            pieces.append(totals[core][:, j * unit : (j + 1) * unit])
-    out_ref[...] = jnp.concatenate(pieces, axis=1).astype(BF16)
+    for j, shift in enumerate(SHIFTS):
+        pieces = [total[:, j * unit : (j + 1) * unit] for total in totals]
+        source = lax.rem(own_x + (len(SHIFTS) - shift), len(SHIFTS))
+        place = pl.multiple_of(source * (cores * unit), cores * unit)
+        out_ref[:, pl.ds(place, cores * unit)] = jnp.concatenate(pieces, axis=1).astype(BF16)
 
 
 def exchange(x, axes):
@@ -147,25 +155,31 @@
     z_size, x_size, y_size = (lax.axis_size(a) for a in ("z", "x", "chan"))
     cores = lax.axis_size("core")
     out_cols = out_weight.shape[1]
-    where = jnp.stack([lax.axis_index(("x", "core")), lax.axis_index("z")]).astype(jnp.int32)
+    where = jnp.stack(
+        [lax.axis_index(("x", "core")), lax.axis_index("z"), lax.axis_index("x")]
+    ).astype(jnp.int32)
 
     own_weight = jnp.broadcast_to(out_weight.T[None], (z_size, out_cols, width))
     weight_z = exchange(own_weight, "z")
-    weight = exchange(jnp.broadcast_to(weight_z[None], (x_size,) + weight_z.shape), "x")
-    weight = weight.reshape(x_size, z_size, out_cols, width)
-
-    amplitude = residue * jnp.sqrt(-jnp.expm1(-2.0 * decay_rate))
-    base, states = pl.pallas_call(
+    state_shape = jax.ShapeDtypeStruct((modes, width), F32)
+    base, states, amplitude, rate = pl.pallas_call(
         own_rows_kernel,
         out_shape=(
             jax.ShapeDtypeStruct((rows, width), F32),
             jax.ShapeDtypeStruct((x_size * cores, modes, width), F32),
+            state_shape,
+            state_shape,
         ),
         in_specs=[VMEM] * 5,
-        out_specs=(VMEM, VMEM),
+        out_specs=(VMEM,) * 4,
         compiler_params=PARAMS,
         name="own_rows",
-    )(key_input, value_input, decay_rate, amplitude, skip_gain[None, :])
+    )(key_input, value_input, decay_rate, residue, skip_gain[None, :])
+    states, weight_z = lax.optimization_barrier((states, weight_z))
+    weights = [weight_z] + [
+        lax.ppermute(weight_z, "x", [(i, (i + shift) % x_size) for i in range(x_size)])
+        for shift in SHIFTS[1:]
+    ]
     states = exchange(states, ("x", "core"))
     before, total = pl.pallas_call(
         lambda *refs: row_block_kernel(rows, *refs),
@@ -177,7 +191,7 @@
         out_specs=(VMEM, VMEM),
         compiler_params=PARAMS,
         name="row_block",
-    )(where, states, decay_rate)
+    )(where, states, rate)
     totals = exchange(total, "z")
     gated = pl.pallas_call(
         lambda *refs: gate_kernel(rows, *refs),
@@ -186,30 +200,26 @@
         out_specs=VMEM,
         compiler_params=PARAMS,
         name="gate",
-    )(where, totals, before, decay_rate, amplitude, base, gate_input)
+    )(where, totals, before, rate, amplitude, base, gate_input)
     gated = lax.all_gather(gated, "core")
     parts = pl.pallas_call(
         project_kernel,
-        grid=(z_size,),
         out_shape=jax.ShapeDtypeStruct((y_size, cores, rows, x_size * out_cols), BF16),
-        in_specs=[
-            pl.BlockSpec((cores, rows, width), lambda i: (0, 0, 0)),
-            pl.BlockSpec((x_size, 1, out_cols, width), lambda i: (0, i, 0, 0)),
-        ],
-        out_specs=pl.BlockSpec((1, cores, rows, x_size * out_cols), lambda i: (i, 0, 0, 0)),
+        in_specs=[VMEM] * (1 + len(weights)),
+        out_specs=VMEM,
         compiler_params=PARAMS,
         name="project",
-    )(gated, weight)
+    )(gated, *weights)
     parts = parts.reshape(y_size * cores, rows, x_size * out_cols)
     parts = exchange(parts, ("chan", "core")).reshape(y_size, cores, rows, x_size * out_cols)
     return pl.pallas_call(
         sum_kernel,
         out_shape=jax.ShapeDtypeStruct((rows, width), BF16),
-        in_specs=[VMEM],
+        in_specs=[SMEM, VMEM],
         out_specs=VMEM,
         compiler_params=PARAMS,
         name="sum_parts",
-    )(parts)
+    )(where, parts)
 
 
 def solution(mesh):

time: 117 us -> 92.4 us (0.79)
  blocking collectives: 67.3 us -> 41.6 us
  starting transfers between devices: 13.9 us -> 25.9 us
  waiting for transfers between devices: 22.2 us -> 17.1 us
  local copies, waits for them, and re-layouts: 6.33 us -> 1.7 us
    all_to_all x3 -> x2, blocking collectives: 61.7 us -> 37.4 us  [exchange(): return lax.all_to_all(x, axes, 0, 0, tiled=True)]
    ppermute x0 -> x3, starting transfers between devices: none -> 10.1 us  [body(): lax.ppermute(weight_z, 'x', [(i, (i + shift) % x_size) for i in range(x_s...]
    all_to_all x2, waiting for transfers between devices: 22.2 us -> 16.2 us  [exchange(): return lax.all_to_all(x, axes, 0, 0, tiled=True)]
    unnamed x14 -> x12, local copies, waits for them, and re-layouts: 3.88 us -> 0.03 us
    all_to_all x2, starting transfers between devices: 13.9 us -> 15.8 us  [exchange(): return lax.all_to_all(x, axes, 0, 0, tiled=True)]
    broadcast_in_dim x1 -> x0, local copies, waits for them, and re-layouts: 1.57 us -> none  [body(): jnp.broadcast_to(weight_z[None], (x_size,) + weight_z.shape)]
    all_gather x1, blocking collectives: 5.58 us -> 4.24 us  [body(): gated = lax.all_gather(gated, 'core')]
    pallas_call x1, Pallas kernels: 2 us -> 0.81 us  [body(): pl.pallas_call(project_kernel, out_shape=jax.ShapeDtypeStruct((y_size, co...]
  transfers between devices with their start and end apart: 2 -> 5, of which waited for: 2 -> 2; matrix products, arithmetic and copies ran while one was open for 0% -> 0% of each run, Pallas kernels for 1% -> 4%
where the time goes in v2:
time: 92.4 us; the launch traced here: 91.8 us
  blocking collectives  41.6 us (45%)
  starting transfers between devices  25.9 us (28%)
  waiting for transfers between devices  17.1 us (19%)
  Pallas kernels  5.35 us (6%)
  local copies, waits for them, and re-layouts  1.7 us (2%)
    all_to_all x2, blocking collectives, exchange(): return lax.all_to_all(x, axes, 0, 0, tiled=True)  37.4 us
    all_to_all x2, waiting for transfers between devices, exchange(): return lax.all_to_all(x, axes, 0, 0, tiled=True)  16.2 us
    all_to_all x2, starting transfers between devices, exchange(): return lax.all_to_all(x, axes, 0, 0, tiled=True)  15.8 us
    ppermute x3, starting transfers between devices, body(): lax.ppermute(weight_z, 'x', [(i, (i + shift) % x_size) for i in range(x_s...  10.1 us
    all_gather x1, blocking collectives, body(): gated = lax.all_gather(gated, 'core')  4.24 us
  transfers between devices with their start and end apart: 5, of which 2 were waited for; matrix products, arithmetic and copies ran while one was open for 0% of the time, Pallas kernels for 4%

profile of v2, /device:TPU:1, one launch (start us, length us, event | category | flops | bytes accessed | tf_op | source)
XLA Modules:
  0.0 91.8 jit_solution(9551467566894030813)
XLA Ops:
  0.0 1.7 %broadcast_in_dim.10 = bf16[8,64,512]{2,1,0:T(8,128)(2,1)} broadcast(bf16[64,512]{1,0:T(8,128)(2,1)} %bitcast.12), dimensions={1,2} | broadcast | bytes 589824 | tf_op jit(solution)/shard_map/broadcast_in_dim | solution.py:162
  1.7 0.0 copy-start.5
  1.7 11.0 %all-to-all-start = ((bf16[8,64,512]{2,1,0:T(8,128)(2,1)}), bf16[8,64,512]{2,1,0:T(8,128)(2,1)S(1)}, u32[]{:S(2)}, u32[]{:S(2)}) async-start(bf16[8,64,512]{2,1,0:T(8,128)(2,1)} %broadcast_in_dim.10), calls=%async_computation | async-start | bytes 1048576 | tf_op jit(solution)/shard_map/all_to_all | solution.py:149
  12.7 0.0 copy-done
  12.7 0.0 copy-done.1
  12.8 1.7 %own_rows.1 = (f32[64,512]{1,0:T(8,128)S(1)}, f32[8,16,512]{2,1,0:T(8,128)}, f32[16,512]{1,0:T(8,128)S(1)}, f32[16,512]{1,0:T(8,128)S(1)}) custom-call(bf16[64,512]{1,0:T(8,128)(2,1)S(1)} %copy-done, bf16[64,512]{1,0:T(8,128)(2,1)S(1)} %copy-done.1, f32[16,512]{1,0:T(8,128)S(1)} %copy-done.3, f32[16,512]{1,0:T(8,128)S(1)} %copy-done.4, f32[1,512]{1,0:T(1,128)S(1)} %bitcast.11), custom_call_target="tpu_custom_call" | custom-call | tf_op jit(solution)/shard_map/own_rows/pallas_call | solution.py:165
  14.5 16.2 %all-to-all-done.refs_0_ = bf16[8,64,512]{2,1,0:T(8,128)(2,1)S(1)} async-done(((bf16[8,64,512]{2,1,0:T(8,128)(2,1)}), bf16[8,64,512]{2,1,0:T(8,128)(2,1)S(1)}, u32[]{:S(2)}, u32[]{:S(2)}) %all-to-all-start) | async-done | bytes 524320 | tf_op jit(solution)/shard_map/all_to_all | solution.py:149
  30.7 4.8 %all-to-all-start.1 = ((f32[8,16,512]{2,1,0:T(8,128)}), f32[8,16,512]{2,1,0:T(8,128)S(1)}, u32[]{:S(2)}, u32[]{:S(2)}) async-start(f32[8,16,512]{2,1,0:T(8,128)} %get-tuple-element.14), calls=%async_computation.1 | async-start | bytes 524288 | tf_op jit(solution)/shard_map/all_to_all | solution.py:149
  35.5 4.8 %collective-permute-start.2 = (bf16[8,64,512]{2,1,0:T(8,128)(2,1)S(1)}, bf16[8,64,512]{2,1,0:T(8,128)(2,1)S(1)}, u32[]{:S(2)}, u32[]{:S(2)}) collective-permute-start(bf16[8,64,512]{2,1,0:T(8,128)(2,1)S(1)} %all-to-all-done.refs_0_), channel_id=1, source_target_pairs={{0,32},{16,48},{32,0},{48,16},{1,33},{17,49},{33,1},{49,17},{2,34}... | collective-permute-start | bytes 1572872 | tf_op jit(solution)/shard_map/ppermute | solution.py:180
  40.2 2.8 %collective-permute-start.1 = (bf16[8,64,512]{2,1,0:T(8,128)(2,1)S(1)}, bf16[8,64,512]{2,1,0:T(8,128)(2,1)S(1)}, u32[]{:S(2)}, u32[]{:S(2)}) collective-permute-start(bf16[8,64,512]{2,1,0:T(8,128)(2,1)S(1)} %all-to-all-done.refs_0_), channel_id=1, source_target_pairs={{0,48},{16,0},{32,16},{48,32},{1,49},{17,1},{33,17},{49,33},{2,50}... | collective-permute-start | bytes 1572872 | tf_op jit(solution)/shard_map/ppermute | solution.py:180
  43.1 2.5 %collective-permute-start = (bf16[8,64,512]{2,1,0:T(8,128)(2,1)S(1)}, bf16[8,64,512]{2,1,0:T(8,128)(2,1)S(1)}, u32[]{:S(2)}, u32[]{:S(2)}) collective-permute-start(bf16[8,64,512]{2,1,0:T(8,128)(2,1)S(1)} %all-to-all-done.refs_0_), channel_id=1, source_target_pairs={{0,16},{16,32},{32,48},{48,0},{1,17},{17,33},{33,49},{49,1},{2,18}... | collective-permute-start | bytes 1572872 | tf_op jit(solution)/shard_map/ppermute | solution.py:180
  45.5 0.1 pad_add_fusion.refs_0_.where_ref
  45.6 0.0 all-to-all-done.1.refs_1_
  45.6 0.6 row_block.1
  46.2 0.0 copy-start.2
  46.2 12.7 %all_to_all.20.refs_1_ = f32[8,16,512]{2,1,0:T(8,128)S(1)} all-to-all(f32[8,16,512]{2,1,0:T(8,128)S(1)} %get-tuple-element.16), channel_id=1, replica_groups=mesh['z'=8,'x'=4,'core'=2,'chan'=8] {'z'}, dimensions={0} | all-to-all | bytes 524288 | tf_op jit(solution)/shard_map/all_to_all | solution.py:149
  58.9 0.9 %gate.1 = bf16[64,512]{1,0:T(8,128)(2,1)S(1)} custom-call(s32[3]{0:T(128)S(1)} %pad_add_fusion.refs_0_.where_ref, f32[8,16,512]{2,1,0:T(8,128)S(1)} %all_to_all.20.refs_1_, f32[16,512]{1,0:T(8,128)S(1)} %get-tuple-element.17.refs_2_, f32[16,512]{1,0:T(8,128)S(1)} %get-tuple-element.15.refs_2_.refs_3_, f32[16,512]{1,0:T(8,128)S(1)} %get-tuple-element.18.refs_4_, ...), custom_call_target="tpu_custom_call" | custom-call | tf_op jit(solution)/shard_map/gate/pallas_call | solution.py:196
  59.8 4.2 %all-gather = bf16[128,512]{1,0:T(8,128)(2,1)S(1)} all-gather(bf16[64,512]{1,0:T(8,128)(2,1)S(1)} %gate.1), channel_id=2, replica_groups=mesh['z'=8,'x'=4,'core'=2,'chan'=8] {'core'}, dimensions={0}, use_global_device_ids=true | all-gather | bytes 196608 | tf_op jit(solution)/shard_map/all_gather | solution.py:204
  64.1 0.0 collective-permute-done.2.refs_3_
  64.1 0.0 collective-permute-done.1.refs_2_
  64.1 0.9 collective-permute-done.refs_1_
  65.0 0.8 project.1
  65.8 24.7 %all_to_all.21 = bf16[16,64,256]{2,1,0:T(8,128)(2,1)S(1)} all-to-all(bf16[16,64,256]{2,1,0:T(8,128)(2,1)S(1)} %bitcast.9), channel_id=1, replica_groups=mesh['z'=8,'x'=4,'core'=2,'chan'=8] {'chan','core'}, dimensions={0} | all-to-all | bytes 1048576 | tf_op jit(solution)/shard_map/all_to_all | solution.py:149
  90.5 1.3 %sum_parts.1 = bf16[64,512]{1,0:T(8,128)(2,1)} custom-call(s32[3]{0:T(128)S(1)} %pad_add_fusion.refs_0_.where_ref, bf16[8,2,64,256]{3,2,1,0:T(8,128)(2,1)S(1)} %bitcast.8), custom_call_target="tpu_custom_call" | custom-call | tf_op jit(solution)/shard_map/sum_parts/pallas_call | solution.py:215
  (8 shorter events, 0.0 us)
Async XLA Ops:
  1.7 11.0 %copy-start = (bf16[64,512]{1,0:T(8,128)(2,1)S(1)}, bf16[64,512]{1,0:T(8,128)(2,1)}, u32[]{:S(2)}) copy-start(bf16[64,512]{1,0:T(8,128)(2,1)} %key_ref.1) | copy-start | bytes 196612
  1.7 11.0 %copy-start.1 = (bf16[64,512]{1,0:T(8,128)(2,1)S(1)}, bf16[64,512]{1,0:T(8,128)(2,1)}, u32[]{:S(2)}) copy-start(bf16[64,512]{1,0:T(8,128)(2,1)} %value_ref.1) | copy-start | bytes 196612
  1.7 11.0 %copy-start.3 = (f32[16,512]{1,0:T(8,128)S(1)}, f32[16,512]{1,0:T(8,128)}, u32[]{:S(2)}) copy-start(f32[16,512]{1,0:T(8,128)} %rate_ref.1) | copy-start | bytes 98308
  1.7 11.1 %copy-start.4 = (f32[16,512]{1,0:T(8,128)S(1)}, f32[16,512]{1,0:T(8,128)}, u32[]{:S(2)}) copy-start(f32[16,512]{1,0:T(8,128)} %residue_ref.1) | copy-start | bytes 98308
  1.7 11.1 %copy-start.5 = (f32[512]{0:T(512)S(1)}, f32[512]{0:T(512)}, u32[]{:S(2)}) copy-start(f32[512]{0:T(512)} %param.12) | copy-start | bytes 6148
  1.7 29.0 %all-to-all-start = ((bf16[8,64,512]{2,1,0:T(8,128)(2,1)}), bf16[8,64,512]{2,1,0:T(8,128)(2,1)S(1)}, u32[]{:S(2)}, u32[]{:S(2)}) async-start(bf16[8,64,512]{2,1,0:T(8,128)(2,1)} %broadcast_in_dim.10), calls=%async_computation | async-start | bytes 1048576 | tf_op jit(solution)/shard_map/all_to_all | solution.py:149
  30.7 15.0 %all-to-all-start.1 = ((f32[8,16,512]{2,1,0:T(8,128)}), f32[8,16,512]{2,1,0:T(8,128)S(1)}, u32[]{:S(2)}, u32[]{:S(2)}) async-start(f32[8,16,512]{2,1,0:T(8,128)} %get-tuple-element.14), calls=%async_computation.1 | async-start | bytes 524288 | tf_op jit(solution)/shard_map/all_to_all | solution.py:149
  35.5 28.6 %collective-permute-start.2 = (bf16[8,64,512]{2,1,0:T(8,128)(2,1)S(1)}, bf16[8,64,512]{2,1,0:T(8,128)(2,1)S(1)}, u32[]{:S(2)}, u32[]{:S(2)}) collective-permute-start(bf16[8,64,512]{2,1,0:T(8,128)(2,1)S(1)} %all-to-all-done.refs_0_), channel_id=1, source_target_pairs={{0,32},{16,48},{32,0},{48,16},{1,33},{17,49},{33,1},{49,17},{2,34}... | collective-permute-start | bytes 1572872 | tf_op jit(solution)/shard_map/ppermute | solution.py:180
  40.2 23.8 %collective-permute-start.1 = (bf16[8,64,512]{2,1,0:T(8,128)(2,1)S(1)}, bf16[8,64,512]{2,1,0:T(8,128)(2,1)S(1)}, u32[]{:S(2)}, u32[]{:S(2)}) collective-permute-start(bf16[8,64,512]{2,1,0:T(8,128)(2,1)S(1)} %all-to-all-done.refs_0_), channel_id=1, source_target_pairs={{0,48},{16,0},{32,16},{48,32},{1,49},{17,1},{33,17},{49,33},{2,50}... | collective-permute-start | bytes 1572872 | tf_op jit(solution)/shard_map/ppermute | solution.py:180
  43.1 21.9 %collective-permute-start = (bf16[8,64,512]{2,1,0:T(8,128)(2,1)S(1)}, bf16[8,64,512]{2,1,0:T(8,128)(2,1)S(1)}, u32[]{:S(2)}, u32[]{:S(2)}) collective-permute-start(bf16[8,64,512]{2,1,0:T(8,128)(2,1)S(1)} %all-to-all-done.refs_0_), channel_id=1, source_target_pairs={{0,16},{16,32},{32,48},{48,0},{1,17},{17,33},{33,49},{49,1},{2,18}... | collective-permute-start | bytes 1572872 | tf_op jit(solution)/shard_map/ppermute | solution.py:180
  46.2 12.7 %copy-start.2 = (bf16[64,512]{1,0:T(8,128)(2,1)S(1)}, bf16[64,512]{1,0:T(8,128)(2,1)}, u32[]{:S(2)}) copy-start(bf16[64,512]{1,0:T(8,128)(2,1)} %refs_6_.1) | copy-start | bytes 196612

commit v3 on v2

--- a/solution.py
+++ b/solution.py
@@ -8,9 +8,9 @@
 
 F32 = jnp.float32
 BF16 = jnp.bfloat16
-SEQ = ("z", "x", "core")
+SEQ = ("zh", "zl", "x", "core")
+CHAN = ("yh", "yl")
 LANES = 128
-SHIFTS = (0, 1, 3, 2)
 VMEM = pl.BlockSpec(memory_space=pltpu.VMEM)
 SMEM = pl.BlockSpec(memory_space=pltpu.SMEM)
 PARAMS = pltpu.CompilerParams(vmem_limit_bytes=48 * 1024 * 1024)
@@ -116,33 +116,33 @@
     lax.fori_loop(0, width // LANES, slab, 0)
 
 
-def project_kernel(gated_ref, *refs):
-    weight_refs, out_ref = refs[:-1], refs[-1]
-    cores, rows, depth = gated_ref.shape
-    gated = gated_ref[...].reshape(cores * rows, depth)
-    for j in range(out_ref.shape[0]):
-        weight = jnp.concatenate([ref[j] for ref in weight_refs], axis=0)
+def project_kernel(gated_ref, weight_ref, out_ref):
+    halves, cores, rows, depth = gated_ref.shape
+    weight = weight_ref[...].reshape(-1, depth)
+    for half in range(halves):
+        gated = gated_ref[half].reshape(cores * rows, depth)
         part = lax.dot_general(
             gated, weight, (((1,), (1,)), ((), ())), preferred_element_type=F32
         ).astype(BF16)
-        out_ref[j] = part.reshape(out_ref.shape[1:])
-
-
-def sum_kernel(where_ref, parts_ref, out_ref):
-    groups, cores, rows, width = parts_ref.shape
-    unit = out_ref.shape[1] // (len(SHIFTS) * cores)
-    own_x = where_ref[2]
-    totals = []
-    for core in range(cores):
-        total = parts_ref[0, core].astype(F32)
-        for j in range(1, groups):
-            total = total + parts_ref[j, core].astype(F32)
-        totals.append(total)
-    for j, shift in enumerate(SHIFTS):
-        pieces = [total[:, j * unit : (j + 1) * unit] for total in totals]
-        source = lax.rem(own_x + (len(SHIFTS) - shift), len(SHIFTS))
-        place = pl.multiple_of(source * (cores * unit), cores * unit)
-        out_ref[:, pl.ds(place, cores * unit)] = jnp.concatenate(pieces, axis=1).astype(BF16)
+        out_ref[half] = part.reshape(out_ref.shape[1:])
+
+
+def sum_kernel(parts_ref, out_ref):
+    total = parts_ref[0].astype(F32)
+    for j in range(1, parts_ref.shape[0]):
+        total = total + parts_ref[j].astype(F32)
+    out_ref[...] = total.astype(BF16)
+
+
+def interleave_kernel(unit, where_ref, pieces_ref, out_ref):
+    own = where_ref[2]
+    cores = pieces_ref.shape[0]
+    pieces = [pieces_ref[core, own] for core in range(cores)]
+    columns = []
+    for j in range(pieces[0].shape[1] // unit):
+        for piece in pieces:
+            columns.append(piece[:, j * unit : (j + 1) * unit])
+    out_ref[...] = jnp.concatenate(columns, axis=1)
 
 
 def exchange(x, axes):
@@ -152,15 +152,16 @@
 def body(gate_input, key_input, value_input, decay_rate, residue, skip_gain, out_weight):
     rows, width = key_input.shape
     modes = decay_rate.shape[0]
-    z_size, x_size, y_size = (lax.axis_size(a) for a in ("z", "x", "chan"))
-    cores = lax.axis_size("core")
+    zh_size, zl_size, x_size, cores = (lax.axis_size(a) for a in SEQ)
+    y_size = lax.axis_size(CHAN)
+    z_size = zh_size * zl_size
     out_cols = out_weight.shape[1]
     where = jnp.stack(
-        [lax.axis_index(("x", "core")), lax.axis_index("z"), lax.axis_index("x")]
+        [lax.axis_index(("x", "core")), lax.axis_index(("zh", "zl")), lax.axis_index("core")]
     ).astype(jnp.int32)
 
-    own_weight = jnp.broadcast_to(out_weight.T[None], (z_size, out_cols, width))
-    weight_z = exchange(own_weight, "z")
+    own_weight = jnp.broadcast_to(out_weight.T[None], (zh_size, out_cols, width))
+    weight_z = exchange(own_weight, "zh")
     state_shape = jax.ShapeDtypeStruct((modes, width), F32)
     base, states, amplitude, rate = pl.pallas_call(
         own_rows_kernel,
@@ -176,10 +177,7 @@
         name="own_rows",
     )(key_input, value_input, decay_rate, residue, skip_gain[None, :])
     states, weight_z = lax.optimization_barrier((states, weight_z))
-    weights = [weight_z] + [
-        lax.ppermute(weight_z, "x", [(i, (i + shift) % x_size) for i in range(x_size)])
-        for shift in SHIFTS[1:]
-    ]
+    weight = lax.all_gather(weight_z, "x")
     states = exchange(states, ("x", "core"))
     before, total = pl.pallas_call(
         lambda *refs: row_block_kernel(rows, *refs),
@@ -192,7 +190,7 @@
         compiler_params=PARAMS,
         name="row_block",
     )(where, states, rate)
-    totals = exchange(total, "z")
+    totals = exchange(total, ("zh", "zl"))
     gated = pl.pallas_call(
         lambda *refs: gate_kernel(rows, *refs),
         out_shape=jax.ShapeDtypeStruct((rows, width), BF16),
@@ -201,43 +199,58 @@
         compiler_params=PARAMS,
         name="gate",
     )(where, totals, before, rate, amplitude, base, gate_input)
-    gated = lax.all_gather(gated, "core")
+    gated = lax.all_gather(lax.all_gather(gated, "core"), "zl")
+    piece = (cores, rows, x_size * out_cols)
     parts = pl.pallas_call(
         project_kernel,
-        out_shape=jax.ShapeDtypeStruct((y_size, cores, rows, x_size * out_cols), BF16),
-        in_specs=[VMEM] * (1 + len(weights)),
+        grid=(zh_size,),
+        out_shape=jax.ShapeDtypeStruct((zh_size * zl_size,) + piece, BF16),
+        in_specs=[
+            pl.BlockSpec((zl_size, cores, rows, width), lambda i: (0, 0, 0, 0)),
+            pl.BlockSpec((x_size, 1, out_cols, width), lambda i: (0, i, 0, 0)),
+        ],
+        out_specs=pl.BlockSpec((zl_size,) + piece, lambda i: (i, 0, 0, 0)),
+        compiler_params=PARAMS,
+        name="project",
+    )(gated, weight)
+    parts = exchange(parts, CHAN)
+    summed = pl.pallas_call(
+        sum_kernel,
+        out_shape=jax.ShapeDtypeStruct(piece, BF16),
+        in_specs=[VMEM],
         out_specs=VMEM,
         compiler_params=PARAMS,
-        name="project",
-    )(gated, *weights)
-    parts = parts.reshape(y_size * cores, rows, x_size * out_cols)
-    parts = exchange(parts, ("chan", "core")).reshape(y_size, cores, rows, x_size * out_cols)
+        name="sum_parts",
+    )(parts)
+    swaps = [
+        (zl * zl_size + yl, yl * zl_size + zl) for zl in range(zl_size) for yl in range(zl_size)
+    ]
+    summed = lax.ppermute(summed, ("zl", "yl"), swaps)
+    summed = lax.all_gather(summed, "core")
     return pl.pallas_call(
-        sum_kernel,
+        lambda *refs: interleave_kernel(out_cols, *refs),
         out_shape=jax.ShapeDtypeStruct((rows, width), BF16),
         in_specs=[SMEM, VMEM],
         out_specs=VMEM,
         compiler_params=PARAMS,
-        name="sum_parts",
-    )(where, parts)
+        name="interleave",
+    )(where, summed)
 
 
 def solution(mesh):
-    finer = Mesh(
-        mesh.devices.reshape(8, 4, 2, mesh.shape["chan"]), ("z", "x", "core", "chan")
-    )
+    finer = Mesh(mesh.devices.reshape(4, 2, 4, 2, 4, 2), SEQ + CHAN)
     return jax.shard_map(
         body,
         mesh=finer,
         in_specs=(
-            P(SEQ, "chan"),
-            P(SEQ, "chan"),
-            P(SEQ, "chan"),
-            P(None, "chan"),
-            P(None, "chan"),
-            P("chan"),
-            P("chan", SEQ),
+            P(SEQ, CHAN),
+            P(SEQ, CHAN),
+            P(SEQ, CHAN),
+            P(None, CHAN),
+            P(None, CHAN),
+            P(CHAN),
+            P(CHAN, SEQ),
         ),
-        out_specs=P(SEQ, "chan"),
+        out_specs=P(SEQ, CHAN),
         check_vma=False,
     )

time: 92.4 us -> 110 us (1.19)
  the two profiles are of different devices: /device:TPU:1 before, /device:TPU:9 now
where the time goes in v3:
time: 110 us; the launch traced here: 109 us
  blocking collectives  49 us (45%)
  starting transfers between devices  22.1 us (20%)
  waiting for transfers between devices  15.1 us (14%)
  between operations  13.5 us (12%)
  Pallas kernels  5.9 us (5%)
  local copies, waits for them, and re-layouts  3.5 us (3%)
    all_to_all x2, blocking collectives, exchange(): return lax.all_to_all(x, axes, 0, 0, tiled=True)  33 us
    all_to_all x2, starting transfers between devices, exchange(): return lax.all_to_all(x, axes, 0, 0, tiled=True)  18.5 us
    all_to_all x2, waiting for transfers between devices, exchange(): return lax.all_to_all(x, axes, 0, 0, tiled=True)  12.8 us
    all_gather x2, blocking collectives, body(): gated = lax.all_gather(lax.all_gather(gated, 'core'), 'zl')  9.68 us
    all_gather x1, blocking collectives, body(): summed = lax.all_gather(summed, 'core')  6.33 us
    ppermute x1, starting transfers between devices, body(): summed = lax.ppermute(summed, ('zl', 'yl'), swaps)  3.61 us
    ppermute x1, waiting for transfers between devices, body(): summed = lax.ppermute(summed, ('zl', 'yl'), swaps)  2.29 us
  transfers between devices with their start and end apart: 4, of which 3 were waited for; matrix products, arithmetic and copies ran while one was open for 0% of the time, Pallas kernels for 3%

profile of v3, /device:TPU:9, one launch (start us, length us, event | category | flops | bytes accessed | tf_op | source)
XLA Modules:
  0.0 109.2 jit_solution(12726636857826681934)
XLA Ops:
  6.5 1.5 %broadcast_in_dim.10 = bf16[4,64,512]{2,1,0:T(8,128)(2,1)} broadcast(bf16[64,512]{1,0:T(8,128)(2,1)} %bitcast.14), dimensions={1,2} | broadcast | bytes 327680 | tf_op jit(solution)/shard_map/broadcast_in_dim | solution.py:163
  8.1 0.0 copy-start.6
  8.1 10.2 %all-to-all-start = ((bf16[4,64,512]{2,1,0:T(8,128)(2,1)}), bf16[4,64,512]{2,1,0:T(8,128)(2,1)S(1)}, u32[]{:S(2)}, u32[]{:S(2)}) async-start(bf16[4,64,512]{2,1,0:T(8,128)(2,1)} %broadcast_in_dim.10), calls=%async_computation | async-start | bytes 524288 | tf_op jit(solution)/shard_map/all_to_all | solution.py:149
  18.3 1.7 %own_rows.1 = (f32[64,512]{1,0:T(8,128)S(1)}, f32[8,16,512]{2,1,0:T(8,128)}, f32[16,512]{1,0:T(8,128)S(1)}, f32[16,512]{1,0:T(8,128)S(1)}) custom-call(bf16[64,512]{1,0:T(8,128)(2,1)S(1)} %copy-done.1, bf16[64,512]{1,0:T(8,128)(2,1)S(1)} %copy-done.2, f32[16,512]{1,0:T(8,128)S(1)} %copy-done.4, f32[16,512]{1,0:T(8,128)S(1)} %copy-done.5, f32[1,512]{1,0:T(1,128)S(1)} %bitcast.12), custom_call_target="tpu_custom_call" | custom-call | tf_op jit(solution)/shard_map/own_rows/pallas_call | solution.py:166
  20.0 6.4 %all-to-all-done = bf16[4,64,512]{2,1,0:T(8,128)(2,1)S(1)} async-done(((bf16[4,64,512]{2,1,0:T(8,128)(2,1)}), bf16[4,64,512]{2,1,0:T(8,128)(2,1)S(1)}, u32[]{:S(2)}, u32[]{:S(2)}) %all-to-all-start) | async-done | bytes 262176 | tf_op jit(solution)/shard_map/all_to_all | solution.py:149
  26.4 0.7 copy-done.7
  27.1 0.0 all-gather.6.cloned.1.call-update
  27.1 8.3 %all-to-all-start.1 = ((f32[8,16,512]{2,1,0:T(8,128)}), f32[8,16,512]{2,1,0:T(8,128)S(1)}, u32[]{:S(2)}, u32[]{:S(2)}) async-start(f32[8,16,512]{2,1,0:T(8,128)} %get-tuple-element.14), calls=%async_computation.1 | async-start | bytes 524288 | tf_op jit(solution)/shard_map/all_to_all | solution.py:149
  35.4 0.1 pad_add_fusion.refs_0_
  35.5 6.4 %all-to-all-done.1.refs_1_ = f32[8,16,512]{2,1,0:T(8,128)S(1)} async-done(((f32[8,16,512]{2,1,0:T(8,128)}), f32[8,16,512]{2,1,0:T(8,128)S(1)}, u32[]{:S(2)}, u32[]{:S(2)}) %all-to-all-start.1) | async-done | bytes 262176 | tf_op jit(solution)/shard_map/all_to_all | solution.py:149
  41.9 0.6 row_block.1
  42.5 0.0 copy-start.3
  42.5 12.6 %all_to_all.20.refs_1_ = f32[8,16,512]{2,1,0:T(8,128)S(1)} all-to-all(f32[8,16,512]{2,1,0:T(8,128)S(1)} %get-tuple-element.16), channel_id=1, replica_groups=mesh['zh'=4,'zl'=2,'x'=4,'core'=2,'yh'=4,'yl'=2] {'zh','zl'}, dimensions={0} | all-to-all | bytes 524288 | tf_op jit(solution)/shard_map/all_to_all | solution.py:149
  55.2 0.9 gate.1
  56.1 4.3 %all-gather = bf16[128,512]{1,0:T(8,128)(2,1)S(1)} all-gather(bf16[64,512]{1,0:T(8,128)(2,1)S(1)} %gate.1), channel_id=2, replica_groups=mesh['zh'=4,'zl'=2,'x'=4,'core'=2,'yh'=4,'yl'=2] {'core'}, dimensions={0}, use_global_device_ids=true | all-gather | bytes 196608 | tf_op jit(solution)/shard_map/all_gather | solution.py:202
  60.4 5.4 %all-gather.1 = bf16[4,64,512]{2,1,0:T(8,128)(2,1)S(1)} all-gather(bf16[2,64,512]{2,1,0:T(8,128)(2,1)S(1)} %bitcast.13), channel_id=3, replica_groups=mesh['zh'=4,'zl'=2,'x'=4,'core'=2,'yh'=4,'yl'=2] {'zl'}, dimensions={0}, use_global_device_ids=true | all-gather | bytes 393216 | tf_op jit(solution)/shard_map/all_gather | solution.py:202
  65.8 1.2 %copy-done = bf16[16,64,512]{2,1,0:T(8,128)(2,1)S(1)} copy-done((bf16[16,64,512]{2,1,0:T(8,128)(2,1)S(1)}, bf16[16,64,512]{2,1,0:T(8,128)(2,1)}, u32[]{:S(2)}) %copy-start) | copy-done | bytes 1048600
  67.0 1.3 %project.1 = bf16[8,2,64,256]{3,2,1,0:T(8,128)(2,1)S(1)} custom-call(bf16[2,2,64,512]{3,2,1,0:T(8,128)(2,1)S(1)} %bitcast.10, bf16[4,4,64,512]{3,2,1,0:T(8,128)(2,1)S(1)} %bitcast.9), custom_call_target="tpu_custom_call" | custom-call | tf_op jit(solution)/shard_map/project/pallas_call | solution.py:204
  68.4 20.4 %all_to_all.21.parts_ref = bf16[8,2,64,256]{3,2,1,0:T(8,128)(2,1)S(1)} all-to-all(bf16[8,2,64,256]{3,2,1,0:T(8,128)(2,1)S(1)} %project.1), channel_id=1, replica_groups=mesh['zh'=4,'zl'=2,'x'=4,'core'=2,'yh'=4,'yl'=2] {'yh','yl'}, dimensions={0} | all-to-all | bytes 1048576 | tf_op jit(solution)/shard_map/all_to_all | solution.py:149
  88.8 0.1 sum_parts.1
  88.8 3.6 %collective-permute-start = (bf16[2,64,256]{2,1,0:T(8,128)(2,1)S(1)}, bf16[2,64,256]{2,1,0:T(8,128)(2,1)S(1)}, u32[]{:S(2)}, u32[]{:S(2)}) collective-permute-start(bf16[2,64,256]{2,1,0:T(8,128)(2,1)S(1)} %sum_parts.1), channel_id=1, source_target_pairs={{0,0},{1,64},{64,1},{65,65},{2,2},{3,66},{66,3},{67,67},{4,4},{5,6... | collective-permute-start | bytes 196616 | tf_op jit(solution)/shard_map/ppermute | solution.py:228
  92.5 2.3 %collective-permute-done = bf16[2,64,256]{2,1,0:T(8,128)(2,1)S(1)} collective-permute-done((bf16[2,64,256]{2,1,0:T(8,128)(2,1)S(1)}, bf16[2,64,256]{2,1,0:T(8,128)(2,1)S(1)}, u32[]{:S(2)}, u32[]{:S(2)}) %collective-permute-start) | collective-permute-done | bytes 65568 | tf_op jit(solution)/shard_map/ppermute | solution.py:228
  94.7 6.3 %all-gather.3 = bf16[4,64,256]{2,1,0:T(8,128)(2,1)S(1)} all-gather(bf16[2,64,256]{2,1,0:T(8,128)(2,1)S(1)} %collective-permute-done), channel_id=5, replica_groups=mesh['zh'=4,'zl'=2,'x'=4,'core'=2,'yh'=4,'yl'=2] {'core'}, dimensions={0}, use_global_device_ids=true | all-gather | bytes 196608 | tf_op jit(solution)/shard_map/all_gather | solution.py:229
  101.1 1.3 %interleave.1 = bf16[64,512]{1,0:T(8,128)(2,1)} custom-call(s32[3]{0:T(128)S(1)} %pad_add_fusion.refs_0_, bf16[2,2,64,256]{3,2,1,0:T(8,128)(2,1)S(1)} %bitcast.11), custom_call_target="tpu_custom_call" | custom-call | tf_op jit(solution)/shard_map/interleave/pallas_call | solution.py:230
  (14 shorter events, 0.0 us)
Async XLA Ops:
  8.1 10.2 %copy-start.1 = (bf16[64,512]{1,0:T(8,128)(2,1)S(1)}, bf16[64,512]{1,0:T(8,128)(2,1)}, u32[]{:S(2)}) copy-start(bf16[64,512]{1,0:T(8,128)(2,1)} %key_ref.1) | copy-start | bytes 196612
  8.1 10.2 %copy-start.2 = (bf16[64,512]{1,0:T(8,128)(2,1)S(1)}, bf16[64,512]{1,0:T(8,128)(2,1)}, u32[]{:S(2)}) copy-start(bf16[64,512]{1,0:T(8,128)(2,1)} %value_ref.1) | copy-start | bytes 196612
  8.1 10.2 %copy-start.4 = (f32[16,512]{1,0:T(8,128)S(1)}, f32[16,512]{1,0:T(8,128)}, u32[]{:S(2)}) copy-start(f32[16,512]{1,0:T(8,128)} %rate_ref.1) | copy-start | bytes 98308
  8.1 10.2 %copy-start.5 = (f32[16,512]{1,0:T(8,128)S(1)}, f32[16,512]{1,0:T(8,128)}, u32[]{:S(2)}) copy-start(f32[16,512]{1,0:T(8,128)} %residue_ref.1) | copy-start | bytes 98308
  8.1 10.2 %copy-start.6 = (f32[512]{0:T(512)S(1)}, f32[512]{0:T(512)}, u32[]{:S(2)}) copy-start(f32[512]{0:T(512)} %param.12) | copy-start | bytes 6148
  8.1 18.3 %all-to-all-start = ((bf16[4,64,512]{2,1,0:T(8,128)(2,1)}), bf16[4,64,512]{2,1,0:T(8,128)(2,1)S(1)}, u32[]{:S(2)}, u32[]{:S(2)}) async-start(bf16[4,64,512]{2,1,0:T(8,128)(2,1)} %broadcast_in_dim.10), calls=%async_computation | async-start | bytes 524288 | tf_op jit(solution)/shard_map/all_to_all | solution.py:149
  18.3 47.5 %all-gather.6.cloned.1.call-start = ((), (), s32[]{:S(2)}) async-start(), calls=%async_computation.4 | async-start | bytes 1310720 | tf_op jit(solution)/shard_map/all_gather | solution.py:180
  26.4 0.7 copy-start.7
  27.1 14.8 %all-to-all-start.1 = ((f32[8,16,512]{2,1,0:T(8,128)}), f32[8,16,512]{2,1,0:T(8,128)S(1)}, u32[]{:S(2)}, u32[]{:S(2)}) async-start(f32[8,16,512]{2,1,0:T(8,128)} %get-tuple-element.14), calls=%async_computation.1 | async-start | bytes 524288 | tf_op jit(solution)/shard_map/all_to_all | solution.py:149
  42.5 12.6 %copy-start.3 = (bf16[64,512]{1,0:T(8,128)(2,1)S(1)}, bf16[64,512]{1,0:T(8,128)(2,1)}, u32[]{:S(2)}) copy-start(bf16[64,512]{1,0:T(8,128)(2,1)} %refs_6_.1) | copy-start | bytes 196612
  65.8 1.2 %copy-start = (bf16[16,64,512]{2,1,0:T(8,128)(2,1)S(1)}, bf16[16,64,512]{2,1,0:T(8,128)(2,1)}, u32[]{:S(2)}) copy-start(bf16[16,64,512]{2,1,0:T(8,128)(2,1)} %all-gather.6.cloned.1.call-done) | copy-start | bytes 3145732
  88.8 5.9 %collective-permute-start = (bf16[2,64,256]{2,1,0:T(8,128)(2,1)S(1)}, bf16[2,64,256]{2,1,0:T(8,128)(2,1)S(1)}, u32[]{:S(2)}, u32[]{:S(2)}) collective-permute-start(bf16[2,64,256]{2,1,0:T(8,128)(2,1)S(1)} %sum_parts.1), channel_id=1, source_target_pairs={{0,0},{1,64},{64,1},{65,65},{2,2},{3,66},{66,3},{67,67},{4,4},{5,6... | collective-permute-start | bytes 196616 | tf_op jit(solution)/shard_map/ppermute | solution.py:228
Sparse Core Ops, SparseCore 0:
  27.2 28.7 all-gather.5

commit v4 on v2

--- a/solution.py
+++ b/solution.py
@@ -8,9 +8,8 @@
 
 F32 = jnp.float32
 BF16 = jnp.bfloat16
-SEQ = ("z", "x", "core")
+SEQ = ("z", "xh", "xl", "core")
 LANES = 128
-SHIFTS = (0, 1, 3, 2)
 VMEM = pl.BlockSpec(memory_space=pltpu.VMEM)
 SMEM = pl.BlockSpec(memory_space=pltpu.SMEM)
 PARAMS = pltpu.CompilerParams(vmem_limit_bytes=48 * 1024 * 1024)
@@ -26,7 +25,6 @@
     rows, width = key_ref.shape
     modes = rate_ref.shape[0]
     tiles = rows // 8
-    copies = state_ref.shape[0]
 
     def slab(index, carry):
         cols = pl.ds(pl.multiple_of(index * LANES, LANES), LANES)
@@ -48,9 +46,7 @@
                 taps[j] = taps[j] + scaled[j][m : m + 1] * ahead
                 held = held + steps[tiles - 1 - j][m : m + 1] * signal[8 * j : 8 * j + 8]
             states.append(jnp.sum(held * behind, axis=0, keepdims=True))
-        state = jnp.concatenate(states, axis=0)
-        for copy in range(copies):
-            state_ref[copy, :, cols] = state
+        state_ref[:, cols] = jnp.concatenate(states, axis=0)
         row_ids = lax.broadcasted_iota(jnp.int32, (rows, LANES), 0)
         totals = [
             skip_ref[0:1, cols] * signal[8 * j : 8 * j + 8] for j in range(tiles)
@@ -116,12 +112,11 @@
     lax.fori_loop(0, width // LANES, slab, 0)
 
 
-def project_kernel(gated_ref, *refs):
-    weight_refs, out_ref = refs[:-1], refs[-1]
-    cores, rows, depth = gated_ref.shape
-    gated = gated_ref[...].reshape(cores * rows, depth)
+def project_kernel(gated_ref, near_ref, far_ref, out_ref):
+    shared, rows, depth = gated_ref.shape
+    gated = gated_ref[...].reshape(shared * rows, depth)
     for j in range(out_ref.shape[0]):
-        weight = jnp.concatenate([ref[j] for ref in weight_refs], axis=0)
+        weight = jnp.concatenate([near_ref[j], far_ref[j]], axis=0)
         part = lax.dot_general(
             gated, weight, (((1,), (1,)), ((), ())), preferred_element_type=F32
         ).astype(BF16)
@@ -129,20 +124,22 @@
 
 
 def sum_kernel(where_ref, parts_ref, out_ref):
-    groups, cores, rows, width = parts_ref.shape
-    unit = out_ref.shape[1] // (len(SHIFTS) * cores)
-    own_x = where_ref[2]
-    totals = []
-    for core in range(cores):
-        total = parts_ref[0, core].astype(F32)
-        for j in range(1, groups):
-            total = total + parts_ref[j, core].astype(F32)
-        totals.append(total)
-    for j, shift in enumerate(SHIFTS):
-        pieces = [total[:, j * unit : (j + 1) * unit] for total in totals]
-        source = lax.rem(own_x + (len(SHIFTS) - shift), len(SHIFTS))
-        place = pl.multiple_of(source * (cores * unit), cores * unit)
-        out_ref[:, pl.ds(place, cores * unit)] = jnp.concatenate(pieces, axis=1).astype(BF16)
+    groups, low, cores, rows, width = parts_ref.shape
+    own_high = where_ref[2]
+    unit = width // 2
+    for x_low in range(low):
+        totals = []
+        for core in range(cores):
+            total = parts_ref[0, x_low, core].astype(F32)
+            for j in range(1, groups):
+                total = total + parts_ref[j, x_low, core].astype(F32)
+            totals.append(total)
+        for far in range(2):
+            high = own_high if far == 0 else 1 - own_high
+            place = pl.multiple_of((high * low + x_low) * (cores * unit), cores * unit)
+            pieces = [total[:, far * unit : (far + 1) * unit] for total in totals]
+            columns = jnp.concatenate(pieces, axis=1)
+            out_ref[:, pl.ds(place, cores * unit)] = columns.astype(BF16)
 
 
 def exchange(x, axes):
@@ -152,35 +149,28 @@
 def body(gate_input, key_input, value_input, decay_rate, residue, skip_gain, out_weight):
     rows, width = key_input.shape
     modes = decay_rate.shape[0]
-    z_size, x_size, y_size = (lax.axis_size(a) for a in ("z", "x", "chan"))
-    cores = lax.axis_size("core")
+    z_size, high_size, low_size, cores = (lax.axis_size(a) for a in SEQ)
+    y_size = lax.axis_size("chan")
     out_cols = out_weight.shape[1]
     where = jnp.stack(
-        [lax.axis_index(("x", "core")), lax.axis_index("z"), lax.axis_index("x")]
+        [lax.axis_index(("xh", "xl", "core")), lax.axis_index("z"), lax.axis_index("xh")]
     ).astype(jnp.int32)
 
     own_weight = jnp.broadcast_to(out_weight.T[None], (z_size, out_cols, width))
-    weight_z = exchange(own_weight, "z")
+    near = exchange(own_weight, "z")
     state_shape = jax.ShapeDtypeStruct((modes, width), F32)
-    base, states, amplitude, rate = pl.pallas_call(
+    base, state, amplitude, rate = pl.pallas_call(
         own_rows_kernel,
-        out_shape=(
-            jax.ShapeDtypeStruct((rows, width), F32),
-            jax.ShapeDtypeStruct((x_size * cores, modes, width), F32),
-            state_shape,
-            state_shape,
-        ),
+        out_shape=(jax.ShapeDtypeStruct((rows, width), F32),) + (state_shape,) * 3,
         in_specs=[VMEM] * 5,
         out_specs=(VMEM,) * 4,
         compiler_params=PARAMS,
         name="own_rows",
     )(key_input, value_input, decay_rate, residue, skip_gain[None, :])
-    states, weight_z = lax.optimization_barrier((states, weight_z))
-    weights = [weight_z] + [
-        lax.ppermute(weight_z, "x", [(i, (i + shift) % x_size) for i in range(x_size)])
-        for shift in SHIFTS[1:]
-    ]
-    states = exchange(states, ("x", "core"))
+    states = lax.all_gather(lax.all_gather(state, "core"), ("xh", "xl"))
+    states = states.reshape(-1, modes, width)
+    states, near = lax.optimization_barrier((states, near))
+    far = lax.ppermute(near, "xh", [(0, 1), (1, 0)])
     before, total = pl.pallas_call(
         lambda *refs: row_block_kernel(rows, *refs),
         out_shape=(
@@ -201,17 +191,18 @@
         compiler_params=PARAMS,
         name="gate",
     )(where, totals, before, rate, amplitude, base, gate_input)
-    gated = lax.all_gather(gated, "core")
+    gated = lax.all_gather(lax.all_gather(gated, "core"), "xl")
+    shared = low_size * cores
+    piece = (rows, high_size * out_cols)
     parts = pl.pallas_call(
         project_kernel,
-        out_shape=jax.ShapeDtypeStruct((y_size, cores, rows, x_size * out_cols), BF16),
-        in_specs=[VMEM] * (1 + len(weights)),
+        out_shape=jax.ShapeDtypeStruct((y_size, shared) + piece, BF16),
+        in_specs=[VMEM] * 3,
         out_specs=VMEM,
         compiler_params=PARAMS,
         name="project",
-    )(gated, *weights)
-    parts = parts.reshape(y_size * cores, rows, x_size * out_cols)
-    parts = exchange(parts, ("chan", "core")).reshape(y_size, cores, rows, x_size * out_cols)
+    )(gated.reshape(shared, rows, width), near, far)
+    parts = exchange(parts.reshape((y_size * shared,) + piece), ("chan", "xl", "core"))
     return pl.pallas_call(
         sum_kernel,
         out_shape=jax.ShapeDtypeStruct((rows, width), BF16),
@@ -219,13 +210,11 @@
         out_specs=VMEM,
         compiler_params=PARAMS,
         name="sum_parts",
-    )(where, parts)
+    )(where, parts.reshape((y_size, low_size, cores) + piece))
 
 
 def solution(mesh):
-    finer = Mesh(
-        mesh.devices.reshape(8, 4, 2, mesh.shape["chan"]), ("z", "x", "core", "chan")
-    )
+    finer = Mesh(mesh.devices.reshape(8, 2, 2, 2, 8), SEQ + ("chan",))
     return jax.shard_map(
         body,
         mesh=finer,

time: 92.4 us -> 85.3 us (0.923)
  waiting for transfers between devices: 17.1 us -> 8.25 us
  blocking collectives: 41.6 us -> 49.3 us
  starting transfers between devices: 25.9 us -> 19.2 us
    all_gather x1 -> x4, blocking collectives: 4.24 us -> 23.7 us  [the longest x2 12.8 us: body(): states = lax.all_gather(lax.all_gather(state, 'core'), ('xh', 'xl'))]
    all_to_all x2 -> x1, blocking collectives: 37.4 us -> 25.6 us  [exchange(): return lax.all_to_all(x, axes, 0, 0, tiled=True)]
    all_to_all x2, waiting for transfers between devices: 16.2 us -> 8.25 us  [exchange(): return lax.all_to_all(x, axes, 0, 0, tiled=True)]
    ppermute x3 -> x1, starting transfers between devices: 10.1 us -> 4.33 us  [body(): far = lax.ppermute(near, 'xh', [(0, 1), (1, 0)])]
    all_to_all x2, starting transfers between devices: 15.8 us -> 14.9 us  [exchange(): return lax.all_to_all(x, axes, 0, 0, tiled=True)]
  transfers between devices with their start and end apart: 5 -> 3, of which waited for: 2 -> 2; matrix products, arithmetic and copies ran while one was open for 0% -> 0% of each run, Pallas kernels for 4% -> 2%
where the time goes in v4:
time: 85.3 us; the launch traced here: 84.7 us
  blocking collectives  49.3 us (58%)
  starting transfers between devices  19.2 us (23%)
  waiting for transfers between devices  8.25 us (10%)
  Pallas kernels  5.4 us (6%)
  local copies, waits for them, and re-layouts  2.41 us (3%)
    all_to_all x1, blocking collectives, exchange(): return lax.all_to_all(x, axes, 0, 0, tiled=True)  25.6 us
    all_to_all x2, starting transfers between devices, exchange(): return lax.all_to_all(x, axes, 0, 0, tiled=True)  14.9 us
    all_gather x2, blocking collectives, body(): states = lax.all_gather(lax.all_gather(state, 'core'), ('xh', 'xl'))  12.8 us
    all_gather x2, blocking collectives, body(): gated = lax.all_gather(lax.all_gather(gated, 'core'), 'xl')  11 us
    all_to_all x2, waiting for transfers between devices, exchange(): return lax.all_to_all(x, axes, 0, 0, tiled=True)  8.25 us
    ppermute x1, starting transfers between devices, body(): far = lax.ppermute(near, 'xh', [(0, 1), (1, 0)])  4.33 us
  transfers between devices with their start and end apart: 3, of which 2 were waited for; matrix products, arithmetic and copies ran while one was open for 0% of the time, Pallas kernels for 2%

profile of v4, /device:TPU:1, one launch (start us, length us, event | category | flops | bytes accessed | tf_op | source)
XLA Modules:
  0.0 84.7 jit_solution(10141101728413914569)
XLA Ops:
  0.0 1.7 %broadcast_in_dim.10 = bf16[8,64,512]{2,1,0:T(8,128)(2,1)} broadcast(bf16[64,512]{1,0:T(8,128)(2,1)} %bitcast.14), dimensions={1,2} | broadcast | bytes 589824 | tf_op jit(solution)/shard_map/broadcast_in_dim | solution.py:159
  1.7 11.0 %all-to-all-start = ((bf16[8,64,512]{2,1,0:T(8,128)(2,1)}), bf16[8,64,512]{2,1,0:T(8,128)(2,1)S(1)}, u32[]{:S(2)}, u32[]{:S(2)}) async-start(bf16[8,64,512]{2,1,0:T(8,128)(2,1)} %broadcast_in_dim.10), calls=%async_computation | async-start | bytes 1048576 | tf_op jit(solution)/shard_map/all_to_all | solution.py:146
  12.7 0.0 copy-start.5
  12.7 0.0 copy-done
  12.7 0.0 copy-done.1
  12.7 0.0 copy-done.4
  12.7 0.7 copy-done.3
  13.4 0.0 copy-done.5
  13.5 1.2 %own_rows.1 = (f32[64,512]{1,0:T(8,128)S(1)}, f32[16,512]{1,0:T(8,128)S(1)}, f32[16,512]{1,0:T(8,128)S(1)}, f32[16,512]{1,0:T(8,128)S(1)}) custom-call(bf16[64,512]{1,0:T(8,128)(2,1)S(1)} %copy-done, bf16[64,512]{1,0:T(8,128)(2,1)S(1)} %copy-done.1, f32[16,512]{1,0:T(8,128)S(1)} %copy-done.3, f32[16,512]{1,0:T(8,128)S(1)} %copy-done.4, f32[1,512]{1,0:T(1,128)S(1)} %bitcast.11), custom_call_target="tpu_custom_call" | custom-call | tf_op jit(solution)/shard_map/own_rows/pallas_call | solution.py:162
  14.6 2.5 %all-gather = f32[32,512]{1,0:T(8,128)S(1)} all-gather(f32[16,512]{1,0:T(8,128)S(1)} %get-tuple-element.13), channel_id=2, replica_groups=mesh['z'=8,'xh'=2,'xl'=2,'core'=2,'chan'=8] {'core'}, dimensions={0}, use_global_device_ids=true | all-gather | bytes 98304 | tf_op jit(solution)/shard_map/all_gather | solution.py:170
  17.1 10.3 %all-gather.1.refs_1_ = f32[8,16,512]{2,1,0:T(8,128)S(1)} all-gather(f32[2,16,512]{2,1,0:T(8,128)S(1)} %bitcast.13), channel_id=3, replica_groups=mesh['z'=8,'xh'=2,'xl'=2,'core'=2,'chan'=8] {'xh','xl'}, dimensions={0}, use_global_device_ids=true | all-gather | bytes 327680 | tf_op jit(solution)/shard_map/all_gather | solution.py:170
  27.4 0.1 pad_add_fusion.refs_0_.where_ref
  27.5 3.2 %all-to-all-done.near_ref = bf16[8,64,512]{2,1,0:T(8,128)(2,1)S(1)} async-done(((bf16[8,64,512]{2,1,0:T(8,128)(2,1)}), bf16[8,64,512]{2,1,0:T(8,128)(2,1)S(1)}, u32[]{:S(2)}, u32[]{:S(2)}) %all-to-all-start) | async-done | bytes 524320 | tf_op jit(solution)/shard_map/all_to_all | solution.py:146
  30.6 1.3 %row_block.1 = (f32[16,512]{1,0:T(8,128)S(1)}, f32[8,16,512]{2,1,0:T(8,128)}) custom-call(s32[3]{0:T(128)S(1)} %pad_add_fusion.refs_0_.where_ref, f32[8,16,512]{2,1,0:T(8,128)S(1)} %all-gather.1.refs_1_, f32[16,512]{1,0:T(8,128)S(1)} %get-tuple-element.15.refs_2_.refs_3_), custom_call_target="tpu_custom_call" | custom-call | tf_op jit(solution)/shard_map/row_block/pallas_call | solution.py:174
  31.9 3.9 %all-to-all-start.1 = ((f32[8,16,512]{2,1,0:T(8,128)}), f32[8,16,512]{2,1,0:T(8,128)S(1)}, u32[]{:S(2)}, u32[]{:S(2)}) async-start(f32[8,16,512]{2,1,0:T(8,128)} %get-tuple-element.16), calls=%async_computation.1 | async-start | bytes 524288 | tf_op jit(solution)/shard_map/all_to_all | solution.py:146
  35.8 4.3 %collective-permute-start = (bf16[8,64,512]{2,1,0:T(8,128)(2,1)S(1)}, bf16[8,64,512]{2,1,0:T(8,128)(2,1)S(1)}, u32[]{:S(2)}, u32[]{:S(2)}) collective-permute-start(bf16[8,64,512]{2,1,0:T(8,128)(2,1)S(1)} %all-to-all-done.near_ref), channel_id=1, source_target_pairs={{0,32},{32,0},{1,33},{33,1},{2,34},{34,2},{3,35},{35,3},{4,36},{36... | collective-permute-start | bytes 1572872 | tf_op jit(solution)/shard_map/ppermute | solution.py:173
  40.2 5.1 %all-to-all-done.1.refs_1_ = f32[8,16,512]{2,1,0:T(8,128)S(1)} async-done(((f32[8,16,512]{2,1,0:T(8,128)}), f32[8,16,512]{2,1,0:T(8,128)S(1)}, u32[]{:S(2)}, u32[]{:S(2)}) %all-to-all-start.1) | async-done | bytes 262176 | tf_op jit(solution)/shard_map/all_to_all | solution.py:146
  45.2 0.9 %gate.1 = bf16[64,512]{1,0:T(8,128)(2,1)S(1)} custom-call(s32[3]{0:T(128)S(1)} %pad_add_fusion.refs_0_.where_ref, f32[8,16,512]{2,1,0:T(8,128)S(1)} %all-to-all-done.1.refs_1_, f32[16,512]{1,0:T(8,128)S(1)} %get-tuple-element.17.refs_2_, f32[16,512]{1,0:T(8,128)S(1)} %get-tuple-element.15.refs_2_.refs_3_, f32[16,512]{1,0:T(8,128)S(1)} %get-tuple-element.18.refs_4_, ...), custom_call_target="tpu_custom_call" | custom-call | tf_op jit(solution)/shard_map/gate/pallas_call | solution.py:186
  46.1 5.6 %all-gather.2 = bf16[128,512]{1,0:T(8,128)(2,1)S(1)} all-gather(bf16[64,512]{1,0:T(8,128)(2,1)S(1)} %gate.1), channel_id=4, replica_groups=mesh['z'=8,'xh'=2,'xl'=2,'core'=2,'chan'=8] {'core'}, dimensions={0}, use_global_device_ids=true | all-gather | bytes 196608 | tf_op jit(solution)/shard_map/all_gather | solution.py:194
  51.7 5.4 %all-gather.3.gated_ref = bf16[4,64,512]{2,1,0:T(8,128)(2,1)S(1)} all-gather(bf16[2,64,512]{2,1,0:T(8,128)(2,1)S(1)} %bitcast.12), channel_id=5, replica_groups=mesh['z'=8,'xh'=2,'xl'=2,'core'=2,'chan'=8] {'xl'}, dimensions={0}, use_global_device_ids=true | all-gather | bytes 393216 | tf_op jit(solution)/shard_map/all_gather | solution.py:194
  57.1 0.0 collective-permute-done.far_ref
  57.1 0.7 project.1
  57.8 25.6 %all_to_all.15 = bf16[32,64,128]{2,1,0:T(8,128)(2,1)S(1)} all-to-all(bf16[32,64,128]{2,1,0:T(8,128)(2,1)S(1)} %bitcast.9), channel_id=1, replica_groups=mesh['z'=8,'xh'=2,'xl'=2,'core'=2,'chan'=8] {'chan','xl','core'}, dimensions={0} | all-to-all | bytes 1048576 | tf_op jit(solution)/shard_map/all_to_all | solution.py:146
  83.4 1.3 %sum_parts.1 = bf16[64,512]{1,0:T(8,128)(2,1)} custom-call(s32[3]{0:T(128)S(1)} %pad_add_fusion.refs_0_.where_ref, bf16[8,2,2,64,128]{4,3,2,1,0:T(8,128)(2,1)S(1)} %bitcast.10), custom_call_target="tpu_custom_call" | custom-call | tf_op jit(solution)/shard_map/sum_parts/pallas_call | solution.py:206
  (6 shorter events, 0.0 us)
Async XLA Ops:
  1.7 11.0 %copy-start = (bf16[64,512]{1,0:T(8,128)(2,1)S(1)}, bf16[64,512]{1,0:T(8,128)(2,1)}, u32[]{:S(2)}) copy-start(bf16[64,512]{1,0:T(8,128)(2,1)} %key_ref.1) | copy-start | bytes 196612
  1.7 11.0 %copy-start.1 = (bf16[64,512]{1,0:T(8,128)(2,1)S(1)}, bf16[64,512]{1,0:T(8,128)(2,1)}, u32[]{:S(2)}) copy-start(bf16[64,512]{1,0:T(8,128)(2,1)} %value_ref.1) | copy-start | bytes 196612
  1.7 11.0 %copy-start.4 = (f32[16,512]{1,0:T(8,128)S(1)}, f32[16,512]{1,0:T(8,128)}, u32[]{:S(2)}) copy-start(f32[16,512]{1,0:T(8,128)} %residue_ref.1) | copy-start | bytes 98308
  1.7 29.0 %all-to-all-start = ((bf16[8,64,512]{2,1,0:T(8,128)(2,1)}), bf16[8,64,512]{2,1,0:T(8,128)(2,1)S(1)}, u32[]{:S(2)}, u32[]{:S(2)}) async-start(bf16[8,64,512]{2,1,0:T(8,128)(2,1)} %broadcast_in_dim.10), calls=%async_computation | async-start | bytes 1048576 | tf_op jit(solution)/shard_map/all_to_all | solution.py:146
  12.7 0.8 copy-start.3
  12.7 0.7 copy-start.5
  31.9 13.3 %copy-start.2 = (bf16[64,512]{1,0:T(8,128)(2,1)S(1)}, bf16[64,512]{1,0:T(8,128)(2,1)}, u32[]{:S(2)}) copy-start(bf16[64,512]{1,0:T(8,128)(2,1)} %refs_6_.1) | copy-start | bytes 196612
  31.9 13.3 %all-to-all-start.1 = ((f32[8,16,512]{2,1,0:T(8,128)}), f32[8,16,512]{2,1,0:T(8,128)S(1)}, u32[]{:S(2)}, u32[]{:S(2)}) async-start(f32[8,16,512]{2,1,0:T(8,128)} %get-tuple-element.16), calls=%async_computation.1 | async-start | bytes 524288 | tf_op jit(solution)/shard_map/all_to_all | solution.py:146
  35.8 21.3 %collective-permute-start = (bf16[8,64,512]{2,1,0:T(8,128)(2,1)S(1)}, bf16[8,64,512]{2,1,0:T(8,128)(2,1)S(1)}, u32[]{:S(2)}, u32[]{:S(2)}) collective-permute-start(bf16[8,64,512]{2,1,0:T(8,128)(2,1)S(1)} %all-to-all-done.near_ref), channel_id=1, source_target_pairs={{0,32},{32,0},{1,33},{33,1},{2,34},{34,2},{3,35},{35,3},{4,36},{36... | collective-permute-start | bytes 1572872 | tf_op jit(solution)/shard_map/ppermute | solution.py:173

commit v5 on v4

v5 whole, which is shorter than its diff:
```python
import jax
import jax.numpy as jnp
from jax import lax
from jax.experimental import pallas as pl
from jax.experimental.pallas import tpu as pltpu
from jax.sharding import Mesh
from jax.sharding import PartitionSpec as P

F32 = jnp.float32
BF16 = jnp.bfloat16
SEQ = ("z", "xh", "xl", "core")
LANES = 128
VMEM = pl.BlockSpec(memory_space=pltpu.VMEM)
SMEM = pl.BlockSpec(memory_space=pltpu.SMEM)
PARAMS = pltpu.CompilerParams(vmem_limit_bytes=48 * 1024 * 1024)


def tile_rows():
    return lax.broadcasted_iota(jnp.int32, (8, LANES), 0).astype(F32)


def chunk_kernel(
    where_ref, signals_ref, rate_ref, residue_ref, skip_ref,
    base_ref, before_ref, send_ref, amp_ref, copy_ref, signal_ref, state_ref,
):
    blocks, rows, width = base_ref.shape
    modes = rate_ref.shape[0]
    tiles = rows // 8
    cores = signals_ref.shape[0]
    first_col = where_ref[1] * width

    def slab(index, carry):
        cols = pl.ds(pl.multiple_of(index * LANES, LANES), LANES)
        source = pl.ds(pl.multiple_of(first_col + index * LANES, LANES), LANES)
        for i in range(blocks):
            signal_ref[i] = signals_ref[i % cores, i // cores, :, source]
        rate = rate_ref[:, source]
        amp = residue_ref[:, source] * jnp.sqrt(1.0 - jnp.exp(-2.0 * rate))
        amp_ref[:, cols] = amp
        copy_ref[:, cols] = rate
        steps = [jnp.exp(-8.0 * j * rate) for j in range(tiles)]
        scaled = [amp * step for step in steps]
        first = tile_rows()
        taps = [jnp.zeros((8, LANES), F32) for _ in range(tiles)]
        for m in range(modes):
            ahead = jnp.exp(-rate[m : m + 1] * first)
            behind = jnp.exp(-rate[m : m + 1] * (7.0 - first))
            held = [jnp.zeros((8, LANES), F32) for _ in range(blocks)]
            for j in range(tiles):
                taps[j] = taps[j] + scaled[j][m : m + 1] * ahead
                step = steps[tiles - 1 - j][m : m + 1]
                for i in range(blocks):
                    held[i] = held[i] + step * signal_ref[i, 8 * j : 8 * j + 8]
            for i in range(blocks):
                state_ref[i, m : m + 1] = jnp.sum(held[i] * behind, axis=0, keepdims=True)
        decay = jnp.exp(-float(rows) * rate)
        running = jnp.zeros((modes, LANES), F32)
        for i in range(blocks):
            before_ref[i, :, cols] = running
            running = decay * running + state_ref[i]
        for copy in range(send_ref.shape[0]):
            send_ref[copy, :, cols] = running
        row_ids = lax.broadcasted_iota(jnp.int32, (rows, LANES), 0)
        skip = skip_ref[0:1, source]

        def block(i, inner):
            signal = signal_ref[i]
            totals = [skip * signal[8 * j : 8 * j + 8] for j in range(tiles)]
            for lag in range(8):
                moved = signal
                if lag:
                    moved = jnp.where(row_ids >= lag, pltpu.roll(signal, lag, 0), 0.0)
                for j in range(tiles):
                    tap = taps[j][lag : lag + 1]
                    for k in range(j, tiles):
                        totals[k] = totals[k] + tap * moved[8 * (k - j) : 8 * (k - j) + 8]
            for j in range(tiles):
                base_ref[i, 8 * j : 8 * j + 8, cols] = totals[j]
            return inner

        return lax.fori_loop(0, blocks, block, carry)

    lax.fori_loop(0, width // LANES, slab, 0)


def gate_kernel(
    where_ref, chunks_ref, before_ref, rate_ref, amp_ref, base_ref, gate_ref, gated_ref
):
    blocks, rows, width = base_ref.shape
    modes = rate_ref.shape[0]
    tiles = rows // 8
    cores = gate_ref.shape[0]
    own = where_ref[0]
    first_col = where_ref[1] * width

    def slab(index, carry):
        cols = pl.ds(pl.multiple_of(index * LANES, LANES), LANES)
        source = pl.ds(pl.multiple_of(first_col + index * LANES, LANES), LANES)
        rate = rate_ref[:, cols]
        amp = amp_ref[:, cols]
        decay = jnp.exp(-float(rows * blocks) * rate)
        running = jnp.zeros((modes, LANES), F32)
        entering = jnp.zeros((modes, LANES), F32)
        for chunk in range(chunks_ref.shape[0]):
            entering = jnp.where(own == chunk, running, entering)
            running = decay * running + chunks_ref[chunk, :, cols]
        steps = [jnp.exp(-8.0 * j * rate) for j in range(tiles)]
        first = tile_rows() + 1.0
        aheads = [jnp.exp(-rate[m : m + 1] * first) for m in range(modes)]
        state = entering
        for i in range(blocks):
            full = (before_ref[i, :, cols] + state) * amp
            if i < blocks - 1:
                state = state * jnp.exp(-float(rows) * rate)
            for j in range(tiles):
                part = base_ref[i, 8 * j : 8 * j + 8, cols]
                scaled = full * steps[j]
                for m in range(modes):
                    part = part + scaled[m : m + 1] * aheads[m]
                gate = gate_ref[i % cores, i // cores, 8 * j : 8 * j + 8, source].astype(F32)
                gated_ref[i, 8 * j : 8 * j + 8, cols] = (gate * part).astype(BF16)
        return carry

    lax.fori_loop(0, width // LANES, slab, 0)


def project_kernel(gated_ref, near_ref, far_ref, out_ref):
    cores, shared, rows, half = gated_ref.shape
    gated = [gated_ref[core].reshape(shared * rows, half) for core in range(cores)]
    for j in range(out_ref.shape[0]):
        total = 0.0
        for core in range(cores):
            depth = slice(core * half, (core + 1) * half)
            weight = jnp.concatenate([near_ref[j, :, depth], far_ref[j, :, depth]], axis=0)
            total = total + lax.dot_general(
                gated[core], weight, (((1,), (1,)), ((), ())), preferred_element_type=F32
            )
        out_ref[j] = total.astype(BF16).reshape(out_ref.shape[1:])


def sum_kernel(where_ref, parts_ref, out_ref):
    groups, low, cores, rows, width = parts_ref.shape
    own_high = where_ref[2]
    unit = width // 2
    for x_low in range(low):
        totals = []
        for core in range(cores):
            total = parts_ref[0, x_low, core].astype(F32)
            for j in range(1, groups):
                total = total + parts_ref[j, x_low, core].astype(F32)
            totals.append(total)
        for far in range(2):
            high = own_high if far == 0 else 1 - own_high
            place = pl.multiple_of((high * low + x_low) * (cores * unit), cores * unit)
            pieces = [total[:, far * unit : (far + 1) * unit] for total in totals]
            columns = jnp.concatenate(pieces, axis=1)
            out_ref[:, pl.ds(place, cores * unit)] = columns.astype(BF16)


def exchange(x, axes):
    return lax.all_to_all(x, axes, 0, 0, tiled=True)


def body(gate_input, key_input, value_input, decay_rate, residue, skip_gain, out_weight):
    rows, width = key_input.shape
    modes = decay_rate.shape[0]
    z_size, high_size, low_size, cores = (lax.axis_size(a) for a in SEQ)
    y_size = lax.axis_size("chan")
    out_cols = out_weight.shape[1]
    chunks = z_size * high_size
    blocks = low_size * cores
    half = width // cores
    where = jnp.stack(
        [lax.axis_index(("z", "xh")), lax.axis_index("core"), lax.axis_index("xh")]
    ).astype(jnp.int32)

    own_weight = jnp.broadcast_to(out_weight.T[None], (z_size, out_cols, width))
    near = exchange(own_weight, "z")
    signal = key_input.astype(F32) * value_input.astype(F32)
    signals = lax.all_gather(lax.all_gather(signal, "xl"), "core")
    gate = lax.all_gather(lax.all_gather(gate_input, "xl"), "core")
    base, before, state, amplitude, rate = pl.pallas_call(
        chunk_kernel,
        out_shape=(
            jax.ShapeDtypeStruct((blocks, rows, half), F32),
            jax.ShapeDtypeStruct((blocks, modes, half), F32),
            jax.ShapeDtypeStruct((chunks, modes, half), F32),
            jax.ShapeDtypeStruct((modes, half), F32),
            jax.ShapeDtypeStruct((modes, half), F32),
        ),
        in_specs=[SMEM] + [VMEM] * 4,
        out_specs=(VMEM,) * 5,
        scratch_shapes=[
            pltpu.VMEM((blocks, rows, LANES), F32),
            pltpu.VMEM((blocks, modes, LANES), F32),
        ],
        compiler_params=PARAMS,
        name="chunk",
    )(where, signals, decay_rate, residue, skip_gain[None, :])
    state, near = lax.optimization_barrier((state, near))
    far = lax.ppermute(near, "xh", [(0, 1), (1, 0)])
    states = exchange(state, ("z", "xh"))
    gated = pl.pallas_call(
        gate_kernel,
        out_shape=jax.ShapeDtypeStruct((blocks, rows, half), BF16),
        in_specs=[SMEM] + [VMEM] * 6,
        out_specs=VMEM,
        compiler_params=PARAMS,
        name="gate",
    )(where, states, before, rate, amplitude, base, gate)
    gated = lax.all_gather(gated, "core")
    piece = (rows, high_size * out_cols)
    parts = pl.pallas_call(
        project_kernel,
        out_shape=jax.ShapeDtypeStruct((y_size, blocks) + piece, BF16),
        in_specs=[VMEM] * 3,
        out_specs=VMEM,
        compiler_params=PARAMS,
        name="project",
    )(gated, near, far)
    parts = exchange(parts.reshape((y_size * blocks,) + piece), ("chan", "xl", "core"))
    return pl.pallas_call(
        sum_kernel,
        out_shape=jax.ShapeDtypeStruct((rows, width), BF16),
        in_specs=[SMEM, VMEM],
        out_specs=VMEM,
        compiler_params=PARAMS,
        name="sum_parts",
    )(where, parts.reshape((y_size, low_size, cores) + piece))


def solution(mesh):
    finer = Mesh(mesh.devices.reshape(8, 2, 2, 2, 8), SEQ + ("chan",))
    return jax.shard_map(
        body,
        mesh=finer,
        in_specs=(
            P(SEQ, "chan"),
            P(SEQ, "chan"),
            P(SEQ, "chan"),
            P(None, "chan"),
            P(None, "chan"),
            P("chan"),
            P("chan", SEQ),
        ),
        out_specs=P(SEQ, "chan"),
        check_vma=False,
    )
```

time: 85.3 us -> 88.2 us (1.034)
  blocking collectives: 49.3 us -> 53.4 us
  waiting for transfers between devices: 8.25 us -> 5.71 us
    all_gather x4 -> x5, blocking collectives: 23.7 us -> 28.6 us  [the longest x2 18 us: body(): gate = lax.all_gather(lax.all_gather(gate_input, 'xl'), 'core')]
    all_to_all x2, waiting for transfers between devices: 8.25 us -> 5.71 us  [exchange(): return lax.all_to_all(x, axes, 0, 0, tiled=True)]
    pallas_call x4 -> x3, Pallas kernels: 4.09 us -> 4.72 us  [the longest x1 2.92 us: body(): pl.pallas_call(chunk_kernel, out_shape=(jax.ShapeDtypeStruct((blocks, row...]
  transfers between devices with their start and end apart: 3 -> 3, of which waited for: 2 -> 1; matrix products, arithmetic and copies ran while one was open for 0% -> 0% of each run, Pallas kernels for 2% -> 5%
where the time goes in v5:
time: 88.2 us; the launch traced here: 87.6 us
  blocking collectives  53.4 us (61%)
  starting transfers between devices  20 us (23%)
  Pallas kernels  6.03 us (7%)
  waiting for transfers between devices  5.71 us (6%)
  local copies, waits for them, and re-layouts  2.36 us (3%)
    all_to_all x1, blocking collectives, exchange(): return lax.all_to_all(x, axes, 0, 0, tiled=True)  24.8 us
    all_gather x2, blocking collectives, body(): gate = lax.all_gather(lax.all_gather(gate_input, 'xl'), 'core')  18 us
    all_to_all x2, starting transfers between devices, exchange(): return lax.all_to_all(x, axes, 0, 0, tiled=True)  15.3 us
    all_gather x2, blocking collectives, body(): signals = lax.all_gather(lax.all_gather(signal, 'xl'), 'core')  8.53 us
    all_to_all x2, waiting for transfers between devices, exchange(): return lax.all_to_all(x, axes, 0, 0, tiled=True)  5.71 us
    ppermute x1, starting transfers between devices, body(): far = lax.ppermute(near, 'xh', [(0, 1), (1, 0)])  4.77 us
    pallas_call x1, Pallas kernels, body(): pl.pallas_call(chunk_kernel, out_shape=(jax.ShapeDtypeStruct((blocks, row...  2.92 us
    all_gather x1, blocking collectives, body(): gated = lax.all_gather(gated, 'core')  1.99 us
  transfers between devices with their start and end apart: 3, of which 1 were waited for; matrix products, arithmetic and copies ran while one was open for 0% of the time, Pallas kernels for 5%

profile of v5, /device:TPU:1, one launch (start us, length us, event | category | flops | bytes accessed | tf_op | source)
XLA Modules:
  0.0 87.6 jit_solution(14413111979196788419)
XLA Ops:
  0.0 1.7 %broadcast_in_dim.10 = bf16[8,64,512]{2,1,0:T(8,128)(2,1)} broadcast(bf16[64,512]{1,0:T(8,128)(2,1)} %bitcast.20), dimensions={1,2} | broadcast | bytes 589824 | tf_op jit(solution)/shard_map/broadcast_in_dim | solution.py:177
  1.7 11.0 %all-to-all-start = ((bf16[8,64,512]{2,1,0:T(8,128)(2,1)}), bf16[8,64,512]{2,1,0:T(8,128)(2,1)S(1)}, u32[]{:S(2)}, u32[]{:S(2)}) async-start(bf16[8,64,512]{2,1,0:T(8,128)(2,1)} %broadcast_in_dim.10), calls=%async_computation | async-start | bytes 1048576 | tf_op jit(solution)/shard_map/all_to_all | solution.py:161
  12.7 0.0 copy-done.4
  12.7 0.0 copy-done.5
  12.7 4.8 %all-gather = f32[128,512]{1,0:T(8,128)S(1)} all-gather(f32[64,512]{1,0:T(8,128)S(1)} %convert_multiply_fusion), channel_id=2, replica_groups=mesh['z'=8,'xh'=2,'xl'=2,'core'=2,'chan'=8] {'xl'}, dimensions={0}, use_global_device_ids=true | all-gather | bytes 393216 | tf_op jit(solution)/shard_map/all_gather | solution.py:180
  17.5 0.1 pad_add_fusion.where_ref
  17.6 3.7 %all-gather.1 = f32[4,64,512]{2,1,0:T(8,128)S(1)} all-gather(f32[2,64,512]{2,1,0:T(8,128)S(1)} %bitcast.18), channel_id=3, replica_groups=mesh['z'=8,'xh'=2,'xl'=2,'core'=2,'chan'=8] {'core'}, dimensions={0}, use_global_device_ids=true | all-gather | bytes 786432 | tf_op jit(solution)/shard_map/all_gather | solution.py:180
  21.3 0.0 copy-done
  21.3 0.0 copy-done.1
  21.3 0.7 copy-done.2
  22.0 2.9 %chunk.1 = (f32[4,64,256]{2,1,0:T(8,128)S(1)}, f32[4,16,256]{2,1,0:T(8,128)S(1)}, f32[16,16,256]{2,1,0:T(8,128)}, f32[16,256]{1,0:T(8,128)S(1)}, f32[16,256]{1,0:T(8,128)S(1)}) custom-call(s32[3]{0:T(128)S(1)} %pad_add_fusion.where_ref, f32[2,2,64,512]{3,2,1,0:T(8,128)S(1)} %bitcast.13, f32[16,512]{1,0:T(8,128)S(1)} %copy-done, f32[16,512]{1,0:T(8,128)S(1)} %copy-done.1, ...), custom_call_target="tpu_custom_call" | custom-call | tf_op jit(solution)/shard_map/chunk/pallas_call | solution.py:182
  24.9 5.7 %all-to-all-done.near_ref = bf16[8,64,512]{2,1,0:T(8,128)(2,1)S(1)} async-done(((bf16[8,64,512]{2,1,0:T(8,128)(2,1)}), bf16[8,64,512]{2,1,0:T(8,128)(2,1)S(1)}, u32[]{:S(2)}, u32[]{:S(2)}) %all-to-all-start) | async-done | bytes 524320 | tf_op jit(solution)/shard_map/all_to_all | solution.py:161
  30.6 4.3 %all-to-all-start.1 = ((f32[16,16,256]{2,1,0:T(8,128)}), f32[16,16,256]{2,1,0:T(8,128)S(1)}, u32[]{:S(2)}, u32[]{:S(2)}) async-start(f32[16,16,256]{2,1,0:T(8,128)} %get-tuple-element.13), calls=%async_computation.1 | async-start | bytes 524288 | tf_op jit(solution)/shard_map/all_to_all | solution.py:161
  34.9 4.8 %collective-permute-start = (bf16[8,64,512]{2,1,0:T(8,128)(2,1)S(1)}, bf16[8,64,512]{2,1,0:T(8,128)(2,1)S(1)}, u32[]{:S(2)}, u32[]{:S(2)}) collective-permute-start(bf16[8,64,512]{2,1,0:T(8,128)(2,1)S(1)} %all-to-all-done.near_ref), channel_id=1, source_target_pairs={{0,32},{32,0},{1,33},{33,1},{2,34},{34,2},{3,35},{35,3},{4,36},{36... | collective-permute-start | bytes 1572872 | tf_op jit(solution)/shard_map/ppermute | solution.py:201
  39.7 0.0 copy-done.3
  39.7 15.3 %all-gather.2 = bf16[128,512]{1,0:T(8,128)(2,1)S(1)} all-gather(bf16[64,512]{1,0:T(8,128)(2,1)S(1)} %copy-done.3), channel_id=4, replica_groups=mesh['z'=8,'xh'=2,'xl'=2,'core'=2,'chan'=8] {'xl'}, dimensions={0}, use_global_device_ids=true | all-gather | bytes 196608 | tf_op jit(solution)/shard_map/all_gather | solution.py:181
  54.9 2.8 %all-gather.3 = bf16[4,64,512]{2,1,0:T(8,128)(2,1)S(1)} all-gather(bf16[2,64,512]{2,1,0:T(8,128)(2,1)S(1)} %bitcast.19), channel_id=5, replica_groups=mesh['z'=8,'xh'=2,'xl'=2,'core'=2,'chan'=8] {'core'}, dimensions={0}, use_global_device_ids=true | all-gather | bytes 393216 | tf_op jit(solution)/shard_map/all_gather | solution.py:181
  57.7 0.0 all-to-all-done.1.chunks_ref
  57.7 1.1 %gate.1 = bf16[4,64,256]{2,1,0:T(8,128)(2,1)S(1)} custom-call(s32[3]{0:T(128)S(1)} %pad_add_fusion.where_ref, f32[16,16,256]{2,1,0:T(8,128)S(1)} %all-to-all-done.1.chunks_ref, f32[4,16,256]{2,1,0:T(8,128)S(1)} %get-tuple-element.14.before_ref, f32[16,256]{1,0:T(8,128)S(1)} %get-tuple-element.15.rate_ref, f32[16,256]{1,0:T(8,128)S(1)} %get-tuple-element.16.amp_ref, ...), custom_call_target="tpu_custom_call" | custom-call | tf_op jit(solution)/shard_map/gate/pallas_call | solution.py:203
  58.8 2.0 %all-gather.4 = bf16[8,64,256]{2,1,0:T(8,128)(2,1)S(1)} all-gather(bf16[4,64,256]{2,1,0:T(8,128)(2,1)S(1)} %gate.1), channel_id=6, replica_groups=mesh['z'=8,'xh'=2,'xl'=2,'core'=2,'chan'=8] {'core'}, dimensions={0}, use_global_device_ids=true | all-gather | bytes 393216 | tf_op jit(solution)/shard_map/all_gather | solution.py:211
  60.8 0.0 collective-permute-done.far_ref
  60.8 0.7 project.1
  61.5 24.8 %all_to_all.15 = bf16[32,64,128]{2,1,0:T(8,128)(2,1)S(1)} all-to-all(bf16[32,64,128]{2,1,0:T(8,128)(2,1)S(1)} %bitcast.12), channel_id=1, replica_groups=mesh['z'=8,'xh'=2,'xl'=2,'core'=2,'chan'=8] {'chan','xl','core'}, dimensions={0} | all-to-all | bytes 1048576 | tf_op jit(solution)/shard_map/all_to_all | solution.py:161
  86.3 1.3 %sum_parts.1 = bf16[64,512]{1,0:T(8,128)(2,1)} custom-call(s32[3]{0:T(128)S(1)} %pad_add_fusion.where_ref, bf16[8,2,2,64,128]{4,3,2,1,0:T(8,128)(2,1)S(1)} %bitcast.14), custom_call_target="tpu_custom_call" | custom-call | tf_op jit(solution)/shard_map/sum_parts/pallas_call | solution.py:222
  (7 shorter events, 0.0 us)
Async XLA Ops:
  1.7 11.0 %copy-start.4 = (bf16[64,512]{1,0:T(8,128)(2,1)S(1)}, bf16[64,512]{1,0:T(8,128)(2,1)}, u32[]{:S(2)}) copy-start(bf16[64,512]{1,0:T(8,128)(2,1)} %param.9) | copy-start | bytes 196612
  1.7 11.0 %copy-start.5 = (bf16[64,512]{1,0:T(8,128)(2,1)S(1)}, bf16[64,512]{1,0:T(8,128)(2,1)}, u32[]{:S(2)}) copy-start(bf16[64,512]{1,0:T(8,128)(2,1)} %param.8) | copy-start | bytes 196612
  1.7 29.0 %all-to-all-start = ((bf16[8,64,512]{2,1,0:T(8,128)(2,1)}), bf16[8,64,512]{2,1,0:T(8,128)(2,1)S(1)}, u32[]{:S(2)}, u32[]{:S(2)}) async-start(bf16[8,64,512]{2,1,0:T(8,128)(2,1)} %broadcast_in_dim.10), calls=%async_computation | async-start | bytes 1048576 | tf_op jit(solution)/shard_map/all_to_all | solution.py:161
  17.6 3.7 %copy-start = (f32[16,512]{1,0:T(8,128)S(1)}, f32[16,512]{1,0:T(8,128)}, u32[]{:S(2)}) copy-start(f32[16,512]{1,0:T(8,128)} %rate_ref.1) | copy-start | bytes 98308
  17.6 3.7 %copy-start.1 = (f32[16,512]{1,0:T(8,128)S(1)}, f32[16,512]{1,0:T(8,128)}, u32[]{:S(2)}) copy-start(f32[16,512]{1,0:T(8,128)} %residue_ref.1) | copy-start | bytes 98308
  21.3 0.7 copy-start.2
  30.6 9.0 %copy-start.3 = (bf16[64,512]{1,0:T(8,128)(2,1)S(1)}, bf16[64,512]{1,0:T(8,128)(2,1)}, u32[]{:S(2)}) copy-start(bf16[64,512]{1,0:T(8,128)(2,1)} %param.7) | copy-start | bytes 196612
  30.6 27.1 %all-to-all-start.1 = ((f32[16,16,256]{2,1,0:T(8,128)}), f32[16,16,256]{2,1,0:T(8,128)S(1)}, u32[]{:S(2)}, u32[]{:S(2)}) async-start(f32[16,16,256]{2,1,0:T(8,128)} %get-tuple-element.13), calls=%async_computation.1 | async-start | bytes 524288 | tf_op jit(solution)/shard_map/all_to_all | solution.py:161
  34.9 25.9 %collective-permute-start = (bf16[8,64,512]{2,1,0:T(8,128)(2,1)S(1)}, bf16[8,64,512]{2,1,0:T(8,128)(2,1)S(1)}, u32[]{:S(2)}, u32[]{:S(2)}) collective-permute-start(bf16[8,64,512]{2,1,0:T(8,128)(2,1)S(1)} %all-to-all-done.near_ref), channel_id=1, source_target_pairs={{0,32},{32,0},{1,33},{33,1},{2,34},{34,2},{3,35},{35,3},{4,36},{36... | collective-permute-start | bytes 1572872 | tf_op jit(solution)/shard_map/ppermute | solution.py:201

commit v6 on v5

--- a/solution.py
+++ b/solution.py
@@ -20,20 +20,21 @@
 
 
 def chunk_kernel(
-    where_ref, signals_ref, rate_ref, residue_ref, skip_ref,
+    where_ref, inputs_ref, rate_ref, residue_ref, skip_ref,
     base_ref, before_ref, send_ref, amp_ref, copy_ref, signal_ref, state_ref,
 ):
     blocks, rows, width = base_ref.shape
     modes = rate_ref.shape[0]
     tiles = rows // 8
-    cores = signals_ref.shape[0]
+    cores = inputs_ref.shape[0]
     first_col = where_ref[1] * width
 
     def slab(index, carry):
         cols = pl.ds(pl.multiple_of(index * LANES, LANES), LANES)
         source = pl.ds(pl.multiple_of(first_col + index * LANES, LANES), LANES)
         for i in range(blocks):
-            signal_ref[i] = signals_ref[i % cores, i // cores, :, source]
+            key = inputs_ref[i % cores, i // cores, 0, :, source].astype(F32)
+            signal_ref[i] = key * inputs_ref[i % cores, i // cores, 1, :, source].astype(F32)
         rate = rate_ref[:, source]
         amp = residue_ref[:, source] * jnp.sqrt(1.0 - jnp.exp(-2.0 * rate))
         amp_ref[:, cols] = amp
@@ -84,12 +85,12 @@
 
 
 def gate_kernel(
-    where_ref, chunks_ref, before_ref, rate_ref, amp_ref, base_ref, gate_ref, gated_ref
+    where_ref, chunks_ref, before_ref, rate_ref, amp_ref, base_ref, inputs_ref, gated_ref
 ):
     blocks, rows, width = base_ref.shape
     modes = rate_ref.shape[0]
     tiles = rows // 8
-    cores = gate_ref.shape[0]
+    cores = inputs_ref.shape[0]
     own = where_ref[0]
     first_col = where_ref[1] * width
 
@@ -112,13 +113,15 @@
             full = (before_ref[i, :, cols] + state) * amp
             if i < blocks - 1:
                 state = state * jnp.exp(-float(rows) * rate)
+            parts = []
             for j in range(tiles):
                 part = base_ref[i, 8 * j : 8 * j + 8, cols]
                 scaled = full * steps[j]
                 for m in range(modes):
                     part = part + scaled[m : m + 1] * aheads[m]
-                gate = gate_ref[i % cores, i // cores, 8 * j : 8 * j + 8, source].astype(F32)
-                gated_ref[i, 8 * j : 8 * j + 8, cols] = (gate * part).astype(BF16)
+                parts.append(part)
+            gate = inputs_ref[i % cores, i // cores, 2, :, source].astype(F32)
+            gated_ref[i, :, cols] = (gate * jnp.concatenate(parts, axis=0)).astype(BF16)
         return carry
 
     lax.fori_loop(0, width // LANES, slab, 0)
@@ -176,9 +179,8 @@
 
     own_weight = jnp.broadcast_to(out_weight.T[None], (z_size, out_cols, width))
     near = exchange(own_weight, "z")
-    signal = key_input.astype(F32) * value_input.astype(F32)
-    signals = lax.all_gather(lax.all_gather(signal, "xl"), "core")
-    gate = lax.all_gather(lax.all_gather(gate_input, "xl"), "core")
+    inputs = jnp.stack([key_input, value_input, gate_input])
+    inputs = lax.all_gather(lax.all_gather(inputs, "xl"), "core")
     base, before, state, amplitude, rate = pl.pallas_call(
         chunk_kernel,
         out_shape=(
@@ -196,7 +198,7 @@
         ],
         compiler_params=PARAMS,
         name="chunk",
-    )(where, signals, decay_rate, residue, skip_gain[None, :])
+    )(where, inputs, decay_rate, residue, skip_gain[None, :])
     state, near = lax.optimization_barrier((state, near))
     far = lax.ppermute(near, "xh", [(0, 1), (1, 0)])
     states = exchange(state, ("z", "xh"))
@@ -207,7 +209,7 @@
         out_specs=VMEM,
         compiler_params=PARAMS,
         name="gate",
-    )(where, states, before, rate, amplitude, base, gate)
+    )(where, states, before, rate, amplitude, base, inputs)
     gated = lax.all_gather(gated, "core")
     piece = (rows, high_size * out_cols)
     parts = pl.pallas_call(

time: 88.2 us -> 82.5 us (0.935)
  blocking collectives: 53.4 us -> 38.7 us
  waiting for transfers between devices: 5.71 us -> 13.7 us
  starting transfers between devices: 20 us -> 20.9 us
    all_gather x4 -> x2, blocking collectives: 26.6 us -> 10.1 us  [body(): inputs = lax.all_gather(lax.all_gather(inputs, 'xl'), 'core')]
    all_to_all x2, waiting for transfers between devices: 5.71 us -> 11.8 us  [exchange(): return lax.all_to_all(x, axes, 0, 0, tiled=True)]
    ppermute x1, waiting for transfers between devices: 0.01 us -> 1.83 us  [body(): far = lax.ppermute(near, 'xh', [(0, 1), (1, 0)])]
    all_gather x1, blocking collectives: 1.99 us -> 3.58 us  [body(): gated = lax.all_gather(gated, 'core')]
  transfers between devices with their start and end apart: 3 -> 3, of which waited for: 1 -> 3; matrix products, arithmetic and copies ran while one was open for 0% -> 0% of each run, Pallas kernels for 5% -> 5%
where the time goes in v6:
time: 82.5 us; the launch traced here: 81.8 us
  blocking collectives  38.7 us (47%)
  starting transfers between devices  20.9 us (25%)
  waiting for transfers between devices  13.7 us (17%)
  Pallas kernels  6.03 us (7%)
  local copies, waits for them, and re-layouts  2.36 us (3%)
    all_to_all x1, blocking collectives, exchange(): return lax.all_to_all(x, axes, 0, 0, tiled=True)  25 us
    all_to_all x2, starting transfers between devices, exchange(): return lax.all_to_all(x, axes, 0, 0, tiled=True)  16.1 us
    all_to_all x2, waiting for transfers between devices, exchange(): return lax.all_to_all(x, axes, 0, 0, tiled=True)  11.8 us
    all_gather x2, blocking collectives, body(): inputs = lax.all_gather(lax.all_gather(inputs, 'xl'), 'core')  10.1 us
    ppermute x1, starting transfers between devices, body(): far = lax.ppermute(near, 'xh', [(0, 1), (1, 0)])  4.77 us
    all_gather x1, blocking collectives, body(): gated = lax.all_gather(gated, 'core')  3.58 us
    pallas_call x1, Pallas kernels, body(): pl.pallas_call(chunk_kernel, out_shape=(jax.ShapeDtypeStruct((blocks, row...  2.92 us
    ppermute x1, waiting for transfers between devices, body(): far = lax.ppermute(near, 'xh', [(0, 1), (1, 0)])  1.83 us
  transfers between devices with their start and end apart: 3, of which 3 were waited for; matrix products, arithmetic and copies ran while one was open for 0% of the time, Pallas kernels for 5%

profile of v6, /device:TPU:1, one launch (start us, length us, event | category | flops | bytes accessed | tf_op | source)
XLA Modules:
  0.0 81.8 jit_solution(4873931571599907511)
XLA Ops:
  0.0 1.7 %broadcast_in_dim.10 = bf16[8,64,512]{2,1,0:T(8,128)(2,1)} broadcast(bf16[64,512]{1,0:T(8,128)(2,1)} %bitcast.20), dimensions={1,2} | broadcast | bytes 589824 | tf_op jit(solution)/shard_map/broadcast_in_dim | solution.py:180
  1.7 0.0 copy-start.3
  1.7 0.0 copy-start.4
  1.7 11.0 %all-to-all-start = ((bf16[8,64,512]{2,1,0:T(8,128)(2,1)}), bf16[8,64,512]{2,1,0:T(8,128)(2,1)S(1)}, u32[]{:S(2)}, u32[]{:S(2)}) async-start(bf16[8,64,512]{2,1,0:T(8,128)(2,1)} %broadcast_in_dim.10), calls=%async_computation | async-start | bytes 1048576 | tf_op jit(solution)/shard_map/all_to_all | solution.py:164
  12.7 0.0 copy-done.3
  12.7 0.0 copy-done.4
  12.7 0.0 copy-done.5
  12.7 6.1 %all-gather = bf16[6,64,512]{2,1,0:T(8,128)(2,1)S(1)} all-gather(bf16[3,64,512]{2,1,0:T(8,128)(2,1)S(1)} %pad_maximum_fusion), channel_id=2, replica_groups=mesh['z'=8,'xh'=2,'xl'=2,'core'=2,'chan'=8] {'xl'}, dimensions={0}, use_global_device_ids=true | all-gather | bytes 589824 | tf_op jit(solution)/shard_map/all_gather | solution.py:183
  18.9 0.1 pad_add_fusion.where_ref
  18.9 4.0 %all-gather.1 = bf16[4,3,64,512]{3,2,1,0:T(8,128)(2,1)S(1)} all-gather(bf16[2,3,64,512]{3,2,1,0:T(8,128)(2,1)S(1)} %bitcast.19), channel_id=3, replica_groups=mesh['z'=8,'xh'=2,'xl'=2,'core'=2,'chan'=8] {'core'}, dimensions={0}, use_global_device_ids=true | all-gather | bytes 1179648 | tf_op jit(solution)/shard_map/all_gather | solution.py:183
  22.9 0.0 copy-done
  22.9 0.0 copy-done.1
  22.9 0.7 copy-done.2
  23.6 2.9 %chunk.1 = (f32[4,64,256]{2,1,0:T(8,128)S(1)}, f32[4,16,256]{2,1,0:T(8,128)S(1)}, f32[16,16,256]{2,1,0:T(8,128)}, f32[16,256]{1,0:T(8,128)S(1)}, f32[16,256]{1,0:T(8,128)S(1)}) custom-call(s32[3]{0:T(128)S(1)} %pad_add_fusion.where_ref, bf16[2,2,3,64,512]{4,3,2,1,0:T(8,128)(2,1)S(1)} %bitcast.13, f32[16,512]{1,0:T(8,128)S(1)} %copy-done, ...), custom_call_target="tpu_custom_call" | custom-call | tf_op jit(solution)/shard_map/chunk/pallas_call | solution.py:184
  26.5 4.1 %all-to-all-done.near_ref = bf16[8,64,512]{2,1,0:T(8,128)(2,1)S(1)} async-done(((bf16[8,64,512]{2,1,0:T(8,128)(2,1)}), bf16[8,64,512]{2,1,0:T(8,128)(2,1)S(1)}, u32[]{:S(2)}, u32[]{:S(2)}) %all-to-all-start) | async-done | bytes 524320 | tf_op jit(solution)/shard_map/all_to_all | solution.py:164
  30.6 5.1 %all-to-all-start.1 = ((f32[16,16,256]{2,1,0:T(8,128)}), f32[16,16,256]{2,1,0:T(8,128)S(1)}, u32[]{:S(2)}, u32[]{:S(2)}) async-start(f32[16,16,256]{2,1,0:T(8,128)} %get-tuple-element.13), calls=%async_computation.1 | async-start | bytes 524288 | tf_op jit(solution)/shard_map/all_to_all | solution.py:164
  35.7 4.8 %collective-permute-start = (bf16[8,64,512]{2,1,0:T(8,128)(2,1)S(1)}, bf16[8,64,512]{2,1,0:T(8,128)(2,1)S(1)}, u32[]{:S(2)}, u32[]{:S(2)}) collective-permute-start(bf16[8,64,512]{2,1,0:T(8,128)(2,1)S(1)} %all-to-all-done.near_ref), channel_id=1, source_target_pairs={{0,32},{32,0},{1,33},{33,1},{2,34},{34,2},{3,35},{35,3},{4,36},{36... | collective-permute-start | bytes 1572872 | tf_op jit(solution)/shard_map/ppermute | solution.py:203
  40.5 7.7 %all-to-all-done.1.chunks_ref = f32[16,16,256]{2,1,0:T(8,128)S(1)} async-done(((f32[16,16,256]{2,1,0:T(8,128)}), f32[16,16,256]{2,1,0:T(8,128)S(1)}, u32[]{:S(2)}, u32[]{:S(2)}) %all-to-all-start.1) | async-done | bytes 262176 | tf_op jit(solution)/shard_map/all_to_all | solution.py:164
  48.2 1.1 %gate.1 = bf16[4,64,256]{2,1,0:T(8,128)(2,1)S(1)} custom-call(s32[3]{0:T(128)S(1)} %pad_add_fusion.where_ref, f32[16,16,256]{2,1,0:T(8,128)S(1)} %all-to-all-done.1.chunks_ref, f32[4,16,256]{2,1,0:T(8,128)S(1)} %get-tuple-element.14.before_ref, f32[16,256]{1,0:T(8,128)S(1)} %get-tuple-element.15.rate_ref, f32[16,256]{1,0:T(8,128)S(1)} %get-tuple-element.16.amp_ref, ...), custom_call_target="tpu_custom_call" | custom-call | tf_op jit(solution)/shard_map/gate/pallas_call | solution.py:205
  49.3 3.6 %all-gather.2 = bf16[8,64,256]{2,1,0:T(8,128)(2,1)S(1)} all-gather(bf16[4,64,256]{2,1,0:T(8,128)(2,1)S(1)} %gate.1), channel_id=4, replica_groups=mesh['z'=8,'xh'=2,'xl'=2,'core'=2,'chan'=8] {'core'}, dimensions={0}, use_global_device_ids=true | all-gather | bytes 393216 | tf_op jit(solution)/shard_map/all_gather | solution.py:213
  52.9 1.8 %collective-permute-done.far_ref = bf16[8,64,512]{2,1,0:T(8,128)(2,1)S(1)} collective-permute-done((bf16[8,64,512]{2,1,0:T(8,128)(2,1)S(1)}, bf16[8,64,512]{2,1,0:T(8,128)(2,1)S(1)}, u32[]{:S(2)}, u32[]{:S(2)}) %collective-permute-start) | collective-permute-done | bytes 524320 | tf_op jit(solution)/shard_map/ppermute | solution.py:203
  54.8 0.7 project.1
  55.5 25.0 %all_to_all.15 = bf16[32,64,128]{2,1,0:T(8,128)(2,1)S(1)} all-to-all(bf16[32,64,128]{2,1,0:T(8,128)(2,1)S(1)} %bitcast.15), channel_id=1, replica_groups=mesh['z'=8,'xh'=2,'xl'=2,'core'=2,'chan'=8] {'chan','xl','core'}, dimensions={0} | all-to-all | bytes 1048576 | tf_op jit(solution)/shard_map/all_to_all | solution.py:164
  80.4 1.3 %sum_parts.1 = bf16[64,512]{1,0:T(8,128)(2,1)} custom-call(s32[3]{0:T(128)S(1)} %pad_add_fusion.where_ref, bf16[8,2,2,64,128]{4,3,2,1,0:T(8,128)(2,1)S(1)} %bitcast.16), custom_call_target="tpu_custom_call" | custom-call | tf_op jit(solution)/shard_map/sum_parts/pallas_call | solution.py:224
  (5 shorter events, 0.0 us)
Async XLA Ops:
  1.7 11.0 %copy-start.3 = (bf16[64,512]{1,0:T(8,128)(2,1)S(1)}, bf16[64,512]{1,0:T(8,128)(2,1)}, u32[]{:S(2)}) copy-start(bf16[64,512]{1,0:T(8,128)(2,1)} %param.7) | copy-start | bytes 196612
  1.7 11.0 %copy-start.4 = (bf16[64,512]{1,0:T(8,128)(2,1)S(1)}, bf16[64,512]{1,0:T(8,128)(2,1)}, u32[]{:S(2)}) copy-start(bf16[64,512]{1,0:T(8,128)(2,1)} %param.9) | copy-start | bytes 196612
  1.7 11.0 %copy-start.5 = (bf16[64,512]{1,0:T(8,128)(2,1)S(1)}, bf16[64,512]{1,0:T(8,128)(2,1)}, u32[]{:S(2)}) copy-start(bf16[64,512]{1,0:T(8,128)(2,1)} %param.8) | copy-start | bytes 196612
  1.7 29.0 %all-to-all-start = ((bf16[8,64,512]{2,1,0:T(8,128)(2,1)}), bf16[8,64,512]{2,1,0:T(8,128)(2,1)S(1)}, u32[]{:S(2)}, u32[]{:S(2)}) async-start(bf16[8,64,512]{2,1,0:T(8,128)(2,1)} %broadcast_in_dim.10), calls=%async_computation | async-start | bytes 1048576 | tf_op jit(solution)/shard_map/all_to_all | solution.py:164
  18.9 4.0 %copy-start = (f32[16,512]{1,0:T(8,128)S(1)}, f32[16,512]{1,0:T(8,128)}, u32[]{:S(2)}) copy-start(f32[16,512]{1,0:T(8,128)} %rate_ref.1) | copy-start | bytes 98308
  18.9 4.0 %copy-start.1 = (f32[16,512]{1,0:T(8,128)S(1)}, f32[16,512]{1,0:T(8,128)}, u32[]{:S(2)}) copy-start(f32[16,512]{1,0:T(8,128)} %residue_ref.1) | copy-start | bytes 98308
  22.9 0.7 copy-start.2
  30.6 17.6 %all-to-all-start.1 = ((f32[16,16,256]{2,1,0:T(8,128)}), f32[16,16,256]{2,1,0:T(8,128)S(1)}, u32[]{:S(2)}, u32[]{:S(2)}) async-start(f32[16,16,256]{2,1,0:T(8,128)} %get-tuple-element.13), calls=%async_computation.1 | async-start | bytes 524288 | tf_op jit(solution)/shard_map/all_to_all | solution.py:164
  35.7 19.0 %collective-permute-start = (bf16[8,64,512]{2,1,0:T(8,128)(2,1)S(1)}, bf16[8,64,512]{2,1,0:T(8,128)(2,1)S(1)}, u32[]{:S(2)}, u32[]{:S(2)}) collective-permute-start(bf16[8,64,512]{2,1,0:T(8,128)(2,1)S(1)} %all-to-all-done.near_ref), channel_id=1, source_target_pairs={{0,32},{32,0},{1,33},{33,1},{2,34},{34,2},{3,35},{35,3},{4,36},{36... | collective-permute-start | bytes 1572872 | tf_op jit(solution)/shard_map/ppermute | solution.py:203

commit v7 on v6

--- a/solution.py
+++ b/solution.py
@@ -210,6 +210,7 @@
         compiler_params=PARAMS,
         name="gate",
     )(where, states, before, rate, amplitude, base, inputs)
+    gated, far = lax.optimization_barrier((gated, far))
     gated = lax.all_gather(gated, "core")
     piece = (rows, high_size * out_cols)
     parts = pl.pallas_call(

time: 82.5 us -> 82.2 us (level)
  blocking collectives: 38.7 us -> 53.4 us
  waiting for transfers between devices: 13.7 us -> 4.81 us
  starting transfers between devices: 20.9 us -> 15.6 us
    all_to_all x1 -> x2, blocking collectives: 25 us -> 39 us  [exchange(): return lax.all_to_all(x, axes, 0, 0, tiled=True)]
    all_to_all x2 -> x1, waiting for transfers between devices: 11.8 us -> 4.81 us  [exchange(): return lax.all_to_all(x, axes, 0, 0, tiled=True)]
    all_to_all x2 -> x1, starting transfers between devices: 16.1 us -> 11 us  [exchange(): return lax.all_to_all(x, axes, 0, 0, tiled=True)]
    ppermute x1, waiting for transfers between devices: 1.83 us -> 0.01 us  [body(): far = lax.ppermute(near, 'xh', [(0, 1), (1, 0)])]
  transfers between devices with their start and end apart: 3 -> 2, of which waited for: 3 -> 1; matrix products, arithmetic and copies ran while one was open for 0% -> 0% of each run, Pallas kernels for 5% -> 4%
where the time goes in v7:
time: 82.2 us; the launch traced here: 81.7 us
  blocking collectives  53.4 us (65%)
  starting transfers between devices  15.6 us (19%)
  Pallas kernels  5.33 us (6%)
  waiting for transfers between devices  4.81 us (6%)
  local copies, waits for them, and re-layouts  2.37 us (3%)
    all_to_all x2, blocking collectives, exchange(): return lax.all_to_all(x, axes, 0, 0, tiled=True)  39 us
    all_to_all x1, starting transfers between devices, exchange(): return lax.all_to_all(x, axes, 0, 0, tiled=True)  11 us
    all_gather x2, blocking collectives, body(): inputs = lax.all_gather(lax.all_gather(inputs, 'xl'), 'core')  10.1 us
    all_to_all x1, waiting for transfers between devices, exchange(): return lax.all_to_all(x, axes, 0, 0, tiled=True)  4.81 us
    ppermute x1, starting transfers between devices, body(): far = lax.ppermute(near, 'xh', [(0, 1), (1, 0)])  4.64 us
    all_gather x1, blocking collectives, body(): gated = lax.all_gather(gated, 'core')  4.31 us
    pallas_call x1, Pallas kernels, body(): pl.pallas_call(chunk_kernel, out_shape=(jax.ShapeDtypeStruct((blocks, row...  2.21 us
    broadcast_in_dim x1, local copies, waits for them, and re-layouts, body(): own_weight = jnp.broadcast_to(out_weight.T[None], (z_size, out_cols, width))  1.68 us
  transfers between devices with their start and end apart: 2, of which 1 were waited for; matrix products, arithmetic and copies ran while one was open for 0% of the time, Pallas kernels for 4%

profile of v7, /device:TPU:1, one launch (start us, length us, event | category | flops | bytes accessed | tf_op | source)
XLA Modules:
  0.0 81.7 jit_solution(5276790524366812183)
XLA Ops:
  0.0 1.7 %broadcast_in_dim.10 = bf16[8,64,512]{2,1,0:T(8,128)(2,1)} broadcast(bf16[64,512]{1,0:T(8,128)(2,1)} %bitcast.20), dimensions={1,2} | broadcast | bytes 589824 | tf_op jit(solution)/shard_map/broadcast_in_dim | solution.py:180
  1.7 0.0 copy-start.3
  1.7 0.0 copy-start.4
  1.7 0.0 copy-start.5
  1.7 11.0 %all-to-all-start = ((bf16[8,64,512]{2,1,0:T(8,128)(2,1)}), bf16[8,64,512]{2,1,0:T(8,128)(2,1)S(1)}, u32[]{:S(2)}, u32[]{:S(2)}) async-start(bf16[8,64,512]{2,1,0:T(8,128)(2,1)} %broadcast_in_dim.10), calls=%async_computation | async-start | bytes 1048576 | tf_op jit(solution)/shard_map/all_to_all | solution.py:164
  12.7 0.0 copy-done.3
  12.7 0.0 copy-done.4
  12.7 0.0 copy-done.5
  12.7 6.1 %all-gather = bf16[6,64,512]{2,1,0:T(8,128)(2,1)S(1)} all-gather(bf16[3,64,512]{2,1,0:T(8,128)(2,1)S(1)} %pad_maximum_fusion), channel_id=2, replica_groups=mesh['z'=8,'xh'=2,'xl'=2,'core'=2,'chan'=8] {'xl'}, dimensions={0}, use_global_device_ids=true | all-gather | bytes 589824 | tf_op jit(solution)/shard_map/all_gather | solution.py:183
  18.9 0.1 pad_add_fusion.where_ref
  19.0 4.0 %all-gather.1 = bf16[4,3,64,512]{3,2,1,0:T(8,128)(2,1)S(1)} all-gather(bf16[2,3,64,512]{3,2,1,0:T(8,128)(2,1)S(1)} %bitcast.19), channel_id=3, replica_groups=mesh['z'=8,'xh'=2,'xl'=2,'core'=2,'chan'=8] {'core'}, dimensions={0}, use_global_device_ids=true | all-gather | bytes 1179648 | tf_op jit(solution)/shard_map/all_gather | solution.py:183
  22.9 0.0 copy-done
  22.9 0.0 copy-done.1
  22.9 0.7 copy-done.2
  23.6 2.2 %chunk.1 = (f32[4,64,256]{2,1,0:T(8,128)S(1)}, f32[4,16,256]{2,1,0:T(8,128)S(1)}, f32[16,16,256]{2,1,0:T(8,128)S(1)}, f32[16,256]{1,0:T(8,128)S(1)}, f32[16,256]{1,0:T(8,128)S(1)}) custom-call(s32[3]{0:T(128)S(1)} %pad_add_fusion.where_ref, bf16[2,2,3,64,512]{4,3,2,1,0:T(8,128)(2,1)S(1)} %bitcast.13, f32[16,512]{1,0:T(8,128)S(1)} %copy-done, ...), custom_call_target="tpu_custom_call" | custom-call | tf_op jit(solution)/shard_map/chunk/pallas_call | solution.py:184
  25.8 4.8 %all-to-all-done.near_ref = bf16[8,64,512]{2,1,0:T(8,128)(2,1)S(1)} async-done(((bf16[8,64,512]{2,1,0:T(8,128)(2,1)}), bf16[8,64,512]{2,1,0:T(8,128)(2,1)S(1)}, u32[]{:S(2)}, u32[]{:S(2)}) %all-to-all-start) | async-done | bytes 524320 | tf_op jit(solution)/shard_map/all_to_all | solution.py:164
  30.6 4.6 %collective-permute-start = (bf16[8,64,512]{2,1,0:T(8,128)(2,1)S(1)}, bf16[8,64,512]{2,1,0:T(8,128)(2,1)S(1)}, u32[]{:S(2)}, u32[]{:S(2)}) collective-permute-start(bf16[8,64,512]{2,1,0:T(8,128)(2,1)S(1)} %all-to-all-done.near_ref), channel_id=1, source_target_pairs={{0,32},{32,0},{1,33},{33,1},{2,34},{34,2},{3,35},{35,3},{4,36},{36... | collective-permute-start | bytes 1572872 | tf_op jit(solution)/shard_map/ppermute | solution.py:203
  35.3 14.9 %all_to_all.15.chunks_ref = f32[16,16,256]{2,1,0:T(8,128)S(1)} all-to-all(f32[16,16,256]{2,1,0:T(8,128)S(1)} %get-tuple-element.15), channel_id=1, replica_groups=mesh['z'=8,'xh'=2,'xl'=2,'core'=2,'chan'=8] {'z','xh'}, dimensions={0} | all-to-all | bytes 524288 | tf_op jit(solution)/shard_map/all_to_all | solution.py:164
  50.1 1.1 %gate.1 = bf16[4,64,256]{2,1,0:T(8,128)(2,1)S(1)} custom-call(s32[3]{0:T(128)S(1)} %pad_add_fusion.where_ref, f32[16,16,256]{2,1,0:T(8,128)S(1)} %all_to_all.15.chunks_ref, f32[4,16,256]{2,1,0:T(8,128)S(1)} %get-tuple-element.16.before_ref, f32[16,256]{1,0:T(8,128)S(1)} %get-tuple-element.17.rate_ref, f32[16,256]{1,0:T(8,128)S(1)} %get-tuple-element.18.amp_ref, ...), custom_call_target="tpu_custom_call" | custom-call | tf_op jit(solution)/shard_map/gate/pallas_call | solution.py:205
  51.2 0.0 collective-permute-done.far_ref
  51.3 4.3 %all-gather.2 = bf16[8,64,256]{2,1,0:T(8,128)(2,1)S(1)} all-gather(bf16[4,64,256]{2,1,0:T(8,128)(2,1)S(1)} %gate.1), channel_id=4, replica_groups=mesh['z'=8,'xh'=2,'xl'=2,'core'=2,'chan'=8] {'core'}, dimensions={0}, use_global_device_ids=true | all-gather | bytes 393216 | tf_op jit(solution)/shard_map/all_gather | solution.py:214
  55.6 0.7 project.1
  56.3 24.1 %all_to_all.16 = bf16[32,64,128]{2,1,0:T(8,128)(2,1)S(1)} all-to-all(bf16[32,64,128]{2,1,0:T(8,128)(2,1)S(1)} %bitcast.15), channel_id=1, replica_groups=mesh['z'=8,'xh'=2,'xl'=2,'core'=2,'chan'=8] {'chan','xl','core'}, dimensions={0} | all-to-all | bytes 1048576 | tf_op jit(solution)/shard_map/all_to_all | solution.py:164
  80.4 1.3 %sum_parts.1 = bf16[64,512]{1,0:T(8,128)(2,1)} custom-call(s32[3]{0:T(128)S(1)} %pad_add_fusion.where_ref, bf16[8,2,2,64,128]{4,3,2,1,0:T(8,128)(2,1)S(1)} %bitcast.16), custom_call_target="tpu_custom_call" | custom-call | tf_op jit(solution)/shard_map/sum_parts/pallas_call | solution.py:225
  (4 shorter events, 0.0 us)
Async XLA Ops:
  1.7 11.0 %copy-start.3 = (bf16[64,512]{1,0:T(8,128)(2,1)S(1)}, bf16[64,512]{1,0:T(8,128)(2,1)}, u32[]{:S(2)}) copy-start(bf16[64,512]{1,0:T(8,128)(2,1)} %param.7) | copy-start | bytes 196612
  1.7 11.0 %copy-start.4 = (bf16[64,512]{1,0:T(8,128)(2,1)S(1)}, bf16[64,512]{1,0:T(8,128)(2,1)}, u32[]{:S(2)}) copy-start(bf16[64,512]{1,0:T(8,128)(2,1)} %param.9) | copy-start | bytes 196612
  1.7 11.0 %copy-start.5 = (bf16[64,512]{1,0:T(8,128)(2,1)S(1)}, bf16[64,512]{1,0:T(8,128)(2,1)}, u32[]{:S(2)}) copy-start(bf16[64,512]{1,0:T(8,128)(2,1)} %param.8) | copy-start | bytes 196612
  1.7 29.0 %all-to-all-start = ((bf16[8,64,512]{2,1,0:T(8,128)(2,1)}), bf16[8,64,512]{2,1,0:T(8,128)(2,1)S(1)}, u32[]{:S(2)}, u32[]{:S(2)}) async-start(bf16[8,64,512]{2,1,0:T(8,128)(2,1)} %broadcast_in_dim.10), calls=%async_computation | async-start | bytes 1048576 | tf_op jit(solution)/shard_map/all_to_all | solution.py:164
  18.9 4.0 %copy-start = (f32[16,512]{1,0:T(8,128)S(1)}, f32[16,512]{1,0:T(8,128)}, u32[]{:S(2)}) copy-start(f32[16,512]{1,0:T(8,128)} %rate_ref.1) | copy-start | bytes 98308
  18.9 4.0 %copy-start.1 = (f32[16,512]{1,0:T(8,128)S(1)}, f32[16,512]{1,0:T(8,128)}, u32[]{:S(2)}) copy-start(f32[16,512]{1,0:T(8,128)} %residue_ref.1) | copy-start | bytes 98308
  22.9 0.7 copy-start.2
  30.6 20.6 %collective-permute-start = (bf16[8,64,512]{2,1,0:T(8,128)(2,1)S(1)}, bf16[8,64,512]{2,1,0:T(8,128)(2,1)S(1)}, u32[]{:S(2)}, u32[]{:S(2)}) collective-permute-start(bf16[8,64,512]{2,1,0:T(8,128)(2,1)S(1)} %all-to-all-done.near_ref), channel_id=1, source_target_pairs={{0,32},{32,0},{1,33},{33,1},{2,34},{34,2},{3,35},{35,3},{4,36},{36... | collective-permute-start | bytes 1572872 | tf_op jit(solution)/shard_map/ppermute | solution.py:203

commit v8 on v6

--- a/solution.py
+++ b/solution.py
@@ -8,7 +8,7 @@
 
 F32 = jnp.float32
 BF16 = jnp.bfloat16
-SEQ = ("z", "xh", "xl", "core")
+SEQ = ("zh", "zl", "xh", "xl", "core")
 LANES = 128
 VMEM = pl.BlockSpec(memory_space=pltpu.VMEM)
 SMEM = pl.BlockSpec(memory_space=pltpu.SMEM)
@@ -127,18 +127,20 @@
     lax.fori_loop(0, width // LANES, slab, 0)
 
 
-def project_kernel(gated_ref, near_ref, far_ref, out_ref):
+def project_kernel(where_ref, gated_ref, weight_ref, other_ref, out_ref):
+    own_low = where_ref[3]
     cores, shared, rows, half = gated_ref.shape
     gated = [gated_ref[core].reshape(shared * rows, half) for core in range(cores)]
-    for j in range(out_ref.shape[0]):
-        total = 0.0
-        for core in range(cores):
-            depth = slice(core * half, (core + 1) * half)
-            weight = jnp.concatenate([near_ref[j, :, depth], far_ref[j, :, depth]], axis=0)
-            total = total + lax.dot_general(
-                gated[core], weight, (((1,), (1,)), ((), ())), preferred_element_type=F32
-            )
-        out_ref[j] = total.astype(BF16).reshape(out_ref.shape[1:])
+    for ref, low in ((weight_ref, own_low), (other_ref, 1 - own_low)):
+        for j in range(ref.shape[1]):
+            total = 0.0
+            for core in range(cores):
+                depth = slice(core * half, (core + 1) * half)
+                weight = jnp.concatenate([ref[i, j, :, depth] for i in range(2)], axis=0)
+                total = total + lax.dot_general(
+                    gated[core], weight, (((1,), (1,)), ((), ())), preferred_element_type=F32
+                )
+            out_ref[2 * j + low] = total.astype(BF16).reshape(out_ref.shape[1:])
 
 
 def sum_kernel(where_ref, parts_ref, out_ref):
@@ -167,20 +169,27 @@
 def body(gate_input, key_input, value_input, decay_rate, residue, skip_gain, out_weight):
     rows, width = key_input.shape
     modes = decay_rate.shape[0]
-    z_size, high_size, low_size, cores = (lax.axis_size(a) for a in SEQ)
+    zh_size, zl_size, high_size, low_size, cores = (lax.axis_size(a) for a in SEQ)
     y_size = lax.axis_size("chan")
     out_cols = out_weight.shape[1]
-    chunks = z_size * high_size
+    chunks = zh_size * zl_size * high_size
     blocks = low_size * cores
     half = width // cores
     where = jnp.stack(
-        [lax.axis_index(("z", "xh")), lax.axis_index("core"), lax.axis_index("xh")]
+        [
+            lax.axis_index(("zh", "zl", "xh")),
+            lax.axis_index("core"),
+            lax.axis_index("xh"),
+            lax.axis_index("zl"),
+        ]
     ).astype(jnp.int32)
 
-    own_weight = jnp.broadcast_to(out_weight.T[None], (z_size, out_cols, width))
-    near = exchange(own_weight, "z")
-    inputs = jnp.stack([key_input, value_input, gate_input])
-    inputs = lax.all_gather(lax.all_gather(inputs, "xl"), "core")
+    own_weight = jnp.broadcast_to(out_weight.T[None], (zh_size, out_cols, width))
+    weight = exchange(own_weight, "zh")
+    inputs = lax.all_gather(jnp.stack([key_input, value_input, gate_input]), "xl")
+    inputs, weight = lax.optimization_barrier((inputs, weight))
+    far = lax.ppermute(weight, "xh", [(0, 1), (1, 0)])
+    inputs = lax.all_gather(inputs, "core")
     base, before, state, amplitude, rate = pl.pallas_call(
         chunk_kernel,
         out_shape=(
@@ -199,9 +208,10 @@
         compiler_params=PARAMS,
         name="chunk",
     )(where, inputs, decay_rate, residue, skip_gain[None, :])
-    state, near = lax.optimization_barrier((state, near))
-    far = lax.ppermute(near, "xh", [(0, 1), (1, 0)])
-    states = exchange(state, ("z", "xh"))
+    state, weight, far = lax.optimization_barrier((state, weight, far))
+    weight = jnp.stack([weight, far])
+    other = lax.ppermute(weight, "zl", [(0, 1), (1, 0)])
+    states = exchange(state, ("zh", "zl", "xh"))
     gated = pl.pallas_call(
         gate_kernel,
         out_shape=jax.ShapeDtypeStruct((blocks, rows, half), BF16),
@@ -215,11 +225,11 @@
     parts = pl.pallas_call(
         project_kernel,
         out_shape=jax.ShapeDtypeStruct((y_size, blocks) + piece, BF16),
-        in_specs=[VMEM] * 3,
+        in_specs=[SMEM] + [VMEM] * 3,
         out_specs=VMEM,
         compiler_params=PARAMS,
         name="project",
-    )(gated, near, far)
+    )(where, gated, weight, other)
     parts = exchange(parts.reshape((y_size * blocks,) + piece), ("chan", "xl", "core"))
     return pl.pallas_call(
         sum_kernel,
@@ -232,7 +242,7 @@
 
 
 def solution(mesh):
-    finer = Mesh(mesh.devices.reshape(8, 2, 2, 2, 8), SEQ + ("chan",))
+    finer = Mesh(mesh.devices.reshape(4, 2, 2, 2, 2, 8), SEQ + ("chan",))
     return jax.shard_map(
         body,
         mesh=finer,

time: 82.5 us -> 86.8 us (1.052)
  blocking collectives: 38.7 us -> 44.2 us
  waiting for transfers between devices: 13.7 us -> 9.75 us
  starting transfers between devices: 20.9 us -> 22.4 us
    ppermute x1 -> x2, starting transfers between devices: 4.77 us -> 7.87 us  [the longest x1 4.64 us: body(): far = lax.ppermute(weight, 'xh', [(0, 1), (1, 0)])]
    all_gather x1, blocking collectives: 3.58 us -> 6.65 us  [body(): gated = lax.all_gather(gated, 'core')]
    all_gather x2, blocking collectives: 10.1 us -> 12.5 us  [the longest x1 6.39 us: body(): inputs = lax.all_gather(inputs, 'core')]
    all_to_all x2, waiting for transfers between devices: 11.8 us -> 9.75 us  [exchange(): return lax.all_to_all(x, axes, 0, 0, tiled=True)]
    ppermute x1 -> x2, waiting for transfers between devices: 1.83 us -> 0.01 us  [the longest x1 0.01 us: body(): far = lax.ppermute(weight, 'xh', [(0, 1), (1, 0)])]
    all_to_all x2, starting transfers between devices: 16.1 us -> 14.5 us  [exchange(): return lax.all_to_all(x, axes, 0, 0, tiled=True)]
  transfers between devices with their start and end apart: 3 -> 4, of which waited for: 3 -> 2; matrix products, arithmetic and copies ran while one was open for 0% -> 0% of each run, Pallas kernels for 5% -> 5%
where the time goes in v8:
time: 86.8 us; the launch traced here: 85.4 us
  blocking collectives  44.2 us (51%)
  starting transfers between devices  22.4 us (26%)
  waiting for transfers between devices  9.75 us (11%)
  Pallas kernels  6.58 us (8%)
  local copies, waits for them, and re-layouts  2.26 us (3%)
    all_to_all x1, blocking collectives, exchange(): return lax.all_to_all(x, axes, 0, 0, tiled=True)  25 us
    all_to_all x2, starting transfers between devices, exchange(): return lax.all_to_all(x, axes, 0, 0, tiled=True)  14.5 us
    all_to_all x2, waiting for transfers between devices, exchange(): return lax.all_to_all(x, axes, 0, 0, tiled=True)  9.75 us
    all_gather x1, blocking collectives, body(): gated = lax.all_gather(gated, 'core')  6.65 us
    all_gather x1, blocking collectives, body(): inputs = lax.all_gather(inputs, 'core')  6.39 us
    all_gather x1, blocking collectives, body(): lax.all_gather(jnp.stack([key_input, value_input, gate_input]), 'xl')  6.13 us
    ppermute x1, starting transfers between devices, body(): far = lax.ppermute(weight, 'xh', [(0, 1), (1, 0)])  4.64 us
    ppermute x1, starting transfers between devices, body(): other = lax.ppermute(weight, 'zl', [(0, 1), (1, 0)])  3.23 us
  transfers between devices with their start and end apart: 4, of which 2 were waited for; matrix products, arithmetic and copies ran while one was open for 0% of the time, Pallas kernels for 5%

profile of v8, /device:TPU:1, one launch (start us, length us, event | category | flops | bytes accessed | tf_op | source)
XLA Modules:
  0.0 85.4 jit_solution(3728308240044953081)
XLA Ops:
  0.0 1.6 %broadcast_in_dim.4 = bf16[4,64,512]{2,1,0:T(8,128)(2,1)} broadcast(bf16[64,512]{1,0:T(8,128)(2,1)} %bitcast.25), dimensions={1,2} | broadcast | bytes 327680 | tf_op jit(solution)/shard_map/broadcast_in_dim | solution.py:187
  1.6 11.0 %all-to-all-start = ((bf16[4,64,512]{2,1,0:T(8,128)(2,1)}), bf16[4,64,512]{2,1,0:T(8,128)(2,1)S(1)}, u32[]{:S(2)}, u32[]{:S(2)}) async-start(bf16[4,64,512]{2,1,0:T(8,128)(2,1)} %broadcast_in_dim.4), calls=%async_computation | async-start | bytes 524288 | tf_op jit(solution)/shard_map/all_to_all | solution.py:166
  12.5 0.0 copy-done.3
  12.6 0.0 copy-done.4
  12.6 0.0 copy-done.5
  12.6 6.1 %all-gather = bf16[6,64,512]{2,1,0:T(8,128)(2,1)S(1)} all-gather(bf16[3,64,512]{2,1,0:T(8,128)(2,1)S(1)} %pad_maximum_fusion.1), channel_id=2, replica_groups=mesh['zh'=4,'zl'=2,'xh'=2,'xl'=2,'core'=2,'chan'=8] {'xl'}, dimensions={0}, use_global_device_ids=true | all-gather | bytes 589824 | tf_op jit(solution)/shard_map/all_gather | solution.py:189
  18.7 2.0 %all-to-all-done = bf16[4,64,512]{2,1,0:T(8,128)(2,1)S(1)} async-done(((bf16[4,64,512]{2,1,0:T(8,128)(2,1)}), bf16[4,64,512]{2,1,0:T(8,128)(2,1)S(1)}, u32[]{:S(2)}, u32[]{:S(2)}) %all-to-all-start) | async-done | bytes 262176 | tf_op jit(solution)/shard_map/all_to_all | solution.py:166
  20.7 4.6 %collective-permute-start = (bf16[4,64,512]{2,1,0:T(8,128)(2,1)S(1)}, bf16[4,64,512]{2,1,0:T(8,128)(2,1)S(1)}, u32[]{:S(2)}, u32[]{:S(2)}) collective-permute-start(bf16[4,64,512]{2,1,0:T(8,128)(2,1)S(1)} %all-to-all-done), channel_id=1, source_target_pairs={{0,32},{32,0},{1,33},{33,1},{2,34},{34,2},{3,35},{35,3},{4,36},{36... | collective-permute-start | bytes 786440 | tf_op jit(solution)/shard_map/ppermute | solution.py:191
  25.3 0.1 pad_add_fusion.where_ref
  25.4 6.4 %all-gather.1 = bf16[4,3,64,512]{3,2,1,0:T(8,128)(2,1)S(1)} all-gather(bf16[2,3,64,512]{3,2,1,0:T(8,128)(2,1)S(1)} %bitcast.22), channel_id=3, replica_groups=mesh['zh'=4,'zl'=2,'xh'=2,'xl'=2,'core'=2,'chan'=8] {'core'}, dimensions={0}, use_global_device_ids=true | all-gather | bytes 1179648 | tf_op jit(solution)/shard_map/all_gather | solution.py:192
  31.8 0.0 copy-done
  31.8 0.7 copy-done.2
  32.5 2.9 %chunk.1 = (f32[4,64,256]{2,1,0:T(8,128)S(1)}, f32[4,16,256]{2,1,0:T(8,128)S(1)}, f32[16,16,256]{2,1,0:T(8,128)}, f32[16,256]{1,0:T(8,128)S(1)}, f32[16,256]{1,0:T(8,128)S(1)}) custom-call(s32[4]{0:T(128)S(1)} %pad_add_fusion.where_ref, bf16[2,2,3,64,512]{4,3,2,1,0:T(8,128)(2,1)S(1)} %bitcast.16, f32[16,512]{1,0:T(8,128)S(1)} %copy-done, ...), custom_call_target="tpu_custom_call" | custom-call | tf_op jit(solution)/shard_map/chunk/pallas_call | solution.py:193
  35.4 0.0 collective-permute-done
  35.4 3.5 %all-to-all-start.1 = ((f32[16,16,256]{2,1,0:T(8,128)}), f32[16,16,256]{2,1,0:T(8,128)S(1)}, u32[]{:S(2)}, u32[]{:S(2)}) async-start(f32[16,16,256]{2,1,0:T(8,128)} %get-tuple-element.18), calls=%async_computation.1 | async-start | bytes 524288 | tf_op jit(solution)/shard_map/all_to_all | solution.py:166
  39.0 0.1 pad_maximum_fusion.weight_ref
  39.0 3.2 %collective-permute-start.1 = (bf16[2,4,64,512]{3,2,1,0:T(8,128)(2,1)S(1)}, bf16[2,4,64,512]{3,2,1,0:T(8,128)(2,1)S(1)}, u32[]{:S(2)}, u32[]{:S(2)}) collective-permute-start(bf16[2,4,64,512]{3,2,1,0:T(8,128)(2,1)S(1)} %pad_maximum_fusion.weight_ref), channel_id=1, source_target_pairs={{0,64},{64,0},{1,65},{65,1},{2,66},{66,2},{3,67},{67,3},{4,68},{68... | collective-permute-start | bytes 1572872 | tf_op jit(solution)/shard_map/ppermute | solution.py:213
  42.3 7.8 %all-to-all-done.1.chunks_ref = f32[16,16,256]{2,1,0:T(8,128)S(1)} async-done(((f32[16,16,256]{2,1,0:T(8,128)}), f32[16,16,256]{2,1,0:T(8,128)S(1)}, u32[]{:S(2)}, u32[]{:S(2)}) %all-to-all-start.1) | async-done | bytes 262176 | tf_op jit(solution)/shard_map/all_to_all | solution.py:166
  50.0 1.1 %gate.1 = bf16[4,64,256]{2,1,0:T(8,128)(2,1)S(1)} custom-call(s32[4]{0:T(128)S(1)} %pad_add_fusion.where_ref, f32[16,16,256]{2,1,0:T(8,128)S(1)} %all-to-all-done.1.chunks_ref, f32[4,16,256]{2,1,0:T(8,128)S(1)} %get-tuple-element.19.before_ref, f32[16,256]{1,0:T(8,128)S(1)} %get-tuple-element.20.rate_ref, f32[16,256]{1,0:T(8,128)S(1)} %get-tuple-element.21.amp_ref, ...), custom_call_target="tpu_custom_call" | custom-call | tf_op jit(solution)/shard_map/gate/pallas_call | solution.py:215
  51.1 6.7 %all-gather.2 = bf16[8,64,256]{2,1,0:T(8,128)(2,1)S(1)} all-gather(bf16[4,64,256]{2,1,0:T(8,128)(2,1)S(1)} %gate.1), channel_id=4, replica_groups=mesh['zh'=4,'zl'=2,'xh'=2,'xl'=2,'core'=2,'chan'=8] {'core'}, dimensions={0}, use_global_device_ids=true | all-gather | bytes 393216 | tf_op jit(solution)/shard_map/all_gather | solution.py:223
  57.8 0.0 collective-permute-done.1.other_ref
  57.8 1.2 %project.1 = bf16[8,4,64,128]{3,2,1,0:T(8,128)(2,1)S(1)} custom-call(s32[4]{0:T(128)S(1)} %pad_add_fusion.where_ref, bf16[2,4,64,256]{3,2,1,0:T(8,128)(2,1)S(1)} %bitcast.20, bf16[2,4,64,512]{3,2,1,0:T(8,128)(2,1)S(1)} %pad_maximum_fusion.weight_ref, bf16[2,4,64,512]{3,2,1,0:T(8,128)(2,1)S(1)} %collective-permute-done.1.other_ref), custom_call_target="tpu_custom_call" | custom-call | tf_op jit(solution)/shard_map/project/pallas_call | solution.py:225
  59.1 25.0 %all_to_all.15 = bf16[32,64,128]{2,1,0:T(8,128)(2,1)S(1)} all-to-all(bf16[32,64,128]{2,1,0:T(8,128)(2,1)S(1)} %bitcast.19), channel_id=1, replica_groups=mesh['zh'=4,'zl'=2,'xh'=2,'xl'=2,'core'=2,'chan'=8] {'chan','xl','core'}, dimensions={0} | all-to-all | bytes 1048576 | tf_op jit(solution)/shard_map/all_to_all | solution.py:166
  84.1 1.3 %sum_parts.1 = bf16[64,512]{1,0:T(8,128)(2,1)} custom-call(s32[4]{0:T(128)S(1)} %pad_add_fusion.where_ref, bf16[8,2,2,64,128]{4,3,2,1,0:T(8,128)(2,1)S(1)} %bitcast.18), custom_call_target="tpu_custom_call" | custom-call | tf_op jit(solution)/shard_map/sum_parts/pallas_call | solution.py:234
  (8 shorter events, 0.0 us)
Async XLA Ops:
  1.6 11.0 %copy-start.3 = (bf16[64,512]{1,0:T(8,128)(2,1)S(1)}, bf16[64,512]{1,0:T(8,128)(2,1)}, u32[]{:S(2)}) copy-start(bf16[64,512]{1,0:T(8,128)(2,1)} %param.7) | copy-start | bytes 196612
  1.6 11.0 %copy-start.4 = (bf16[64,512]{1,0:T(8,128)(2,1)S(1)}, bf16[64,512]{1,0:T(8,128)(2,1)}, u32[]{:S(2)}) copy-start(bf16[64,512]{1,0:T(8,128)(2,1)} %param.9) | copy-start | bytes 196612
  1.6 11.0 %copy-start.5 = (bf16[64,512]{1,0:T(8,128)(2,1)S(1)}, bf16[64,512]{1,0:T(8,128)(2,1)}, u32[]{:S(2)}) copy-start(bf16[64,512]{1,0:T(8,128)(2,1)} %param.8) | copy-start | bytes 196612
  1.6 19.1 %all-to-all-start = ((bf16[4,64,512]{2,1,0:T(8,128)(2,1)}), bf16[4,64,512]{2,1,0:T(8,128)(2,1)S(1)}, u32[]{:S(2)}, u32[]{:S(2)}) async-start(bf16[4,64,512]{2,1,0:T(8,128)(2,1)} %broadcast_in_dim.4), calls=%async_computation | async-start | bytes 524288 | tf_op jit(solution)/shard_map/all_to_all | solution.py:166
  20.7 14.7 %collective-permute-start = (bf16[4,64,512]{2,1,0:T(8,128)(2,1)S(1)}, bf16[4,64,512]{2,1,0:T(8,128)(2,1)S(1)}, u32[]{:S(2)}, u32[]{:S(2)}) collective-permute-start(bf16[4,64,512]{2,1,0:T(8,128)(2,1)S(1)} %all-to-all-done), channel_id=1, source_target_pairs={{0,32},{32,0},{1,33},{33,1},{2,34},{34,2},{3,35},{35,3},{4,36},{36... | collective-permute-start | bytes 786440 | tf_op jit(solution)/shard_map/ppermute | solution.py:191
  25.4 6.4 %copy-start = (f32[16,512]{1,0:T(8,128)S(1)}, f32[16,512]{1,0:T(8,128)}, u32[]{:S(2)}) copy-start(f32[16,512]{1,0:T(8,128)} %rate_ref.1) | copy-start | bytes 98308
  25.4 6.4 %copy-start.1 = (f32[16,512]{1,0:T(8,128)S(1)}, f32[16,512]{1,0:T(8,128)}, u32[]{:S(2)}) copy-start(f32[16,512]{1,0:T(8,128)} %residue_ref.1) | copy-start | bytes 98308
  31.8 0.7 copy-start.2
  35.4 14.6 %all-to-all-start.1 = ((f32[16,16,256]{2,1,0:T(8,128)}), f32[16,16,256]{2,1,0:T(8,128)S(1)}, u32[]{:S(2)}, u32[]{:S(2)}) async-start(f32[16,16,256]{2,1,0:T(8,128)} %get-tuple-element.18), calls=%async_computation.1 | async-start | bytes 524288 | tf_op jit(solution)/shard_map/all_to_all | solution.py:166
  39.0 18.8 %collective-permute-start.1 = (bf16[2,4,64,512]{3,2,1,0:T(8,128)(2,1)S(1)}, bf16[2,4,64,512]{3,2,1,0:T(8,128)(2,1)S(1)}, u32[]{:S(2)}, u32[]{:S(2)}) collective-permute-start(bf16[2,4,64,512]{3,2,1,0:T(8,128)(2,1)S(1)} %pad_maximum_fusion.weight_ref), channel_id=1, source_target_pairs={{0,64},{64,0},{1,65},{65,1},{2,66},{66,2},{3,67},{67,3},{4,68},{68... | collective-permute-start | bytes 1572872 | tf_op jit(solution)/shard_map/ppermute | solution.py:213

commit v9 on v8

--- a/solution.py
+++ b/solution.py
@@ -127,16 +127,16 @@
     lax.fori_loop(0, width // LANES, slab, 0)
 
 
-def project_kernel(where_ref, gated_ref, weight_ref, other_ref, out_ref):
+def project_kernel(where_ref, gated_ref, own_ref, x_ref, z_ref, both_ref, out_ref):
     own_low = where_ref[3]
     cores, shared, rows, half = gated_ref.shape
     gated = [gated_ref[core].reshape(shared * rows, half) for core in range(cores)]
-    for ref, low in ((weight_ref, own_low), (other_ref, 1 - own_low)):
-        for j in range(ref.shape[1]):
+    for refs, low in (((own_ref, x_ref), own_low), ((z_ref, both_ref), 1 - own_low)):
+        for j in range(own_ref.shape[0]):
             total = 0.0
             for core in range(cores):
                 depth = slice(core * half, (core + 1) * half)
-                weight = jnp.concatenate([ref[i, j, :, depth] for i in range(2)], axis=0)
+                weight = jnp.concatenate([ref[j, :, depth] for ref in refs], axis=0)
                 total = total + lax.dot_general(
                     gated[core], weight, (((1,), (1,)), ((), ())), preferred_element_type=F32
                 )
@@ -187,8 +187,6 @@
     own_weight = jnp.broadcast_to(out_weight.T[None], (zh_size, out_cols, width))
     weight = exchange(own_weight, "zh")
     inputs = lax.all_gather(jnp.stack([key_input, value_input, gate_input]), "xl")
-    inputs, weight = lax.optimization_barrier((inputs, weight))
-    far = lax.ppermute(weight, "xh", [(0, 1), (1, 0)])
     inputs = lax.all_gather(inputs, "core")
     base, before, state, amplitude, rate = pl.pallas_call(
         chunk_kernel,
@@ -208,9 +206,14 @@
         compiler_params=PARAMS,
         name="chunk",
     )(where, inputs, decay_rate, residue, skip_gain[None, :])
-    state, weight, far = lax.optimization_barrier((state, weight, far))
-    weight = jnp.stack([weight, far])
-    other = lax.ppermute(weight, "zl", [(0, 1), (1, 0)])
+    state, weight = lax.optimization_barrier((state, weight))
+    swap, cross = [(0, 1), (1, 0)], [(0, 3), (1, 2), (2, 1), (3, 0)]
+    weights = (
+        weight,
+        lax.ppermute(weight, "xh", swap),
+        lax.ppermute(weight, "zl", swap),
+        lax.ppermute(weight, ("zl", "xh"), cross),
+    )
     states = exchange(state, ("zh", "zl", "xh"))
     gated = pl.pallas_call(
         gate_kernel,
@@ -225,11 +228,11 @@
     parts = pl.pallas_call(
         project_kernel,
         out_shape=jax.ShapeDtypeStruct((y_size, blocks) + piece, BF16),
-        in_specs=[SMEM] + [VMEM] * 3,
+        in_specs=[SMEM] + [VMEM] * 5,
         out_specs=VMEM,
         compiler_params=PARAMS,
         name="project",
-    )(where, gated, weight, other)
+    )(where, gated, *weights)
     parts = exchange(parts.reshape((y_size * blocks,) + piece), ("chan", "xl", "core"))
     return pl.pallas_call(
         sum_kernel,

time: 86.8 us -> 85.7 us (0.987)
  starting transfers between devices: 22.4 us -> 30.1 us
  blocking collectives: 44.2 us -> 38.8 us
  waiting for transfers between devices: 9.75 us -> 7.24 us
    all_to_all x2, waiting for transfers between devices: 9.75 us -> 3.04 us  [exchange(): return lax.all_to_all(x, axes, 0, 0, tiled=True)]
    all_to_all x2, starting transfers between devices: 14.5 us -> 20.2 us  [exchange(): return lax.all_to_all(x, axes, 0, 0, tiled=True)]
    ppermute x2 -> x3, waiting for transfers between devices: 0.01 us -> 4.2 us  [the longest x1 3.02 us: body(): lax.ppermute(weight, 'xh', swap)]
    all_gather x1, blocking collectives: 6.39 us -> 3.98 us  [body(): inputs = lax.all_gather(inputs, 'core')]
    all_gather x1, blocking collectives: 6.65 us -> 4.4 us  [body(): gated = lax.all_gather(gated, 'core')]
    ppermute x2 -> x3, starting transfers between devices: 7.87 us -> 9.88 us  [the longest x1 5.67 us: body(): lax.ppermute(weight, ('zl', 'xh'), cross)]
  transfers between devices with their start and end apart: 4 -> 5, of which waited for: 2 -> 3; matrix products, arithmetic and copies ran while one was open for 0% -> 0% of each run, Pallas kernels for 5% -> 5%
where the time goes in v9:
time: 85.7 us; the launch traced here: 85.1 us
  blocking collectives  38.8 us (45%)
  starting transfers between devices  30.1 us (35%)
  waiting for transfers between devices  7.24 us (8%)
  Pallas kernels  6.57 us (8%)
  local copies, waits for them, and re-layouts  2.25 us (3%)
    all_to_all x1, blocking collectives, exchange(): return lax.all_to_all(x, axes, 0, 0, tiled=True)  24.3 us
    all_to_all x2, starting transfers between devices, exchange(): return lax.all_to_all(x, axes, 0, 0, tiled=True)  20.2 us
    all_gather x1, blocking collectives, body(): lax.all_gather(jnp.stack([key_input, value_input, gate_input]), 'xl')  6.13 us
    ppermute x1, starting transfers between devices, body(): lax.ppermute(weight, ('zl', 'xh'), cross)  5.67 us
    all_gather x1, blocking collectives, body(): gated = lax.all_gather(gated, 'core')  4.4 us
    all_gather x1, blocking collectives, body(): inputs = lax.all_gather(inputs, 'core')  3.98 us
    all_to_all x2, waiting for transfers between devices, exchange(): return lax.all_to_all(x, axes, 0, 0, tiled=True)  3.04 us
    ppermute x1, waiting for transfers between devices, body(): lax.ppermute(weight, 'xh', swap)  3.02 us
  transfers between devices with their start and end apart: 5, of which 3 were waited for; matrix products, arithmetic and copies ran while one was open for 0% of the time, Pallas kernels for 5%

profile of v9, /device:TPU:1, one launch (start us, length us, event | category | flops | bytes accessed | tf_op | source)
XLA Modules:
  0.0 85.1 jit_solution(16031258435232400181)
XLA Ops:
  0.0 1.6 %broadcast_in_dim.10 = bf16[4,64,512]{2,1,0:T(8,128)(2,1)} broadcast(bf16[64,512]{1,0:T(8,128)(2,1)} %bitcast.21), dimensions={1,2} | broadcast | bytes 327680 | tf_op jit(solution)/shard_map/broadcast_in_dim | solution.py:187
  1.6 11.0 %all-to-all-start = ((bf16[4,64,512]{2,1,0:T(8,128)(2,1)}), bf16[4,64,512]{2,1,0:T(8,128)(2,1)S(1)}, u32[]{:S(2)}, u32[]{:S(2)}) async-start(bf16[4,64,512]{2,1,0:T(8,128)(2,1)} %broadcast_in_dim.10), calls=%async_computation | async-start | bytes 524288 | tf_op jit(solution)/shard_map/all_to_all | solution.py:166
  12.5 0.0 copy-done.3
  12.5 0.0 copy-done.4
  12.5 0.0 copy-done.5
  12.6 6.1 %all-gather = bf16[6,64,512]{2,1,0:T(8,128)(2,1)S(1)} all-gather(bf16[3,64,512]{2,1,0:T(8,128)(2,1)S(1)} %pad_maximum_fusion), channel_id=2, replica_groups=mesh['zh'=4,'zl'=2,'xh'=2,'xl'=2,'core'=2,'chan'=8] {'xl'}, dimensions={0}, use_global_device_ids=true | all-gather | bytes 589824 | tf_op jit(solution)/shard_map/all_gather | solution.py:189
  18.7 0.1 pad_add_fusion.where_ref
  18.8 4.0 %all-gather.1 = bf16[4,3,64,512]{3,2,1,0:T(8,128)(2,1)S(1)} all-gather(bf16[2,3,64,512]{3,2,1,0:T(8,128)(2,1)S(1)} %bitcast.20), channel_id=3, replica_groups=mesh['zh'=4,'zl'=2,'xh'=2,'xl'=2,'core'=2,'chan'=8] {'core'}, dimensions={0}, use_global_device_ids=true | all-gather | bytes 1179648 | tf_op jit(solution)/shard_map/all_gather | solution.py:190
  22.8 0.7 copy-done.2
  23.5 2.9 %chunk.1 = (f32[4,64,256]{2,1,0:T(8,128)S(1)}, f32[4,16,256]{2,1,0:T(8,128)S(1)}, f32[16,16,256]{2,1,0:T(8,128)}, f32[16,256]{1,0:T(8,128)S(1)}, f32[16,256]{1,0:T(8,128)S(1)}) custom-call(s32[4]{0:T(128)S(1)} %pad_add_fusion.where_ref, bf16[2,2,3,64,512]{4,3,2,1,0:T(8,128)(2,1)S(1)} %bitcast.14, f32[16,512]{1,0:T(8,128)S(1)} %copy-done, ...), custom_call_target="tpu_custom_call" | custom-call | tf_op jit(solution)/shard_map/chunk/pallas_call | solution.py:191
  26.4 0.0 all-to-all-done.own_ref
  26.4 9.2 %all-to-all-start.1 = ((f32[16,16,256]{2,1,0:T(8,128)}), f32[16,16,256]{2,1,0:T(8,128)S(1)}, u32[]{:S(2)}, u32[]{:S(2)}) async-start(f32[16,16,256]{2,1,0:T(8,128)} %get-tuple-element.13), calls=%async_computation.1 | async-start | bytes 524288 | tf_op jit(solution)/shard_map/all_to_all | solution.py:166
  35.6 5.7 %collective-permute-start.2 = (bf16[4,64,512]{2,1,0:T(8,128)(2,1)S(1)}, bf16[4,64,512]{2,1,0:T(8,128)(2,1)S(1)}, u32[]{:S(2)}, u32[]{:S(2)}) collective-permute-start(bf16[4,64,512]{2,1,0:T(8,128)(2,1)S(1)} %all-to-all-done.own_ref), channel_id=1, source_target_pairs={{0,96},{32,64},{64,32},{96,0},{1,97},{33,65},{65,33},{97,1},{2,98}... | collective-permute-start | bytes 786440 | tf_op jit(solution)/shard_map/ppermute | solution.py:215
  41.3 2.2 %collective-permute-start.1 = (bf16[4,64,512]{2,1,0:T(8,128)(2,1)S(1)}, bf16[4,64,512]{2,1,0:T(8,128)(2,1)S(1)}, u32[]{:S(2)}, u32[]{:S(2)}) collective-permute-start(bf16[4,64,512]{2,1,0:T(8,128)(2,1)S(1)} %all-to-all-done.own_ref), channel_id=1, source_target_pairs={{0,64},{64,0},{1,65},{65,1},{2,66},{66,2},{3,67},{67,3},{4,68},{68... | collective-permute-start | bytes 786440 | tf_op jit(solution)/shard_map/ppermute | solution.py:214
  43.5 2.0 %collective-permute-start = (bf16[4,64,512]{2,1,0:T(8,128)(2,1)S(1)}, bf16[4,64,512]{2,1,0:T(8,128)(2,1)S(1)}, u32[]{:S(2)}, u32[]{:S(2)}) collective-permute-start(bf16[4,64,512]{2,1,0:T(8,128)(2,1)S(1)} %all-to-all-done.own_ref), channel_id=1, source_target_pairs={{0,32},{32,0},{1,33},{33,1},{2,34},{34,2},{3,35},{35,3},{4,36},{36... | collective-permute-start | bytes 786440 | tf_op jit(solution)/shard_map/ppermute | solution.py:213
  45.5 3.0 %all-to-all-done.1.chunks_ref = f32[16,16,256]{2,1,0:T(8,128)S(1)} async-done(((f32[16,16,256]{2,1,0:T(8,128)}), f32[16,16,256]{2,1,0:T(8,128)S(1)}, u32[]{:S(2)}, u32[]{:S(2)}) %all-to-all-start.1) | async-done | bytes 262176 | tf_op jit(solution)/shard_map/all_to_all | solution.py:166
  48.6 1.1 %gate.1 = bf16[4,64,256]{2,1,0:T(8,128)(2,1)S(1)} custom-call(s32[4]{0:T(128)S(1)} %pad_add_fusion.where_ref, f32[16,16,256]{2,1,0:T(8,128)S(1)} %all-to-all-done.1.chunks_ref, f32[4,16,256]{2,1,0:T(8,128)S(1)} %get-tuple-element.14.before_ref, f32[16,256]{1,0:T(8,128)S(1)} %get-tuple-element.15.rate_ref, f32[16,256]{1,0:T(8,128)S(1)} %get-tuple-element.16.amp_ref, ...), custom_call_target="tpu_custom_call" | custom-call | tf_op jit(solution)/shard_map/gate/pallas_call | solution.py:218
  49.7 4.4 %all-gather.2 = bf16[8,64,256]{2,1,0:T(8,128)(2,1)S(1)} all-gather(bf16[4,64,256]{2,1,0:T(8,128)(2,1)S(1)} %gate.1), channel_id=4, replica_groups=mesh['zh'=4,'zl'=2,'xh'=2,'xl'=2,'core'=2,'chan'=8] {'core'}, dimensions={0}, use_global_device_ids=true | all-gather | bytes 393216 | tf_op jit(solution)/shard_map/all_gather | solution.py:226
  54.1 0.0 collective-permute-done.2.both_ref
  54.1 1.2 %collective-permute-done.1.z_ref = bf16[4,64,512]{2,1,0:T(8,128)(2,1)S(1)} collective-permute-done((bf16[4,64,512]{2,1,0:T(8,128)(2,1)S(1)}, bf16[4,64,512]{2,1,0:T(8,128)(2,1)S(1)}, u32[]{:S(2)}, u32[]{:S(2)}) %collective-permute-start.1) | collective-permute-done | bytes 262176 | tf_op jit(solution)/shard_map/ppermute | solution.py:214
  55.2 3.0 %collective-permute-done.x_ref = bf16[4,64,512]{2,1,0:T(8,128)(2,1)S(1)} collective-permute-done((bf16[4,64,512]{2,1,0:T(8,128)(2,1)S(1)}, bf16[4,64,512]{2,1,0:T(8,128)(2,1)S(1)}, u32[]{:S(2)}, u32[]{:S(2)}) %collective-permute-start) | collective-permute-done | bytes 262176 | tf_op jit(solution)/shard_map/ppermute | solution.py:213
  58.3 1.2 %project.1 = bf16[8,4,64,128]{3,2,1,0:T(8,128)(2,1)S(1)} custom-call(s32[4]{0:T(128)S(1)} %pad_add_fusion.where_ref, bf16[2,4,64,256]{3,2,1,0:T(8,128)(2,1)S(1)} %bitcast.18, bf16[4,64,512]{2,1,0:T(8,128)(2,1)S(1)} %all-to-all-done.own_ref, bf16[4,64,512]{2,1,0:T(8,128)(2,1)S(1)} %collective-permute-done.x_ref, ...), custom_call_target="tpu_custom_call" | custom-call | tf_op jit(solution)/shard_map/project/pallas_call | solution.py:228
  59.5 24.3 %all_to_all.15 = bf16[32,64,128]{2,1,0:T(8,128)(2,1)S(1)} all-to-all(bf16[32,64,128]{2,1,0:T(8,128)(2,1)S(1)} %bitcast.17), channel_id=1, replica_groups=mesh['zh'=4,'zl'=2,'xh'=2,'xl'=2,'core'=2,'chan'=8] {'chan','xl','core'}, dimensions={0} | all-to-all | bytes 1048576 | tf_op jit(solution)/shard_map/all_to_all | solution.py:166
  83.8 1.3 %sum_parts.1 = bf16[64,512]{1,0:T(8,128)(2,1)} custom-call(s32[4]{0:T(128)S(1)} %pad_add_fusion.where_ref, bf16[8,2,2,64,128]{4,3,2,1,0:T(8,128)(2,1)S(1)} %bitcast.16), custom_call_target="tpu_custom_call" | custom-call | tf_op jit(solution)/shard_map/sum_parts/pallas_call | solution.py:237
  (9 shorter events, 0.0 us)
Async XLA Ops:
  1.6 11.0 %copy-start.3 = (bf16[64,512]{1,0:T(8,128)(2,1)S(1)}, bf16[64,512]{1,0:T(8,128)(2,1)}, u32[]{:S(2)}) copy-start(bf16[64,512]{1,0:T(8,128)(2,1)} %param.7) | copy-start | bytes 196612
  1.6 11.0 %copy-start.4 = (bf16[64,512]{1,0:T(8,128)(2,1)S(1)}, bf16[64,512]{1,0:T(8,128)(2,1)}, u32[]{:S(2)}) copy-start(bf16[64,512]{1,0:T(8,128)(2,1)} %param.9) | copy-start | bytes 196612
  1.6 11.0 %copy-start.5 = (bf16[64,512]{1,0:T(8,128)(2,1)S(1)}, bf16[64,512]{1,0:T(8,128)(2,1)}, u32[]{:S(2)}) copy-start(bf16[64,512]{1,0:T(8,128)(2,1)} %param.8) | copy-start | bytes 196612
  1.6 24.8 %all-to-all-start = ((bf16[4,64,512]{2,1,0:T(8,128)(2,1)}), bf16[4,64,512]{2,1,0:T(8,128)(2,1)S(1)}, u32[]{:S(2)}, u32[]{:S(2)}) async-start(bf16[4,64,512]{2,1,0:T(8,128)(2,1)} %broadcast_in_dim.10), calls=%async_computation | async-start | bytes 524288 | tf_op jit(solution)/shard_map/all_to_all | solution.py:166
  18.8 4.0 %copy-start = (f32[16,512]{1,0:T(8,128)S(1)}, f32[16,512]{1,0:T(8,128)}, u32[]{:S(2)}) copy-start(f32[16,512]{1,0:T(8,128)} %rate_ref.1) | copy-start | bytes 98308
  18.8 4.0 %copy-start.1 = (f32[16,512]{1,0:T(8,128)S(1)}, f32[16,512]{1,0:T(8,128)}, u32[]{:S(2)}) copy-start(f32[16,512]{1,0:T(8,128)} %residue_ref.1) | copy-start | bytes 98308
  22.8 0.7 copy-start.2
  26.4 22.2 %all-to-all-start.1 = ((f32[16,16,256]{2,1,0:T(8,128)}), f32[16,16,256]{2,1,0:T(8,128)S(1)}, u32[]{:S(2)}, u32[]{:S(2)}) async-start(f32[16,16,256]{2,1,0:T(8,128)} %get-tuple-element.13), calls=%async_computation.1 | async-start | bytes 524288 | tf_op jit(solution)/shard_map/all_to_all | solution.py:166
  35.6 18.5 %collective-permute-start.2 = (bf16[4,64,512]{2,1,0:T(8,128)(2,1)S(1)}, bf16[4,64,512]{2,1,0:T(8,128)(2,1)S(1)}, u32[]{:S(2)}, u32[]{:S(2)}) collective-permute-start(bf16[4,64,512]{2,1,0:T(8,128)(2,1)S(1)} %all-to-all-done.own_ref), channel_id=1, source_target_pairs={{0,96},{32,64},{64,32},{96,0},{1,97},{33,65},{65,33},{97,1},{2,98}... | collective-permute-start | bytes 786440 | tf_op jit(solution)/shard_map/ppermute | solution.py:215
  41.3 14.0 %collective-permute-start.1 = (bf16[4,64,512]{2,1,0:T(8,128)(2,1)S(1)}, bf16[4,64,512]{2,1,0:T(8,128)(2,1)S(1)}, u32[]{:S(2)}, u32[]{:S(2)}) collective-permute-start(bf16[4,64,512]{2,1,0:T(8,128)(2,1)S(1)} %all-to-all-done.own_ref), channel_id=1, source_target_pairs={{0,64},{64,0},{1,65},{65,1},{2,66},{66,2},{3,67},{67,3},{4,68},{68... | collective-permute-start | bytes 786440 | tf_op jit(solution)/shard_map/ppermute | solution.py:214
  43.5 14.8 %collective-permute-start = (bf16[4,64,512]{2,1,0:T(8,128)(2,1)S(1)}, bf16[4,64,512]{2,1,0:T(8,128)(2,1)S(1)}, u32[]{:S(2)}, u32[]{:S(2)}) collective-permute-start(bf16[4,64,512]{2,1,0:T(8,128)(2,1)S(1)} %all-to-all-done.own_ref), channel_id=1, source_target_pairs={{0,32},{32,0},{1,33},{33,1},{2,34},{34,2},{3,35},{35,3},{4,36},{36... | collective-permute-start | bytes 786440 | tf_op jit(solution)/shard_map/ppermute | solution.py:213

commit v10 on v9

--- a/solution.py
+++ b/solution.py
@@ -127,25 +127,31 @@
     lax.fori_loop(0, width // LANES, slab, 0)
 
 
-def project_kernel(where_ref, gated_ref, own_ref, x_ref, z_ref, both_ref, out_ref):
-    own_low = where_ref[3]
+def project_kernel(where_ref, gated_ref, own_ref, below_ref, above_ref, out_ref):
+    own_low = where_ref[2]
     cores, shared, rows, half = gated_ref.shape
     gated = [gated_ref[core].reshape(shared * rows, half) for core in range(cores)]
-    for refs, low in (((own_ref, x_ref), own_low), ((z_ref, both_ref), 1 - own_low)):
-        for j in range(own_ref.shape[0]):
-            total = 0.0
-            for core in range(cores):
-                depth = slice(core * half, (core + 1) * half)
-                weight = jnp.concatenate([ref[j, :, depth] for ref in refs], axis=0)
-                total = total + lax.dot_general(
-                    gated[core], weight, (((1,), (1,)), ((), ())), preferred_element_type=F32
-                )
-            out_ref[2 * j + low] = total.astype(BF16).reshape(out_ref.shape[1:])
-
-
-def sum_kernel(where_ref, parts_ref, out_ref):
+    split = below_ref.shape[0]
+
+    def columns(ref, j, place):
+        total = 0.0
+        for core in range(cores):
+            depth = slice(core * half, (core + 1) * half)
+            weight = jnp.concatenate([ref[j, i, :, depth] for i in range(ref.shape[1])], axis=0)
+            total = total + lax.dot_general(
+                gated[core], weight, (((1,), (1,)), ((), ())), preferred_element_type=F32
+            )
+        out_ref[place] = total.astype(BF16).reshape(out_ref.shape[1:])
+
+    for j in range(own_ref.shape[0]):
+        columns(own_ref, j, 2 * j + own_low)
+    for j in range(split):
+        columns(below_ref, j, 2 * j + 1 - own_low)
+        columns(above_ref, j, 2 * (split + j) + 1 - own_low)
+
+
+def sum_kernel(parts_ref, out_ref):
     groups, low, cores, rows, width = parts_ref.shape
-    own_high = where_ref[2]
     unit = width // 2
     for x_low in range(low):
         totals = []
@@ -154,12 +160,11 @@
             for j in range(1, groups):
                 total = total + parts_ref[j, x_low, core].astype(F32)
             totals.append(total)
-        for far in range(2):
-            high = own_high if far == 0 else 1 - own_high
-            place = pl.multiple_of((high * low + x_low) * (cores * unit), cores * unit)
-            pieces = [total[:, far * unit : (far + 1) * unit] for total in totals]
+        for high in range(width // unit):
+            place = (high * low + x_low) * (cores * unit)
+            pieces = [total[:, high * unit : (high + 1) * unit] for total in totals]
             columns = jnp.concatenate(pieces, axis=1)
-            out_ref[:, pl.ds(place, cores * unit)] = columns.astype(BF16)
+            out_ref[:, place : place + cores * unit] = columns.astype(BF16)
 
 
 def exchange(x, axes):
@@ -179,13 +184,15 @@
         [
             lax.axis_index(("zh", "zl", "xh")),
             lax.axis_index("core"),
-            lax.axis_index("xh"),
             lax.axis_index("zl"),
         ]
     ).astype(jnp.int32)
 
-    own_weight = jnp.broadcast_to(out_weight.T[None], (zh_size, out_cols, width))
-    weight = exchange(own_weight, "zh")
+    own_weight = jnp.broadcast_to(
+        out_weight.T[None, None], (zh_size, high_size, out_cols, width)
+    )
+    weight = exchange(own_weight.reshape(-1, out_cols, width), ("zh", "xh"))
+    weight = weight.reshape(own_weight.shape)
     inputs = lax.all_gather(jnp.stack([key_input, value_input, gate_input]), "xl")
     inputs = lax.all_gather(inputs, "core")
     base, before, state, amplitude, rate = pl.pallas_call(
@@ -207,12 +214,14 @@
         name="chunk",
     )(where, inputs, decay_rate, residue, skip_gain[None, :])
     state, weight = lax.optimization_barrier((state, weight))
-    swap, cross = [(0, 1), (1, 0)], [(0, 3), (1, 2), (2, 1), (3, 0)]
+    ring = zh_size * zl_size
+    up = [(i, (i + 1) % ring) for i in range(ring)]
+    down = [(i, (i + ring - 1) % ring) for i in range(ring)]
+    split = zh_size // 2
     weights = (
         weight,
-        lax.ppermute(weight, "xh", swap),
-        lax.ppermute(weight, "zl", swap),
-        lax.ppermute(weight, ("zl", "xh"), cross),
+        lax.ppermute(weight[:split], ("zh", "zl"), up),
+        lax.ppermute(weight[split:], ("zh", "zl"), down),
     )
     states = exchange(state, ("zh", "zl", "xh"))
     gated = pl.pallas_call(
@@ -228,7 +237,7 @@
     parts = pl.pallas_call(
         project_kernel,
         out_shape=jax.ShapeDtypeStruct((y_size, blocks) + piece, BF16),
-        in_specs=[SMEM] + [VMEM] * 5,
+        in_specs=[SMEM] + [VMEM] * 4,
         out_specs=VMEM,
         compiler_params=PARAMS,
         name="project",
@@ -237,11 +246,11 @@
     return pl.pallas_call(
         sum_kernel,
         out_shape=jax.ShapeDtypeStruct((rows, width), BF16),
-        in_specs=[SMEM, VMEM],
+        in_specs=[VMEM],
         out_specs=VMEM,
         compiler_params=PARAMS,
         name="sum_parts",
-    )(where, parts.reshape((y_size, low_size, cores) + piece))
+    )(parts.reshape((y_size, low_size, cores) + piece))
 
 
 def solution(mesh):

time: 85.7 us -> 86.7 us (1.012)
  blocking collectives: 38.8 us -> 41.6 us
  waiting for transfers between devices: 7.24 us -> 6.04 us
    all_gather x1, blocking collectives: 6.13 us -> 10.7 us  [body(): lax.all_gather(jnp.stack([key_input, value_input, gate_input]), 'xl')]
    ppermute x3 -> x2, waiting for transfers between devices: 4.2 us -> 0.01 us  [the longest x1 0.01 us: body(): lax.ppermute(weight[split:], ('zh', 'zl'), down)]
    ppermute x3 -> x2, starting transfers between devices: 9.88 us -> 6.41 us  [the longest x1 4.49 us: body(): lax.ppermute(weight[split:], ('zh', 'zl'), down)]
    all_to_all x2, starting transfers between devices: 20.2 us -> 23.5 us  [exchange(): return lax.all_to_all(x, axes, 0, 0, tiled=True)]
    all_to_all x2, waiting for transfers between devices: 3.04 us -> 6.03 us  [exchange(): return lax.all_to_all(x, axes, 0, 0, tiled=True)]
    reshape x0 -> x1, local copies, waits for them, and re-layouts: none -> 1.68 us  [body(): weight = exchange(own_weight.reshape(-1, out_cols, width), ('zh', 'xh'))]
    broadcast_in_dim x1 -> x0, local copies, waits for them, and re-layouts: 1.55 us -> none  [body(): jnp.broadcast_to(out_weight.T[None], (zh_size, out_cols, width))]
  transfers between devices with their start and end apart: 5 -> 4, of which waited for: 3 -> 1; matrix products, arithmetic and copies ran while one was open for 0% -> 0% of each run, Pallas kernels for 5% -> 5%
where the time goes in v10:
time: 86.7 us; the launch traced here: 86.1 us
  blocking collectives  41.6 us (48%)
  starting transfers between devices  29.9 us (34%)
  Pallas kernels  6.04 us (7%)
  waiting for transfers between devices  6.04 us (7%)
  local copies, waits for them, and re-layouts  2.41 us (3%)
    all_to_all x1, blocking collectives, exchange(): return lax.all_to_all(x, axes, 0, 0, tiled=True)  24.1 us
    all_to_all x2, starting transfers between devices, exchange(): return lax.all_to_all(x, axes, 0, 0, tiled=True)  23.5 us
    all_gather x1, blocking collectives, body(): lax.all_gather(jnp.stack([key_input, value_input, gate_input]), 'xl')  10.7 us
    all_to_all x2, waiting for transfers between devices, exchange(): return lax.all_to_all(x, axes, 0, 0, tiled=True)  6.03 us
    ppermute x1, starting transfers between devices, body(): lax.ppermute(weight[split:], ('zh', 'zl'), down)  4.49 us
    all_gather x1, blocking collectives, body(): gated = lax.all_gather(gated, 'core')  3.68 us
    all_gather x1, blocking collectives, body(): inputs = lax.all_gather(inputs, 'core')  3.13 us
    pallas_call x1, Pallas kernels, body(): pl.pallas_call(chunk_kernel, out_shape=(jax.ShapeDtypeStruct((blocks, row...  2.92 us
  transfers between devices with their start and end apart: 4, of which 1 were waited for; matrix products, arithmetic and copies ran while one was open for 0% of the time, Pallas kernels for 5%

profile of v10, /device:TPU:1, one launch (start us, length us, event | category | flops | bytes accessed | tf_op | source)
XLA Modules:
  0.0 86.1 jit_solution(14293815862094100291)
XLA Ops:
  0.0 1.7 %reshape.13 = bf16[8,64,512]{2,1,0:T(8,128)(2,1)} broadcast(bf16[64,512]{1,0:T(8,128)(2,1)} %bitcast.23), dimensions={1,2} | broadcast | bytes 589824 | tf_op jit(solution)/shard_map/reshape | solution.py:194
  1.7 13.4 %all-to-all-start = ((bf16[8,64,512]{2,1,0:T(8,128)(2,1)}), bf16[8,64,512]{2,1,0:T(8,128)(2,1)S(1)}, u32[]{:S(2)}, u32[]{:S(2)}) async-start(bf16[8,64,512]{2,1,0:T(8,128)(2,1)} %reshape.13), calls=%async_computation | async-start | bytes 1048576 | tf_op jit(solution)/shard_map/all_to_all | solution.py:171
  15.1 0.0 copy-done.3
  15.1 0.0 copy-done.4
  15.1 0.0 copy-done.5
  15.2 10.7 %all-gather = bf16[6,64,512]{2,1,0:T(8,128)(2,1)S(1)} all-gather(bf16[3,64,512]{2,1,0:T(8,128)(2,1)S(1)} %pad_maximum_fusion), channel_id=2, replica_groups=mesh['zh'=4,'zl'=2,'xh'=2,'xl'=2,'core'=2,'chan'=8] {'xl'}, dimensions={0}, use_global_device_ids=true | all-gather | bytes 589824 | tf_op jit(solution)/shard_map/all_gather | solution.py:196
  25.8 0.1 pad_add_fusion.where_ref
  25.9 3.1 %all-gather.1 = bf16[4,3,64,512]{3,2,1,0:T(8,128)(2,1)S(1)} all-gather(bf16[2,3,64,512]{3,2,1,0:T(8,128)(2,1)S(1)} %bitcast.22), channel_id=3, replica_groups=mesh['zh'=4,'zl'=2,'xh'=2,'xl'=2,'core'=2,'chan'=8] {'core'}, dimensions={0}, use_global_device_ids=true | all-gather | bytes 1179648 | tf_op jit(solution)/shard_map/all_gather | solution.py:197
  29.1 0.0 copy-done
  29.1 0.0 copy-done.1
  29.1 0.7 copy-done.2
  29.7 2.9 %chunk.1 = (f32[4,64,256]{2,1,0:T(8,128)S(1)}, f32[4,16,256]{2,1,0:T(8,128)S(1)}, f32[16,16,256]{2,1,0:T(8,128)}, f32[16,256]{1,0:T(8,128)S(1)}, f32[16,256]{1,0:T(8,128)S(1)}) custom-call(s32[3]{0:T(128)S(1)} %pad_add_fusion.where_ref, bf16[2,2,3,64,512]{4,3,2,1,0:T(8,128)(2,1)S(1)} %bitcast.14, f32[16,512]{1,0:T(8,128)S(1)} %copy-done, ...), custom_call_target="tpu_custom_call" | custom-call | tf_op jit(solution)/shard_map/chunk/pallas_call | solution.py:198
  32.7 0.0 all-to-all-done
  32.7 10.0 %all-to-all-start.1 = ((f32[16,16,256]{2,1,0:T(8,128)}), f32[16,16,256]{2,1,0:T(8,128)S(1)}, u32[]{:S(2)}, u32[]{:S(2)}) async-start(f32[16,16,256]{2,1,0:T(8,128)} %get-tuple-element.13), calls=%async_computation.1 | async-start | bytes 524288 | tf_op jit(solution)/shard_map/all_to_all | solution.py:171
  42.7 4.5 %collective-permute-start.1 = (bf16[2,2,64,512]{3,2,1,0:T(8,128)(2,1)S(1)}, bf16[2,2,64,512]{3,2,1,0:T(8,128)(2,1)S(1)}, u32[]{:S(2)}, u32[]{:S(2)}) collective-permute-start(bf16[2,2,64,512]{3,2,1,0:T(8,128)(2,1)S(1)} %get-tuple-element.19), channel_id=1, source_target_pairs={{0,448},{64,0},{128,64},{192,128},{256,192},{320,256},{384,320},{4... | collective-permute-start | bytes 786440 | tf_op jit(solution)/shard_map/ppermute | solution.py:224
  47.2 1.9 %collective-permute-start = (bf16[2,2,64,512]{3,2,1,0:T(8,128)(2,1)S(1)}, bf16[2,2,64,512]{3,2,1,0:T(8,128)(2,1)S(1)}, u32[]{:S(2)}, u32[]{:S(2)}) collective-permute-start(bf16[2,2,64,512]{3,2,1,0:T(8,128)(2,1)S(1)} %get-tuple-element.20), channel_id=1, source_target_pairs={{0,64},{64,128},{128,192},{192,256},{256,320},{320,384},{384,448},... | collective-permute-start | bytes 786440 | tf_op jit(solution)/shard_map/ppermute | solution.py:223
  49.2 6.0 %all-to-all-done.1.chunks_ref = f32[16,16,256]{2,1,0:T(8,128)S(1)} async-done(((f32[16,16,256]{2,1,0:T(8,128)}), f32[16,16,256]{2,1,0:T(8,128)S(1)}, u32[]{:S(2)}, u32[]{:S(2)}) %all-to-all-start.1) | async-done | bytes 262176 | tf_op jit(solution)/shard_map/all_to_all | solution.py:171
  55.2 1.1 %gate.1 = bf16[4,64,256]{2,1,0:T(8,128)(2,1)S(1)} custom-call(s32[3]{0:T(128)S(1)} %pad_add_fusion.where_ref, f32[16,16,256]{2,1,0:T(8,128)S(1)} %all-to-all-done.1.chunks_ref, f32[4,16,256]{2,1,0:T(8,128)S(1)} %get-tuple-element.14.before_ref, f32[16,256]{1,0:T(8,128)S(1)} %get-tuple-element.15.rate_ref, f32[16,256]{1,0:T(8,128)S(1)} %get-tuple-element.16.amp_ref, ...), custom_call_target="tpu_custom_call" | custom-call | tf_op jit(solution)/shard_map/gate/pallas_call | solution.py:227
  56.3 3.7 %all-gather.2 = bf16[8,64,256]{2,1,0:T(8,128)(2,1)S(1)} all-gather(bf16[4,64,256]{2,1,0:T(8,128)(2,1)S(1)} %gate.1), channel_id=4, replica_groups=mesh['zh'=4,'zl'=2,'xh'=2,'xl'=2,'core'=2,'chan'=8] {'core'}, dimensions={0}, use_global_device_ids=true | all-gather | bytes 393216 | tf_op jit(solution)/shard_map/all_gather | solution.py:235
  60.0 0.0 collective-permute-done.1.above_ref
  60.0 0.0 collective-permute-done.below_ref
  60.0 1.2 %project.1 = bf16[8,4,64,128]{3,2,1,0:T(8,128)(2,1)S(1)} custom-call(s32[3]{0:T(128)S(1)} %pad_add_fusion.where_ref, bf16[2,4,64,256]{3,2,1,0:T(8,128)(2,1)S(1)} %bitcast.20, bf16[4,2,64,512]{3,2,1,0:T(8,128)(2,1)S(1)} %bitcast.17, bf16[2,2,64,512]{3,2,1,0:T(8,128)(2,1)S(1)} %collective-permute-done.below_ref, ...), custom_call_target="tpu_custom_call" | custom-call | tf_op jit(solution)/shard_map/project/pallas_call | solution.py:237
  61.2 24.1 %all_to_all.15 = bf16[32,64,128]{2,1,0:T(8,128)(2,1)S(1)} all-to-all(bf16[32,64,128]{2,1,0:T(8,128)(2,1)S(1)} %bitcast.19), channel_id=1, replica_groups=mesh['zh'=4,'zl'=2,'xh'=2,'xl'=2,'core'=2,'chan'=8] {'chan','xl','core'}, dimensions={0} | all-to-all | bytes 1048576 | tf_op jit(solution)/shard_map/all_to_all | solution.py:171
  85.4 0.8 sum_parts.1
  (8 shorter events, 0.1 us)
Async XLA Ops:
  1.7 13.5 %copy-start.3 = (bf16[64,512]{1,0:T(8,128)(2,1)S(1)}, bf16[64,512]{1,0:T(8,128)(2,1)}, u32[]{:S(2)}) copy-start(bf16[64,512]{1,0:T(8,128)(2,1)} %param.7) | copy-start | bytes 196612
  1.7 13.5 %copy-start.4 = (bf16[64,512]{1,0:T(8,128)(2,1)S(1)}, bf16[64,512]{1,0:T(8,128)(2,1)}, u32[]{:S(2)}) copy-start(bf16[64,512]{1,0:T(8,128)(2,1)} %param.9) | copy-start | bytes 196612
  1.7 13.5 %copy-start.5 = (bf16[64,512]{1,0:T(8,128)(2,1)S(1)}, bf16[64,512]{1,0:T(8,128)(2,1)}, u32[]{:S(2)}) copy-start(bf16[64,512]{1,0:T(8,128)(2,1)} %param.8) | copy-start | bytes 196612
  1.7 31.0 %all-to-all-start = ((bf16[8,64,512]{2,1,0:T(8,128)(2,1)}), bf16[8,64,512]{2,1,0:T(8,128)(2,1)S(1)}, u32[]{:S(2)}, u32[]{:S(2)}) async-start(bf16[8,64,512]{2,1,0:T(8,128)(2,1)} %reshape.13), calls=%async_computation | async-start | bytes 1048576 | tf_op jit(solution)/shard_map/all_to_all | solution.py:171
  25.9 3.1 %copy-start = (f32[16,512]{1,0:T(8,128)S(1)}, f32[16,512]{1,0:T(8,128)}, u32[]{:S(2)}) copy-start(f32[16,512]{1,0:T(8,128)} %rate_ref.1) | copy-start | bytes 98308
  25.9 3.1 %copy-start.1 = (f32[16,512]{1,0:T(8,128)S(1)}, f32[16,512]{1,0:T(8,128)}, u32[]{:S(2)}) copy-start(f32[16,512]{1,0:T(8,128)} %residue_ref.1) | copy-start | bytes 98308
  29.0 0.7 copy-start.2
  32.7 22.5 %all-to-all-start.1 = ((f32[16,16,256]{2,1,0:T(8,128)}), f32[16,16,256]{2,1,0:T(8,128)S(1)}, u32[]{:S(2)}, u32[]{:S(2)}) async-start(f32[16,16,256]{2,1,0:T(8,128)} %get-tuple-element.13), calls=%async_computation.1 | async-start | bytes 524288 | tf_op jit(solution)/shard_map/all_to_all | solution.py:171
  42.7 17.2 %collective-permute-start.1 = (bf16[2,2,64,512]{3,2,1,0:T(8,128)(2,1)S(1)}, bf16[2,2,64,512]{3,2,1,0:T(8,128)(2,1)S(1)}, u32[]{:S(2)}, u32[]{:S(2)}) collective-permute-start(bf16[2,2,64,512]{3,2,1,0:T(8,128)(2,1)S(1)} %get-tuple-element.19), channel_id=1, source_target_pairs={{0,448},{64,0},{128,64},{192,128},{256,192},{320,256},{384,320},{4... | collective-permute-start | bytes 786440 | tf_op jit(solution)/shard_map/ppermute | solution.py:224
  47.2 12.7 %collective-permute-start = (bf16[2,2,64,512]{3,2,1,0:T(8,128)(2,1)S(1)}, bf16[2,2,64,512]{3,2,1,0:T(8,128)(2,1)S(1)}, u32[]{:S(2)}, u32[]{:S(2)}) collective-permute-start(bf16[2,2,64,512]{3,2,1,0:T(8,128)(2,1)S(1)} %get-tuple-element.20), channel_id=1, source_target_pairs={{0,64},{64,128},{128,192},{192,256},{256,320},{320,384},{384,448},... | collective-permute-start | bytes 786440 | tf_op jit(solution)/shard_map/ppermute | solution.py:223

commit v11 on v7

--- a/solution.py
+++ b/solution.py
@@ -17,6 +17,17 @@
 
 def tile_rows():
     return lax.broadcasted_iota(jnp.int32, (8, LANES), 0).astype(F32)
+
+
+def copies_kernel(weight_ref, out_ref, sems):
+    copies = [
+        pltpu.make_async_copy(weight_ref, out_ref.at[i], sems.at[i])
+        for i in range(out_ref.shape[0])
+    ]
+    for copy in copies:
+        copy.start()
+    for copy in copies:
+        copy.wait()
 
 
 def chunk_kernel(
@@ -152,12 +163,13 @@
             for j in range(1, groups):
                 total = total + parts_ref[j, x_low, core].astype(F32)
             totals.append(total)
-        for far in range(2):
-            high = own_high if far == 0 else 1 - own_high
-            place = pl.multiple_of((high * low + x_low) * (cores * unit), cores * unit)
-            pieces = [total[:, far * unit : (far + 1) * unit] for total in totals]
-            columns = jnp.concatenate(pieces, axis=1)
-            out_ref[:, pl.ds(place, cores * unit)] = columns.astype(BF16)
+        near = [total[:, :unit] for total in totals]
+        far = [total[:, unit:] for total in totals]
+        near, far = jnp.concatenate(near, axis=1), jnp.concatenate(far, axis=1)
+        for high in range(2):
+            place = (high * low + x_low) * (cores * unit)
+            columns = jnp.where(own_high == high, near, far)
+            out_ref[:, place : place + cores * unit] = columns.astype(BF16)
 
 
 def exchange(x, axes):
@@ -177,7 +189,15 @@
         [lax.axis_index(("z", "xh")), lax.axis_index("core"), lax.axis_index("xh")]
     ).astype(jnp.int32)
 
-    own_weight = jnp.broadcast_to(out_weight.T[None], (z_size, out_cols, width))
+    own_weight = pl.pallas_call(
+        copies_kernel,
+        out_shape=jax.ShapeDtypeStruct((z_size, out_cols, width), BF16),
+        in_specs=[pl.BlockSpec(memory_space=pl.ANY)],
+        out_specs=pl.BlockSpec(memory_space=pl.ANY),
+        scratch_shapes=[pltpu.SemaphoreType.DMA((z_size,))],
+        compiler_params=PARAMS,
+        name="copies",
+    )(out_weight.T)
     near = exchange(own_weight, "z")
     inputs = jnp.stack([key_input, value_input, gate_input])
     inputs = lax.all_gather(lax.all_gather(inputs, "xl"), "core")

time: 82.2 us -> 82.3 us (level)
  Pallas kernels: 5.33 us -> 6.2 us
  local copies, waits for them, and re-layouts: 2.37 us -> 1.54 us
    broadcast_in_dim x1 -> x0, local copies, waits for them, and re-layouts: 1.68 us -> none  [body(): own_weight = jnp.broadcast_to(out_weight.T[None], (z_size, out_cols, width))]
    pallas_call x0 -> x1, Pallas kernels: none -> 0.86 us  [body(): pl.pallas_call(copies_kernel, out_shape=jax.ShapeDtypeStruct((z_size, out...]
    unnamed x12 -> x14, local copies, waits for them, and re-layouts: 0.69 us -> 1.54 us
where the time goes in v11:
time: 82.3 us; the launch traced here: 81.8 us
  blocking collectives  53.4 us (65%)
  starting transfers between devices  15.6 us (19%)
  Pallas kernels  6.2 us (8%)
  waiting for transfers between devices  4.81 us (6%)
  local copies, waits for them, and re-layouts  1.54 us (2%)
    all_to_all x2, blocking collectives, exchange(): return lax.all_to_all(x, axes, 0, 0, tiled=True)  39 us
    all_to_all x1, starting transfers between devices, exchange(): return lax.all_to_all(x, axes, 0, 0, tiled=True)  11 us
    all_gather x2, blocking collectives, body(): inputs = lax.all_gather(lax.all_gather(inputs, 'xl'), 'core')  10.1 us
    all_to_all x1, waiting for transfers between devices, exchange(): return lax.all_to_all(x, axes, 0, 0, tiled=True)  4.81 us
    ppermute x1, starting transfers between devices, body(): far = lax.ppermute(near, 'xh', [(0, 1), (1, 0)])  4.64 us
    all_gather x1, blocking collectives, body(): gated = lax.all_gather(gated, 'core')  4.31 us
    pallas_call x1, Pallas kernels, body(): pl.pallas_call(chunk_kernel, out_shape=(jax.ShapeDtypeStruct((blocks, row...  2.21 us
  transfers between devices with their start and end apart: 2, of which 1 were waited for; matrix products, arithmetic and copies ran while one was open for 0% of the time, Pallas kernels for 4%

profile of v11, /device:TPU:1, one launch (start us, length us, event | category | flops | bytes accessed | tf_op | source)
XLA Modules:
  0.0 81.8 jit_solution(9310280414193256852)
XLA Ops:
  0.0 0.8 %copy-done = bf16[512,64]{0,1:T(8,128)(2,1)S(1)} copy-done((bf16[512,64]{0,1:T(8,128)(2,1)S(1)}, bf16[512,64]{0,1:T(8,128)(2,1)}, u32[]{:S(2)}) %copy-start) | copy-done | bytes 65560
  0.8 0.9 %copies.1 = bf16[8,64,512]{2,1,0:T(8,128)(2,1)} custom-call(bf16[64,512]{1,0:T(8,128)(2,1)S(1)} %bitcast.18), custom_call_target="tpu_custom_call" | custom-call | tf_op jit(solution)/shard_map/copies/pallas_call | solution.py:192
  1.7 0.0 copy-start.4
  1.7 0.0 copy-start.5
  1.7 0.0 copy-start.6
  1.7 11.0 %all-to-all-start = ((bf16[8,64,512]{2,1,0:T(8,128)(2,1)}), bf16[8,64,512]{2,1,0:T(8,128)(2,1)S(1)}, u32[]{:S(2)}, u32[]{:S(2)}) async-start(bf16[8,64,512]{2,1,0:T(8,128)(2,1)} %copies.1), calls=%async_computation | async-start | bytes 1048576 | tf_op jit(solution)/shard_map/all_to_all | solution.py:176
  12.8 0.0 copy-done.4
  12.8 0.0 copy-done.5
  12.8 0.0 copy-done.6
  12.8 6.1 %all-gather = bf16[6,64,512]{2,1,0:T(8,128)(2,1)S(1)} all-gather(bf16[3,64,512]{2,1,0:T(8,128)(2,1)S(1)} %pad_maximum_fusion), channel_id=2, replica_groups=mesh['z'=8,'xh'=2,'xl'=2,'core'=2,'chan'=8] {'xl'}, dimensions={0}, use_global_device_ids=true | all-gather | bytes 589824 | tf_op jit(solution)/shard_map/all_gather | solution.py:203
  18.9 0.1 pad_add_fusion.where_ref
  19.0 4.0 %all-gather.1 = bf16[4,3,64,512]{3,2,1,0:T(8,128)(2,1)S(1)} all-gather(bf16[2,3,64,512]{3,2,1,0:T(8,128)(2,1)S(1)} %bitcast.20), channel_id=3, replica_groups=mesh['z'=8,'xh'=2,'xl'=2,'core'=2,'chan'=8] {'core'}, dimensions={0}, use_global_device_ids=true | all-gather | bytes 1179648 | tf_op jit(solution)/shard_map/all_gather | solution.py:203
  23.0 0.0 copy-done.1
  23.0 0.7 copy-done.3
  23.7 2.2 %chunk.1 = (f32[4,64,256]{2,1,0:T(8,128)S(1)}, f32[4,16,256]{2,1,0:T(8,128)S(1)}, f32[16,16,256]{2,1,0:T(8,128)S(1)}, f32[16,256]{1,0:T(8,128)S(1)}, f32[16,256]{1,0:T(8,128)S(1)}) custom-call(s32[3]{0:T(128)S(1)} %pad_add_fusion.where_ref, bf16[2,2,3,64,512]{4,3,2,1,0:T(8,128)(2,1)S(1)} %bitcast.13, f32[16,512]{1,0:T(8,128)S(1)} %copy-done.1, ...), custom_call_target="tpu_custom_call" | custom-call | tf_op jit(solution)/shard_map/chunk/pallas_call | solution.py:204
  25.9 4.8 %all-to-all-done.near_ref = bf16[8,64,512]{2,1,0:T(8,128)(2,1)S(1)} async-done(((bf16[8,64,512]{2,1,0:T(8,128)(2,1)}), bf16[8,64,512]{2,1,0:T(8,128)(2,1)S(1)}, u32[]{:S(2)}, u32[]{:S(2)}) %all-to-all-start) | async-done | bytes 524320 | tf_op jit(solution)/shard_map/all_to_all | solution.py:176
  30.7 4.6 %collective-permute-start = (bf16[8,64,512]{2,1,0:T(8,128)(2,1)S(1)}, bf16[8,64,512]{2,1,0:T(8,128)(2,1)S(1)}, u32[]{:S(2)}, u32[]{:S(2)}) collective-permute-start(bf16[8,64,512]{2,1,0:T(8,128)(2,1)S(1)} %all-to-all-done.near_ref), channel_id=1, source_target_pairs={{0,32},{32,0},{1,33},{33,1},{2,34},{34,2},{3,35},{35,3},{4,36},{36... | collective-permute-start | bytes 1572872 | tf_op jit(solution)/shard_map/ppermute | solution.py:223
  35.4 14.9 %all_to_all.15.chunks_ref = f32[16,16,256]{2,1,0:T(8,128)S(1)} all-to-all(f32[16,16,256]{2,1,0:T(8,128)S(1)} %get-tuple-element.15), channel_id=1, replica_groups=mesh['z'=8,'xh'=2,'xl'=2,'core'=2,'chan'=8] {'z','xh'}, dimensions={0} | all-to-all | bytes 524288 | tf_op jit(solution)/shard_map/all_to_all | solution.py:176
  50.2 1.1 %gate.1 = bf16[4,64,256]{2,1,0:T(8,128)(2,1)S(1)} custom-call(s32[3]{0:T(128)S(1)} %pad_add_fusion.where_ref, f32[16,16,256]{2,1,0:T(8,128)S(1)} %all_to_all.15.chunks_ref, f32[4,16,256]{2,1,0:T(8,128)S(1)} %get-tuple-element.16.before_ref, f32[16,256]{1,0:T(8,128)S(1)} %get-tuple-element.17.rate_ref, f32[16,256]{1,0:T(8,128)S(1)} %get-tuple-element.18.amp_ref, ...), custom_call_target="tpu_custom_call" | custom-call | tf_op jit(solution)/shard_map/gate/pallas_call | solution.py:225
  51.3 0.0 collective-permute-done.far_ref
  51.3 4.3 %all-gather.2 = bf16[8,64,256]{2,1,0:T(8,128)(2,1)S(1)} all-gather(bf16[4,64,256]{2,1,0:T(8,128)(2,1)S(1)} %gate.1), channel_id=4, replica_groups=mesh['z'=8,'xh'=2,'xl'=2,'core'=2,'chan'=8] {'core'}, dimensions={0}, use_global_device_ids=true | all-gather | bytes 393216 | tf_op jit(solution)/shard_map/all_gather | solution.py:234
  55.6 0.7 project.1
  56.4 24.1 %all_to_all.16 = bf16[32,64,128]{2,1,0:T(8,128)(2,1)S(1)} all-to-all(bf16[32,64,128]{2,1,0:T(8,128)(2,1)S(1)} %bitcast.15), channel_id=1, replica_groups=mesh['z'=8,'xh'=2,'xl'=2,'core'=2,'chan'=8] {'chan','xl','core'}, dimensions={0} | all-to-all | bytes 1048576 | tf_op jit(solution)/shard_map/all_to_all | solution.py:176
  80.5 1.3 %sum_parts.1 = bf16[64,512]{1,0:T(8,128)(2,1)} custom-call(s32[3]{0:T(128)S(1)} %pad_add_fusion.where_ref, bf16[8,2,2,64,128]{4,3,2,1,0:T(8,128)(2,1)S(1)} %bitcast.16), custom_call_target="tpu_custom_call" | custom-call | tf_op jit(solution)/shard_map/sum_parts/pallas_call | solution.py:245
  (6 shorter events, 0.0 us)
Async XLA Ops:
  0.0 0.8 %copy-start = (bf16[512,64]{0,1:T(8,128)(2,1)S(1)}, bf16[512,64]{0,1:T(8,128)(2,1)}, u32[]{:S(2)}) copy-start(bf16[512,64]{0,1:T(8,128)(2,1)} %param.13) | copy-start | bytes 196612
  1.7 11.0 %copy-start.4 = (bf16[64,512]{1,0:T(8,128)(2,1)S(1)}, bf16[64,512]{1,0:T(8,128)(2,1)}, u32[]{:S(2)}) copy-start(bf16[64,512]{1,0:T(8,128)(2,1)} %param.7) | copy-start | bytes 196612
  1.7 11.0 %copy-start.5 = (bf16[64,512]{1,0:T(8,128)(2,1)S(1)}, bf16[64,512]{1,0:T(8,128)(2,1)}, u32[]{:S(2)}) copy-start(bf16[64,512]{1,0:T(8,128)(2,1)} %param.9) | copy-start | bytes 196612
  1.7 11.0 %copy-start.6 = (bf16[64,512]{1,0:T(8,128)(2,1)S(1)}, bf16[64,512]{1,0:T(8,128)(2,1)}, u32[]{:S(2)}) copy-start(bf16[64,512]{1,0:T(8,128)(2,1)} %param.8) | copy-start | bytes 196612
  1.7 29.0 %all-to-all-start = ((bf16[8,64,512]{2,1,0:T(8,128)(2,1)}), bf16[8,64,512]{2,1,0:T(8,128)(2,1)S(1)}, u32[]{:S(2)}, u32[]{:S(2)}) async-start(bf16[8,64,512]{2,1,0:T(8,128)(2,1)} %copies.1), calls=%async_computation | async-start | bytes 1048576 | tf_op jit(solution)/shard_map/all_to_all | solution.py:176
  19.0 4.0 %copy-start.1 = (f32[16,512]{1,0:T(8,128)S(1)}, f32[16,512]{1,0:T(8,128)}, u32[]{:S(2)}) copy-start(f32[16,512]{1,0:T(8,128)} %rate_ref.1) | copy-start | bytes 98308
  19.0 4.0 %copy-start.2 = (f32[16,512]{1,0:T(8,128)S(1)}, f32[16,512]{1,0:T(8,128)}, u32[]{:S(2)}) copy-start(f32[16,512]{1,0:T(8,128)} %residue_ref.1) | copy-start | bytes 98308
  23.0 0.7 copy-start.3
  30.7 20.6 %collective-permute-start = (bf16[8,64,512]{2,1,0:T(8,128)(2,1)S(1)}, bf16[8,64,512]{2,1,0:T(8,128)(2,1)S(1)}, u32[]{:S(2)}, u32[]{:S(2)}) collective-permute-start(bf16[8,64,512]{2,1,0:T(8,128)(2,1)S(1)} %all-to-all-done.near_ref), channel_id=1, source_target_pairs={{0,32},{32,0},{1,33},{33,1},{2,34},{34,2},{3,35},{35,3},{4,36},{36... | collective-permute-start | bytes 1572872 | tf_op jit(solution)/shard_map/ppermute | solution.py:223

commit v12 on v7

--- a/solution.py
+++ b/solution.py
@@ -11,7 +11,6 @@
 SEQ = ("z", "xh", "xl", "core")
 LANES = 128
 VMEM = pl.BlockSpec(memory_space=pltpu.VMEM)
-SMEM = pl.BlockSpec(memory_space=pltpu.SMEM)
 PARAMS = pltpu.CompilerParams(vmem_limit_bytes=48 * 1024 * 1024)
 
 
@@ -20,14 +19,14 @@
 
 
 def chunk_kernel(
-    where_ref, inputs_ref, rate_ref, residue_ref, skip_ref,
+    inputs_ref, rate_ref, residue_ref, skip_ref,
     base_ref, before_ref, send_ref, amp_ref, copy_ref, signal_ref, state_ref,
 ):
     blocks, rows, width = base_ref.shape
     modes = rate_ref.shape[0]
     tiles = rows // 8
     cores = inputs_ref.shape[0]
-    first_col = where_ref[1] * width
+    first_col = lax.axis_index("core") * width
 
     def slab(index, carry):
         cols = pl.ds(pl.multiple_of(index * LANES, LANES), LANES)
@@ -85,14 +84,14 @@
 
 
 def gate_kernel(
-    where_ref, chunks_ref, before_ref, rate_ref, amp_ref, base_ref, inputs_ref, gated_ref
+    chunks_ref, before_ref, rate_ref, amp_ref, base_ref, inputs_ref, gated_ref
 ):
     blocks, rows, width = base_ref.shape
     modes = rate_ref.shape[0]
     tiles = rows // 8
     cores = inputs_ref.shape[0]
-    own = where_ref[0]
-    first_col = where_ref[1] * width
+    own = lax.axis_index("z") * lax.axis_size("xh") + lax.axis_index("xh")
+    first_col = lax.axis_index("core") * width
 
     def slab(index, carry):
         cols = pl.ds(pl.multiple_of(index * LANES, LANES), LANES)
@@ -141,9 +140,9 @@
         out_ref[j] = total.astype(BF16).reshape(out_ref.shape[1:])
 
 
-def sum_kernel(where_ref, parts_ref, out_ref):
+def sum_kernel(parts_ref, out_ref):
     groups, low, cores, rows, width = parts_ref.shape
-    own_high = where_ref[2]
+    own_high = lax.axis_index("xh")
     unit = width // 2
     for x_low in range(low):
         totals = []
@@ -152,12 +151,13 @@
             for j in range(1, groups):
                 total = total + parts_ref[j, x_low, core].astype(F32)
             totals.append(total)
-        for far in range(2):
-            high = own_high if far == 0 else 1 - own_high
-            place = pl.multiple_of((high * low + x_low) * (cores * unit), cores * unit)
-            pieces = [total[:, far * unit : (far + 1) * unit] for total in totals]
-            columns = jnp.concatenate(pieces, axis=1)
-            out_ref[:, pl.ds(place, cores * unit)] = columns.astype(BF16)
+        near = [total[:, :unit] for total in totals]
+        far = [total[:, unit:] for total in totals]
+        near, far = jnp.concatenate(near, axis=1), jnp.concatenate(far, axis=1)
+        for high in range(2):
+            place = (high * low + x_low) * (cores * unit)
+            columns = jnp.where(own_high == high, near, far)
+            out_ref[:, place : place + cores * unit] = columns.astype(BF16)
 
 
 def exchange(x, axes):
@@ -173,10 +173,6 @@
     chunks = z_size * high_size
     blocks = low_size * cores
     half = width // cores
-    where = jnp.stack(
-        [lax.axis_index(("z", "xh")), lax.axis_index("core"), lax.axis_index("xh")]
-    ).astype(jnp.int32)
-
     own_weight = jnp.broadcast_to(out_weight.T[None], (z_size, out_cols, width))
     near = exchange(own_weight, "z")
     inputs = jnp.stack([key_input, value_input, gate_input])
@@ -190,7 +186,7 @@
             jax.ShapeDtypeStruct((modes, half), F32),
             jax.ShapeDtypeStruct((modes, half), F32),
         ),
-        in_specs=[SMEM] + [VMEM] * 4,
+        in_specs=[VMEM] * 4,
         out_specs=(VMEM,) * 5,
         scratch_shapes=[
             pltpu.VMEM((blocks, rows, LANES), F32),
@@ -198,18 +194,18 @@
         ],
         compiler_params=PARAMS,
         name="chunk",
-    )(where, inputs, decay_rate, residue, skip_gain[None, :])
+    )(inputs, decay_rate, residue, skip_gain[None, :])
     state, near = lax.optimization_barrier((state, near))
     far = lax.ppermute(near, "xh", [(0, 1), (1, 0)])
     states = exchange(state, ("z", "xh"))
     gated = pl.pallas_call(
         gate_kernel,
         out_shape=jax.ShapeDtypeStruct((blocks, rows, half), BF16),
-        in_specs=[SMEM] + [VMEM] * 6,
+        in_specs=[VMEM] * 6,
         out_specs=VMEM,
         compiler_params=PARAMS,
         name="gate",
-    )(where, states, before, rate, amplitude, base, inputs)
+    )(states, before, rate, amplitude, base, inputs)
     gated, far = lax.optimization_barrier((gated, far))
     gated = lax.all_gather(gated, "core")
     piece = (rows, high_size * out_cols)
@@ -225,11 +221,11 @@
     return pl.pallas_call(
         sum_kernel,
         out_shape=jax.ShapeDtypeStruct((rows, width), BF16),
-        in_specs=[SMEM, VMEM],
+        in_specs=[VMEM],
         out_specs=VMEM,
         compiler_params=PARAMS,
         name="sum_parts",
-    )(where, parts.reshape((y_size, low_size, cores) + piece))
+    )(parts.reshape((y_size, low_size, cores) + piece))
 
 
 def solution(mesh):

time: 82.2 us -> 81.1 us (0.987)
  Pallas kernels: 5.33 us -> 3.7 us
  transfers between devices with their start and end apart: 2 -> 2, of which waited for: 1 -> 1; matrix products, arithmetic and copies ran while one was open for 0% -> 0% of each run, Pallas kernels for 4% -> 3%
where the time goes in v12:
time: 81.1 us; the launch traced here: 80.7 us
  blocking collectives  53.4 us (66%)
  starting transfers between devices  15.6 us (19%)
  waiting for transfers between devices  5.43 us (7%)
  Pallas kernels  3.7 us (5%)
  local copies, waits for them, and re-layouts  2.37 us (3%)
    all_to_all x2, blocking collectives, exchange(): return lax.all_to_all(x, axes, 0, 0, tiled=True)  39 us
    all_to_all x1, starting transfers between devices, exchange(): return lax.all_to_all(x, axes, 0, 0, tiled=True)  11 us
    all_gather x2, blocking collectives, body(): inputs = lax.all_gather(lax.all_gather(inputs, 'xl'), 'core')  10.1 us
    all_to_all x1, waiting for transfers between devices, exchange(): return lax.all_to_all(x, axes, 0, 0, tiled=True)  5.43 us
    ppermute x1, starting transfers between devices, body(): far = lax.ppermute(near, 'xh', [(0, 1), (1, 0)])  4.64 us
    all_gather x1, blocking collectives, body(): gated = lax.all_gather(gated, 'core')  4.31 us
    broadcast_in_dim x1, local copies, waits for them, and re-layouts, body(): own_weight = jnp.broadcast_to(out_weight.T[None], (z_size, out_cols, width))  1.68 us
    pallas_call x1, Pallas kernels, body(): pl.pallas_call(chunk_kernel, out_shape=(jax.ShapeDtypeStruct((blocks, row...  1.67 us
  transfers between devices with their start and end apart: 2, of which 1 were waited for; matrix products, arithmetic and copies ran while one was open for 0% of the time, Pallas kernels for 3%

profile of v12, /device:TPU:1, one launch (start us, length us, event | category | flops | bytes accessed | tf_op | source)
XLA Modules:
  0.0 80.7 jit_solution(121498522128996779)
XLA Ops:
  0.0 1.7 %broadcast_in_dim.10 = bf16[8,64,512]{2,1,0:T(8,128)(2,1)} broadcast(bf16[64,512]{1,0:T(8,128)(2,1)} %bitcast.17), dimensions={1,2} | broadcast | bytes 589824 | tf_op jit(solution)/shard_map/broadcast_in_dim | solution.py:176
  1.7 0.0 copy-start.3
  1.7 0.0 copy-start.4
  1.7 0.0 copy-start.5
  1.7 11.0 %all-to-all-start = ((bf16[8,64,512]{2,1,0:T(8,128)(2,1)}), bf16[8,64,512]{2,1,0:T(8,128)(2,1)S(1)}, u32[]{:S(2)}, u32[]{:S(2)}) async-start(bf16[8,64,512]{2,1,0:T(8,128)(2,1)} %broadcast_in_dim.10), calls=%async_computation | async-start | bytes 1048576 | tf_op jit(solution)/shard_map/all_to_all | solution.py:164
  12.7 0.0 copy-done.3
  12.7 0.0 copy-done.4
  12.7 0.0 copy-done.5
  12.7 6.1 %all-gather = bf16[6,64,512]{2,1,0:T(8,128)(2,1)S(1)} all-gather(bf16[3,64,512]{2,1,0:T(8,128)(2,1)S(1)} %pad_maximum_fusion), channel_id=2, replica_groups=mesh['z'=8,'xh'=2,'xl'=2,'core'=2,'chan'=8] {'xl'}, dimensions={0}, use_global_device_ids=true | all-gather | bytes 589824 | tf_op jit(solution)/shard_map/all_gather | solution.py:179
  18.9 0.0 copy-start
  18.9 4.0 %all-gather.1 = bf16[4,3,64,512]{3,2,1,0:T(8,128)(2,1)S(1)} all-gather(bf16[2,3,64,512]{3,2,1,0:T(8,128)(2,1)S(1)} %bitcast.16), channel_id=3, replica_groups=mesh['z'=8,'xh'=2,'xl'=2,'core'=2,'chan'=8] {'core'}, dimensions={0}, use_global_device_ids=true | all-gather | bytes 1179648 | tf_op jit(solution)/shard_map/all_gather | solution.py:179
  22.9 0.0 copy-done
  22.9 0.0 copy-done.1
  22.9 0.7 copy-done.2
  23.5 1.7 %chunk.1 = (f32[4,64,256]{2,1,0:T(8,128)S(1)}, f32[4,16,256]{2,1,0:T(8,128)S(1)}, f32[16,16,256]{2,1,0:T(8,128)S(1)}, f32[16,256]{1,0:T(8,128)S(1)}, f32[16,256]{1,0:T(8,128)S(1)}) custom-call(bf16[2,2,3,64,512]{4,3,2,1,0:T(8,128)(2,1)S(1)} %bitcast.10, f32[16,512]{1,0:T(8,128)S(1)} %copy-done, f32[16,512]{1,0:T(8,128)S(1)} %copy-done.1, f32[1,512]{1,0:T(1,128)S(1)} %bitcast.15), custom_call_target="tpu_custom_call" | custom-call | tf_op jit(solution)/shard_map/chunk/pallas_call | solution.py:180
  25.2 5.4 %all-to-all-done.near_ref = bf16[8,64,512]{2,1,0:T(8,128)(2,1)S(1)} async-done(((bf16[8,64,512]{2,1,0:T(8,128)(2,1)}), bf16[8,64,512]{2,1,0:T(8,128)(2,1)S(1)}, u32[]{:S(2)}, u32[]{:S(2)}) %all-to-all-start) | async-done | bytes 524320 | tf_op jit(solution)/shard_map/all_to_all | solution.py:164
  30.6 4.6 %collective-permute-start = (bf16[8,64,512]{2,1,0:T(8,128)(2,1)S(1)}, bf16[8,64,512]{2,1,0:T(8,128)(2,1)S(1)}, u32[]{:S(2)}, u32[]{:S(2)}) collective-permute-start(bf16[8,64,512]{2,1,0:T(8,128)(2,1)S(1)} %all-to-all-done.near_ref), channel_id=1, source_target_pairs={{0,32},{32,0},{1,33},{33,1},{2,34},{34,2},{3,35},{35,3},{4,36},{36... | collective-permute-start | bytes 1572872 | tf_op jit(solution)/shard_map/ppermute | solution.py:199
  35.3 14.9 %all_to_all.15.chunks_ref = f32[16,16,256]{2,1,0:T(8,128)S(1)} all-to-all(f32[16,16,256]{2,1,0:T(8,128)S(1)} %get-tuple-element.15), channel_id=1, replica_groups=mesh['z'=8,'xh'=2,'xl'=2,'core'=2,'chan'=8] {'z','xh'}, dimensions={0} | all-to-all | bytes 524288 | tf_op jit(solution)/shard_map/all_to_all | solution.py:164
  50.1 0.6 gate.1
  50.7 0.0 collective-permute-done.far_ref
  50.7 4.3 %all-gather.2 = bf16[8,64,256]{2,1,0:T(8,128)(2,1)S(1)} all-gather(bf16[4,64,256]{2,1,0:T(8,128)(2,1)S(1)} %gate.1), channel_id=4, replica_groups=mesh['z'=8,'xh'=2,'xl'=2,'core'=2,'chan'=8] {'core'}, dimensions={0}, use_global_device_ids=true | all-gather | bytes 393216 | tf_op jit(solution)/shard_map/all_gather | solution.py:210
  55.0 0.7 project.1
  55.7 24.2 %all_to_all.16 = bf16[32,64,128]{2,1,0:T(8,128)(2,1)S(1)} all-to-all(bf16[32,64,128]{2,1,0:T(8,128)(2,1)S(1)} %bitcast.12), channel_id=1, replica_groups=mesh['z'=8,'xh'=2,'xl'=2,'core'=2,'chan'=8] {'chan','xl','core'}, dimensions={0} | all-to-all | bytes 1048576 | tf_op jit(solution)/shard_map/all_to_all | solution.py:164
  79.9 0.8 sum_parts.1
  (3 shorter events, 0.0 us)
Async XLA Ops:
  1.7 11.0 %copy-start.3 = (bf16[64,512]{1,0:T(8,128)(2,1)S(1)}, bf16[64,512]{1,0:T(8,128)(2,1)}, u32[]{:S(2)}) copy-start(bf16[64,512]{1,0:T(8,128)(2,1)} %param.7) | copy-start | bytes 196612
  1.7 11.0 %copy-start.4 = (bf16[64,512]{1,0:T(8,128)(2,1)S(1)}, bf16[64,512]{1,0:T(8,128)(2,1)}, u32[]{:S(2)}) copy-start(bf16[64,512]{1,0:T(8,128)(2,1)} %param.9) | copy-start | bytes 196612
  1.7 11.0 %copy-start.5 = (bf16[64,512]{1,0:T(8,128)(2,1)S(1)}, bf16[64,512]{1,0:T(8,128)(2,1)}, u32[]{:S(2)}) copy-start(bf16[64,512]{1,0:T(8,128)(2,1)} %param.8) | copy-start | bytes 196612
  1.7 29.0 %all-to-all-start = ((bf16[8,64,512]{2,1,0:T(8,128)(2,1)}), bf16[8,64,512]{2,1,0:T(8,128)(2,1)S(1)}, u32[]{:S(2)}, u32[]{:S(2)}) async-start(bf16[8,64,512]{2,1,0:T(8,128)(2,1)} %broadcast_in_dim.10), calls=%async_computation | async-start | bytes 1048576 | tf_op jit(solution)/shard_map/all_to_all | solution.py:164
  18.9 4.0 %copy-start = (f32[16,512]{1,0:T(8,128)S(1)}, f32[16,512]{1,0:T(8,128)}, u32[]{:S(2)}) copy-start(f32[16,512]{1,0:T(8,128)} %rate_ref.1) | copy-start | bytes 98308
  18.9 4.0 %copy-start.1 = (f32[16,512]{1,0:T(8,128)S(1)}, f32[16,512]{1,0:T(8,128)}, u32[]{:S(2)}) copy-start(f32[16,512]{1,0:T(8,128)} %residue_ref.1) | copy-start | bytes 98308
  22.9 0.7 copy-start.2
  30.6 20.1 %collective-permute-start = (bf16[8,64,512]{2,1,0:T(8,128)(2,1)S(1)}, bf16[8,64,512]{2,1,0:T(8,128)(2,1)S(1)}, u32[]{:S(2)}, u32[]{:S(2)}) collective-permute-start(bf16[8,64,512]{2,1,0:T(8,128)(2,1)S(1)} %all-to-all-done.near_ref), channel_id=1, source_target_pairs={{0,32},{32,0},{1,33},{33,1},{2,34},{34,2},{3,35},{35,3},{4,36},{36... | collective-permute-start | bytes 1572872 | tf_op jit(solution)/shard_map/ppermute | solution.py:199

commit v13 on v12

--- a/solution.py
+++ b/solution.py
@@ -58,8 +58,7 @@
         for i in range(blocks):
             before_ref[i, :, cols] = running
             running = decay * running + state_ref[i]
-        for copy in range(send_ref.shape[0]):
-            send_ref[copy, :, cols] = running
+        send_ref[:, cols] = running
         row_ids = lax.broadcasted_iota(jnp.int32, (rows, LANES), 0)
         skip = skip_ref[0:1, source]
 
@@ -83,27 +82,43 @@
     lax.fori_loop(0, width // LANES, slab, 0)
 
 
+def total_kernel(length, states_ref, rate_ref, total_ref):
+    decay = jnp.exp(-float(length) * rate_ref[...])
+    total = states_ref[0]
+    for i in range(1, states_ref.shape[0]):
+        total = decay * total + states_ref[i]
+    for copy in range(total_ref.shape[0]):
+        total_ref[copy] = total
+
+
 def gate_kernel(
-    chunks_ref, before_ref, rate_ref, amp_ref, base_ref, inputs_ref, gated_ref
+    totals_ref, states_ref, before_ref, rate_ref, amp_ref, base_ref, inputs_ref, gated_ref
 ):
     blocks, rows, width = base_ref.shape
     modes = rate_ref.shape[0]
     tiles = rows // 8
     cores = inputs_ref.shape[0]
-    own = lax.axis_index("z") * lax.axis_size("xh") + lax.axis_index("xh")
+    own_z = lax.axis_index("z")
+    own_high = lax.axis_index("xh")
     first_col = lax.axis_index("core") * width
+    highs = states_ref.shape[0]
 
     def slab(index, carry):
         cols = pl.ds(pl.multiple_of(index * LANES, LANES), LANES)
         source = pl.ds(pl.multiple_of(first_col + index * LANES, LANES), LANES)
         rate = rate_ref[:, cols]
         amp = amp_ref[:, cols]
-        decay = jnp.exp(-float(rows * blocks) * rate)
+        decay = jnp.exp(-float(rows * blocks * highs) * rate)
         running = jnp.zeros((modes, LANES), F32)
         entering = jnp.zeros((modes, LANES), F32)
-        for chunk in range(chunks_ref.shape[0]):
-            entering = jnp.where(own == chunk, running, entering)
-            running = decay * running + chunks_ref[chunk, :, cols]
+        for z in range(totals_ref.shape[0]):
+            entering = jnp.where(own_z == z, running, entering)
+            running = decay * running + totals_ref[z, :, cols]
+        decay = jnp.exp(-float(rows * blocks) * rate)
+        running = entering
+        for high in range(1, highs):
+            running = decay * running + states_ref[high - 1, :, cols]
+            entering = jnp.where(own_high == high, running, entering)
         steps = [jnp.exp(-8.0 * j * rate) for j in range(tiles)]
         first = tile_rows() + 1.0
         aheads = [jnp.exp(-rate[m : m + 1] * first) for m in range(modes)]
@@ -170,7 +185,6 @@
     z_size, high_size, low_size, cores = (lax.axis_size(a) for a in SEQ)
     y_size = lax.axis_size("chan")
     out_cols = out_weight.shape[1]
-    chunks = z_size * high_size
     blocks = low_size * cores
     half = width // cores
     own_weight = jnp.broadcast_to(out_weight.T[None], (z_size, out_cols, width))
@@ -182,7 +196,7 @@
         out_shape=(
             jax.ShapeDtypeStruct((blocks, rows, half), F32),
             jax.ShapeDtypeStruct((blocks, modes, half), F32),
-            jax.ShapeDtypeStruct((chunks, modes, half), F32),
+            jax.ShapeDtypeStruct((modes, half), F32),
             jax.ShapeDtypeStruct((modes, half), F32),
             jax.ShapeDtypeStruct((modes, half), F32),
         ),
@@ -195,17 +209,26 @@
         compiler_params=PARAMS,
         name="chunk",
     )(inputs, decay_rate, residue, skip_gain[None, :])
-    state, near = lax.optimization_barrier((state, near))
+    states = lax.all_gather(state, "xh")
+    total = pl.pallas_call(
+        lambda *refs: total_kernel(rows * blocks, *refs),
+        out_shape=jax.ShapeDtypeStruct((z_size, modes, half), F32),
+        in_specs=[VMEM] * 2,
+        out_specs=VMEM,
+        compiler_params=PARAMS,
+        name="total",
+    )(states, rate)
+    total, near = lax.optimization_barrier((total, near))
     far = lax.ppermute(near, "xh", [(0, 1), (1, 0)])
-    states = exchange(state, ("z", "xh"))
+    totals = exchange(total, "z")
     gated = pl.pallas_call(
         gate_kernel,
         out_shape=jax.ShapeDtypeStruct((blocks, rows, half), BF16),
-        in_specs=[VMEM] * 6,
+        in_specs=[VMEM] * 7,
         out_specs=VMEM,
         compiler_params=PARAMS,
         name="gate",
-    )(states, before, rate, amplitude, base, inputs)
+    )(totals, states, before, rate, amplitude, base, inputs)
     gated, far = lax.optimization_barrier((gated, far))
     gated = lax.all_gather(gated, "core")
     piece = (rows, high_size * out_cols)

time: 81.1 us -> 80.6 us (level)
  waiting for transfers between devices: 5.43 us -> 0.36 us
  blocking collectives: 53.4 us -> 57.9 us
    all_to_all x1, waiting for transfers between devices: 5.43 us -> 0.35 us  [exchange(): return lax.all_to_all(x, axes, 0, 0, tiled=True)]
    all_gather x0 -> x1, blocking collectives: none -> 5.07 us  [body(): states = lax.all_gather(state, 'xh')]
    all_to_all x2, blocking collectives: 39 us -> 38 us  [exchange(): return lax.all_to_all(x, axes, 0, 0, tiled=True)]
where the time goes in v13:
time: 80.6 us; the launch traced here: 80.1 us
  blocking collectives  57.9 us (72%)
  starting transfers between devices  15.6 us (19%)
  Pallas kernels  3.68 us (5%)
  local copies, waits for them, and re-layouts  2.37 us (3%)
    all_to_all x2, blocking collectives, exchange(): return lax.all_to_all(x, axes, 0, 0, tiled=True)  38 us
    all_to_all x1, starting transfers between devices, exchange(): return lax.all_to_all(x, axes, 0, 0, tiled=True)  11 us
    all_gather x2, blocking collectives, body(): inputs = lax.all_gather(lax.all_gather(inputs, 'xl'), 'core')  10.1 us
    all_gather x1, blocking collectives, body(): states = lax.all_gather(state, 'xh')  5.07 us
    all_gather x1, blocking collectives, body(): gated = lax.all_gather(gated, 'core')  4.77 us
    ppermute x1, starting transfers between devices, body(): far = lax.ppermute(near, 'xh', [(0, 1), (1, 0)])  4.64 us
    broadcast_in_dim x1, local copies, waits for them, and re-layouts, body(): own_weight = jnp.broadcast_to(out_weight.T[None], (z_size, out_cols, width))  1.68 us
    pallas_call x1, Pallas kernels, body(): pl.pallas_call(chunk_kernel, out_shape=(jax.ShapeDtypeStruct((blocks, row...  1.65 us
  transfers between devices with their start and end apart: 2, of which 1 were waited for; matrix products, arithmetic and copies ran while one was open for 0% of the time, Pallas kernels for 3%

profile of v13, /device:TPU:1, one launch (start us, length us, event | category | flops | bytes accessed | tf_op | source)
XLA Modules:
  0.0 80.1 jit_solution(15679114503532179967)
XLA Ops:
  0.0 1.7 %broadcast_in_dim.10 = bf16[8,64,512]{2,1,0:T(8,128)(2,1)} broadcast(bf16[64,512]{1,0:T(8,128)(2,1)} %bitcast.20), dimensions={1,2} | broadcast | bytes 589824 | tf_op jit(solution)/shard_map/broadcast_in_dim | solution.py:190
  1.7 0.0 copy-start.3
  1.7 0.0 copy-start.4
  1.7 0.0 copy-start.5
  1.7 11.0 %all-to-all-start = ((bf16[8,64,512]{2,1,0:T(8,128)(2,1)}), bf16[8,64,512]{2,1,0:T(8,128)(2,1)S(1)}, u32[]{:S(2)}, u32[]{:S(2)}) async-start(bf16[8,64,512]{2,1,0:T(8,128)(2,1)} %broadcast_in_dim.10), calls=%async_computation | async-start | bytes 1048576 | tf_op jit(solution)/shard_map/all_to_all | solution.py:179
  12.7 0.0 copy-done.3
  12.7 0.0 copy-done.4
  12.7 0.0 copy-done.5
  12.7 6.1 %all-gather = bf16[6,64,512]{2,1,0:T(8,128)(2,1)S(1)} all-gather(bf16[3,64,512]{2,1,0:T(8,128)(2,1)S(1)} %pad_maximum_fusion), channel_id=2, replica_groups=mesh['z'=8,'xh'=2,'xl'=2,'core'=2,'chan'=8] {'xl'}, dimensions={0}, use_global_device_ids=true | all-gather | bytes 589824 | tf_op jit(solution)/shard_map/all_gather | solution.py:193
  18.9 4.0 %all-gather.1 = bf16[4,3,64,512]{3,2,1,0:T(8,128)(2,1)S(1)} all-gather(bf16[2,3,64,512]{3,2,1,0:T(8,128)(2,1)S(1)} %bitcast.19), channel_id=3, replica_groups=mesh['z'=8,'xh'=2,'xl'=2,'core'=2,'chan'=8] {'core'}, dimensions={0}, use_global_device_ids=true | all-gather | bytes 1179648 | tf_op jit(solution)/shard_map/all_gather | solution.py:193
  22.9 0.0 copy-done
  22.9 0.0 copy-done.1
  22.9 0.7 copy-done.2
  23.5 1.7 %chunk.1 = (f32[4,64,256]{2,1,0:T(8,128)S(1)}, f32[4,16,256]{2,1,0:T(8,128)S(1)}, f32[16,256]{1,0:T(8,128)S(1)}, f32[16,256]{1,0:T(8,128)S(1)}, f32[16,256]{1,0:T(8,128)S(1)}) custom-call(bf16[2,2,3,64,512]{4,3,2,1,0:T(8,128)(2,1)S(1)} %bitcast.11, f32[16,512]{1,0:T(8,128)S(1)} %copy-done, f32[16,512]{1,0:T(8,128)S(1)} %copy-done.1, f32[1,512]{1,0:T(1,128)S(1)} %bitcast.18), custom_call_target="tpu_custom_call" | custom-call | tf_op jit(solution)/shard_map/chunk/pallas_call | solution.py:194
  25.2 5.1 %all-gather.2 = f32[32,256]{1,0:T(8,128)S(1)} all-gather(f32[16,256]{1,0:T(8,128)S(1)} %get-tuple-element.14), channel_id=4, replica_groups=mesh['z'=8,'xh'=2,'xl'=2,'core'=2,'chan'=8] {'xh'}, dimensions={0}, use_global_device_ids=true | all-gather | bytes 49152 | tf_op jit(solution)/shard_map/all_gather | solution.py:212
  30.3 0.4 all-to-all-done.near_ref
  30.6 4.6 %collective-permute-start = (bf16[8,64,512]{2,1,0:T(8,128)(2,1)S(1)}, bf16[8,64,512]{2,1,0:T(8,128)(2,1)S(1)}, u32[]{:S(2)}, u32[]{:S(2)}) collective-permute-start(bf16[8,64,512]{2,1,0:T(8,128)(2,1)S(1)} %all-to-all-done.near_ref), channel_id=1, source_target_pairs={{0,32},{32,0},{1,33},{33,1},{2,34},{34,2},{3,35},{35,3},{4,36},{36... | collective-permute-start | bytes 1572872 | tf_op jit(solution)/shard_map/ppermute | solution.py:222
  35.3 13.8 %all_to_all.15.totals_ref = f32[8,16,256]{2,1,0:T(8,128)S(1)} all-to-all(f32[8,16,256]{2,1,0:T(8,128)S(1)} %total.1), channel_id=1, replica_groups=mesh['z'=8,'xh'=2,'xl'=2,'core'=2,'chan'=8] {'z'}, dimensions={0} | all-to-all | bytes 262144 | tf_op jit(solution)/shard_map/all_to_all | solution.py:179
  49.1 0.5 gate.1
  49.7 0.0 collective-permute-done.far_ref
  49.7 4.8 %all-gather.3 = bf16[8,64,256]{2,1,0:T(8,128)(2,1)S(1)} all-gather(bf16[4,64,256]{2,1,0:T(8,128)(2,1)S(1)} %gate.1), channel_id=5, replica_groups=mesh['z'=8,'xh'=2,'xl'=2,'core'=2,'chan'=8] {'core'}, dimensions={0}, use_global_device_ids=true | all-gather | bytes 393216 | tf_op jit(solution)/shard_map/all_gather | solution.py:233
  54.4 0.7 project.1
  55.2 24.2 %all_to_all.16 = bf16[32,64,128]{2,1,0:T(8,128)(2,1)S(1)} all-to-all(bf16[32,64,128]{2,1,0:T(8,128)(2,1)S(1)} %bitcast.13), channel_id=1, replica_groups=mesh['z'=8,'xh'=2,'xl'=2,'core'=2,'chan'=8] {'chan','xl','core'}, dimensions={0} | all-to-all | bytes 1048576 | tf_op jit(solution)/shard_map/all_to_all | solution.py:179
  79.3 0.8 sum_parts.1
  (5 shorter events, 0.0 us)
Async XLA Ops:
  1.7 11.0 %copy-start.3 = (bf16[64,512]{1,0:T(8,128)(2,1)S(1)}, bf16[64,512]{1,0:T(8,128)(2,1)}, u32[]{:S(2)}) copy-start(bf16[64,512]{1,0:T(8,128)(2,1)} %param.7) | copy-start | bytes 196612
  1.7 11.0 %copy-start.4 = (bf16[64,512]{1,0:T(8,128)(2,1)S(1)}, bf16[64,512]{1,0:T(8,128)(2,1)}, u32[]{:S(2)}) copy-start(bf16[64,512]{1,0:T(8,128)(2,1)} %param.9) | copy-start | bytes 196612
  1.7 11.0 %copy-start.5 = (bf16[64,512]{1,0:T(8,128)(2,1)S(1)}, bf16[64,512]{1,0:T(8,128)(2,1)}, u32[]{:S(2)}) copy-start(bf16[64,512]{1,0:T(8,128)(2,1)} %param.8) | copy-start | bytes 196612
  1.7 29.0 %all-to-all-start = ((bf16[8,64,512]{2,1,0:T(8,128)(2,1)}), bf16[8,64,512]{2,1,0:T(8,128)(2,1)S(1)}, u32[]{:S(2)}, u32[]{:S(2)}) async-start(bf16[8,64,512]{2,1,0:T(8,128)(2,1)} %broadcast_in_dim.10), calls=%async_computation | async-start | bytes 1048576 | tf_op jit(solution)/shard_map/all_to_all | solution.py:179
  18.9 4.0 %copy-start = (f32[16,512]{1,0:T(8,128)S(1)}, f32[16,512]{1,0:T(8,128)}, u32[]{:S(2)}) copy-start(f32[16,512]{1,0:T(8,128)} %rate_ref.1) | copy-start | bytes 98308
  18.9 4.0 %copy-start.1 = (f32[16,512]{1,0:T(8,128)S(1)}, f32[16,512]{1,0:T(8,128)}, u32[]{:S(2)}) copy-start(f32[16,512]{1,0:T(8,128)} %residue_ref.1) | copy-start | bytes 98308
  22.9 0.7 copy-start.2
  30.6 19.0 %collective-permute-start = (bf16[8,64,512]{2,1,0:T(8,128)(2,1)S(1)}, bf16[8,64,512]{2,1,0:T(8,128)(2,1)S(1)}, u32[]{:S(2)}, u32[]{:S(2)}) collective-permute-start(bf16[8,64,512]{2,1,0:T(8,128)(2,1)S(1)} %all-to-all-done.near_ref), channel_id=1, source_target_pairs={{0,32},{32,0},{1,33},{33,1},{2,34},{34,2},{3,35},{35,3},{4,36},{36... | collective-permute-start | bytes 1572872 | tf_op jit(solution)/shard_map/ppermute | solution.py:222

commit v14 on v13

--- a/solution.py
+++ b/solution.py
@@ -229,7 +229,6 @@
         compiler_params=PARAMS,
         name="gate",
     )(totals, states, before, rate, amplitude, base, inputs)
-    gated, far = lax.optimization_barrier((gated, far))
     gated = lax.all_gather(gated, "core")
     piece = (rows, high_size * out_cols)
     parts = pl.pallas_call(

time: 80.6 us -> 80.6 us (level)
  no operation moved by 1% of the time
where the time goes in v14:
time: 80.6 us; the launch traced here: 80.1 us
  blocking collectives  57.9 us (72%)
  starting transfers between devices  15.6 us (19%)
  Pallas kernels  3.68 us (5%)
  local copies, waits for them, and re-layouts  2.37 us (3%)
    all_to_all x2, blocking collectives, exchange(): return lax.all_to_all(x, axes, 0, 0, tiled=True)  38 us
    all_to_all x1, starting transfers between devices, exchange(): return lax.all_to_all(x, axes, 0, 0, tiled=True)  11 us
    all_gather x2, blocking collectives, body(): inputs = lax.all_gather(lax.all_gather(inputs, 'xl'), 'core')  10.1 us
    all_gather x1, blocking collectives, body(): states = lax.all_gather(state, 'xh')  5.07 us
    all_gather x1, blocking collectives, body(): gated = lax.all_gather(gated, 'core')  4.77 us
    ppermute x1, starting transfers between devices, body(): far = lax.ppermute(near, 'xh', [(0, 1), (1, 0)])  4.64 us
    broadcast_in_dim x1, local copies, waits for them, and re-layouts, body(): own_weight = jnp.broadcast_to(out_weight.T[None], (z_size, out_cols, width))  1.68 us
    pallas_call x1, Pallas kernels, body(): pl.pallas_call(chunk_kernel, out_shape=(jax.ShapeDtypeStruct((blocks, row...  1.65 us
  transfers between devices with their start and end apart: 2, of which 1 were waited for; matrix products, arithmetic and copies ran while one was open for 0% of the time, Pallas kernels for 3%

profile of v14, /device:TPU:1, one launch (start us, length us, event | category | flops | bytes accessed | tf_op | source)
XLA Modules:
  0.0 80.1 jit_solution(17799354856321998415)
XLA Ops:
  0.0 1.7 %broadcast_in_dim.10 = bf16[8,64,512]{2,1,0:T(8,128)(2,1)} broadcast(bf16[64,512]{1,0:T(8,128)(2,1)} %bitcast.20), dimensions={1,2} | broadcast | bytes 589824 | tf_op jit(solution)/shard_map/broadcast_in_dim | solution.py:190
  1.7 0.0 copy-start.3
  1.7 0.0 copy-start.4
  1.7 0.0 copy-start.5
  1.7 11.0 %all-to-all-start = ((bf16[8,64,512]{2,1,0:T(8,128)(2,1)}), bf16[8,64,512]{2,1,0:T(8,128)(2,1)S(1)}, u32[]{:S(2)}, u32[]{:S(2)}) async-start(bf16[8,64,512]{2,1,0:T(8,128)(2,1)} %broadcast_in_dim.10), calls=%async_computation | async-start | bytes 1048576 | tf_op jit(solution)/shard_map/all_to_all | solution.py:179
  12.7 0.0 copy-done.3
  12.7 0.0 copy-done.4
  12.7 0.0 copy-done.5
  12.7 6.1 %all-gather = bf16[6,64,512]{2,1,0:T(8,128)(2,1)S(1)} all-gather(bf16[3,64,512]{2,1,0:T(8,128)(2,1)S(1)} %pad_maximum_fusion), channel_id=2, replica_groups=mesh['z'=8,'xh'=2,'xl'=2,'core'=2,'chan'=8] {'xl'}, dimensions={0}, use_global_device_ids=true | all-gather | bytes 589824 | tf_op jit(solution)/shard_map/all_gather | solution.py:193
  18.9 4.0 %all-gather.1 = bf16[4,3,64,512]{3,2,1,0:T(8,128)(2,1)S(1)} all-gather(bf16[2,3,64,512]{3,2,1,0:T(8,128)(2,1)S(1)} %bitcast.19), channel_id=3, replica_groups=mesh['z'=8,'xh'=2,'xl'=2,'core'=2,'chan'=8] {'core'}, dimensions={0}, use_global_device_ids=true | all-gather | bytes 1179648 | tf_op jit(solution)/shard_map/all_gather | solution.py:193
  22.9 0.0 copy-done
  22.9 0.0 copy-done.1
  22.9 0.7 copy-done.2
  23.5 1.7 %chunk.1 = (f32[4,64,256]{2,1,0:T(8,128)S(1)}, f32[4,16,256]{2,1,0:T(8,128)S(1)}, f32[16,256]{1,0:T(8,128)S(1)}, f32[16,256]{1,0:T(8,128)S(1)}, f32[16,256]{1,0:T(8,128)S(1)}) custom-call(bf16[2,2,3,64,512]{4,3,2,1,0:T(8,128)(2,1)S(1)} %bitcast.11, f32[16,512]{1,0:T(8,128)S(1)} %copy-done, f32[16,512]{1,0:T(8,128)S(1)} %copy-done.1, f32[1,512]{1,0:T(1,128)S(1)} %bitcast.18), custom_call_target="tpu_custom_call" | custom-call | tf_op jit(solution)/shard_map/chunk/pallas_call | solution.py:194
  25.2 5.1 %all-gather.2 = f32[32,256]{1,0:T(8,128)S(1)} all-gather(f32[16,256]{1,0:T(8,128)S(1)} %get-tuple-element.12), channel_id=4, replica_groups=mesh['z'=8,'xh'=2,'xl'=2,'core'=2,'chan'=8] {'xh'}, dimensions={0}, use_global_device_ids=true | all-gather | bytes 49152 | tf_op jit(solution)/shard_map/all_gather | solution.py:212
  30.3 0.4 all-to-all-done.near_ref
  30.6 4.6 %collective-permute-start = (bf16[8,64,512]{2,1,0:T(8,128)(2,1)S(1)}, bf16[8,64,512]{2,1,0:T(8,128)(2,1)S(1)}, u32[]{:S(2)}, u32[]{:S(2)}) collective-permute-start(bf16[8,64,512]{2,1,0:T(8,128)(2,1)S(1)} %all-to-all-done.near_ref), channel_id=1, source_target_pairs={{0,32},{32,0},{1,33},{33,1},{2,34},{34,2},{3,35},{35,3},{4,36},{36... | collective-permute-start | bytes 1572872 | tf_op jit(solution)/shard_map/ppermute | solution.py:222
  35.3 13.8 %all_to_all.15.totals_ref = f32[8,16,256]{2,1,0:T(8,128)S(1)} all-to-all(f32[8,16,256]{2,1,0:T(8,128)S(1)} %total.1), channel_id=1, replica_groups=mesh['z'=8,'xh'=2,'xl'=2,'core'=2,'chan'=8] {'z'}, dimensions={0} | all-to-all | bytes 262144 | tf_op jit(solution)/shard_map/all_to_all | solution.py:179
  49.1 0.5 gate.1
  49.7 4.8 %all-gather.3 = bf16[8,64,256]{2,1,0:T(8,128)(2,1)S(1)} all-gather(bf16[4,64,256]{2,1,0:T(8,128)(2,1)S(1)} %gate.1), channel_id=5, replica_groups=mesh['z'=8,'xh'=2,'xl'=2,'core'=2,'chan'=8] {'core'}, dimensions={0}, use_global_device_ids=true | all-gather | bytes 393216 | tf_op jit(solution)/shard_map/all_gather | solution.py:232
  54.4 0.0 collective-permute-done.far_ref
  54.4 0.7 project.1
  55.1 24.2 %all_to_all.16 = bf16[32,64,128]{2,1,0:T(8,128)(2,1)S(1)} all-to-all(bf16[32,64,128]{2,1,0:T(8,128)(2,1)S(1)} %bitcast.13), channel_id=1, replica_groups=mesh['z'=8,'xh'=2,'xl'=2,'core'=2,'chan'=8] {'chan','xl','core'}, dimensions={0} | all-to-all | bytes 1048576 | tf_op jit(solution)/shard_map/all_to_all | solution.py:179
  79.3 0.8 sum_parts.1
  (5 shorter events, 0.0 us)
Async XLA Ops:
  1.7 11.0 %copy-start.3 = (bf16[64,512]{1,0:T(8,128)(2,1)S(1)}, bf16[64,512]{1,0:T(8,128)(2,1)}, u32[]{:S(2)}) copy-start(bf16[64,512]{1,0:T(8,128)(2,1)} %param.7) | copy-start | bytes 196612
  1.7 11.0 %copy-start.4 = (bf16[64,512]{1,0:T(8,128)(2,1)S(1)}, bf16[64,512]{1,0:T(8,128)(2,1)}, u32[]{:S(2)}) copy-start(bf16[64,512]{1,0:T(8,128)(2,1)} %param.9) | copy-start | bytes 196612
  1.7 11.0 %copy-start.5 = (bf16[64,512]{1,0:T(8,128)(2,1)S(1)}, bf16[64,512]{1,0:T(8,128)(2,1)}, u32[]{:S(2)}) copy-start(bf16[64,512]{1,0:T(8,128)(2,1)} %param.8) | copy-start | bytes 196612
  1.7 29.0 %all-to-all-start = ((bf16[8,64,512]{2,1,0:T(8,128)(2,1)}), bf16[8,64,512]{2,1,0:T(8,128)(2,1)S(1)}, u32[]{:S(2)}, u32[]{:S(2)}) async-start(bf16[8,64,512]{2,1,0:T(8,128)(2,1)} %broadcast_in_dim.10), calls=%async_computation | async-start | bytes 1048576 | tf_op jit(solution)/shard_map/all_to_all | solution.py:179
  18.9 4.0 %copy-start = (f32[16,512]{1,0:T(8,128)S(1)}, f32[16,512]{1,0:T(8,128)}, u32[]{:S(2)}) copy-start(f32[16,512]{1,0:T(8,128)} %rate_ref.1) | copy-start | bytes 98308
  18.9 4.0 %copy-start.1 = (f32[16,512]{1,0:T(8,128)S(1)}, f32[16,512]{1,0:T(8,128)}, u32[]{:S(2)}) copy-start(f32[16,512]{1,0:T(8,128)} %residue_ref.1) | copy-start | bytes 98308
  22.9 0.7 copy-start.2
  30.6 23.8 %collective-permute-start = (bf16[8,64,512]{2,1,0:T(8,128)(2,1)S(1)}, bf16[8,64,512]{2,1,0:T(8,128)(2,1)S(1)}, u32[]{:S(2)}, u32[]{:S(2)}) collective-permute-start(bf16[8,64,512]{2,1,0:T(8,128)(2,1)S(1)} %all-to-all-done.near_ref), channel_id=1, source_target_pairs={{0,32},{32,0},{1,33},{33,1},{2,34},{34,2},{3,35},{35,3},{4,36},{36... | collective-permute-start | bytes 1572872 | tf_op jit(solution)/shard_map/ppermute | solution.py:222

commit v15 on v14

--- a/solution.py
+++ b/solution.py
@@ -144,7 +144,7 @@
 def project_kernel(gated_ref, near_ref, far_ref, out_ref):
     cores, shared, rows, half = gated_ref.shape
     gated = [gated_ref[core].reshape(shared * rows, half) for core in range(cores)]
-    for j in range(out_ref.shape[0]):
+    for j in range(out_ref.shape[1]):
         total = 0.0
         for core in range(cores):
             depth = slice(core * half, (core + 1) * half)
@@ -152,19 +152,19 @@
             total = total + lax.dot_general(
                 gated[core], weight, (((1,), (1,)), ((), ())), preferred_element_type=F32
             )
-        out_ref[j] = total.astype(BF16).reshape(out_ref.shape[1:])
+        out_ref[:, j] = total.astype(BF16).reshape(shared, rows, -1)
 
 
 def sum_kernel(parts_ref, out_ref):
-    groups, low, cores, rows, width = parts_ref.shape
+    low, cores, groups, rows, width = parts_ref.shape
     own_high = lax.axis_index("xh")
     unit = width // 2
     for x_low in range(low):
         totals = []
         for core in range(cores):
-            total = parts_ref[0, x_low, core].astype(F32)
+            total = parts_ref[x_low, core, 0].astype(F32)
             for j in range(1, groups):
-                total = total + parts_ref[j, x_low, core].astype(F32)
+                total = total + parts_ref[x_low, core, j].astype(F32)
             totals.append(total)
         near = [total[:, :unit] for total in totals]
         far = [total[:, unit:] for total in totals]
@@ -233,13 +233,13 @@
     piece = (rows, high_size * out_cols)
     parts = pl.pallas_call(
         project_kernel,
-        out_shape=jax.ShapeDtypeStruct((y_size, blocks) + piece, BF16),
+        out_shape=jax.ShapeDtypeStruct((blocks, y_size) + piece, BF16),
         in_specs=[VMEM] * 3,
         out_specs=VMEM,
         compiler_params=PARAMS,
         name="project",
     )(gated, near, far)
-    parts = exchange(parts.reshape((y_size * blocks,) + piece), ("chan", "xl", "core"))
+    parts = exchange(parts.reshape((y_size * blocks,) + piece), ("xl", "core", "chan"))
     return pl.pallas_call(
         sum_kernel,
         out_shape=jax.ShapeDtypeStruct((rows, width), BF16),
@@ -247,7 +247,7 @@
         out_specs=VMEM,
         compiler_params=PARAMS,
         name="sum_parts",
-    )(parts.reshape((y_size, low_size, cores) + piece))
+    )(parts.reshape((low_size, cores, y_size) + piece))
 
 
 def solution(mesh):

time: 80.6 us -> 80 us (level)
  no operation moved by 1% of the time
where the time goes in v15:
time: 80 us; the launch traced here: 79.4 us
  blocking collectives  57.2 us (72%)
  starting transfers between devices  15.6 us (20%)
  Pallas kernels  3.68 us (5%)
  local copies, waits for them, and re-layouts  2.37 us (3%)
    all_to_all x2, blocking collectives, exchange(): return lax.all_to_all(x, axes, 0, 0, tiled=True)  37.3 us
    all_to_all x1, starting transfers between devices, exchange(): return lax.all_to_all(x, axes, 0, 0, tiled=True)  11 us
    all_gather x2, blocking collectives, body(): inputs = lax.all_gather(lax.all_gather(inputs, 'xl'), 'core')  10.1 us
    all_gather x1, blocking collectives, body(): states = lax.all_gather(state, 'xh')  5.07 us
    all_gather x1, blocking collectives, body(): gated = lax.all_gather(gated, 'core')  4.77 us
    ppermute x1, starting transfers between devices, body(): far = lax.ppermute(near, 'xh', [(0, 1), (1, 0)])  4.64 us
    broadcast_in_dim x1, local copies, waits for them, and re-layouts, body(): own_weight = jnp.broadcast_to(out_weight.T[None], (z_size, out_cols, width))  1.68 us
    pallas_call x1, Pallas kernels, body(): pl.pallas_call(chunk_kernel, out_shape=(jax.ShapeDtypeStruct((blocks, row...  1.65 us
  transfers between devices with their start and end apart: 2, of which 1 were waited for; matrix products, arithmetic and copies ran while one was open for 0% of the time, Pallas kernels for 3%

profile of v15, /device:TPU:1, one launch (start us, length us, event | category | flops | bytes accessed | tf_op | source)
XLA Modules:
  0.0 79.4 jit_solution(16371259372229864141)
XLA Ops:
  0.0 1.7 %broadcast_in_dim.10 = bf16[8,64,512]{2,1,0:T(8,128)(2,1)} broadcast(bf16[64,512]{1,0:T(8,128)(2,1)} %bitcast.20), dimensions={1,2} | broadcast | bytes 589824 | tf_op jit(solution)/shard_map/broadcast_in_dim | solution.py:190
  1.7 0.0 copy-start.3
  1.7 0.0 copy-start.4
  1.7 0.0 copy-start.5
  1.7 11.0 %all-to-all-start = ((bf16[8,64,512]{2,1,0:T(8,128)(2,1)}), bf16[8,64,512]{2,1,0:T(8,128)(2,1)S(1)}, u32[]{:S(2)}, u32[]{:S(2)}) async-start(bf16[8,64,512]{2,1,0:T(8,128)(2,1)} %broadcast_in_dim.10), calls=%async_computation | async-start | bytes 1048576 | tf_op jit(solution)/shard_map/all_to_all | solution.py:179
  12.7 0.0 copy-done.3
  12.7 0.0 copy-done.4
  12.7 0.0 copy-done.5
  12.7 6.1 %all-gather = bf16[6,64,512]{2,1,0:T(8,128)(2,1)S(1)} all-gather(bf16[3,64,512]{2,1,0:T(8,128)(2,1)S(1)} %pad_maximum_fusion), channel_id=2, replica_groups=mesh['z'=8,'xh'=2,'xl'=2,'core'=2,'chan'=8] {'xl'}, dimensions={0}, use_global_device_ids=true | all-gather | bytes 589824 | tf_op jit(solution)/shard_map/all_gather | solution.py:193
  18.9 4.0 %all-gather.1 = bf16[4,3,64,512]{3,2,1,0:T(8,128)(2,1)S(1)} all-gather(bf16[2,3,64,512]{3,2,1,0:T(8,128)(2,1)S(1)} %bitcast.19), channel_id=3, replica_groups=mesh['z'=8,'xh'=2,'xl'=2,'core'=2,'chan'=8] {'core'}, dimensions={0}, use_global_device_ids=true | all-gather | bytes 1179648 | tf_op jit(solution)/shard_map/all_gather | solution.py:193
  22.9 0.0 copy-done
  22.9 0.0 copy-done.1
  22.9 0.7 copy-done.2
  23.5 1.7 %chunk.1 = (f32[4,64,256]{2,1,0:T(8,128)S(1)}, f32[4,16,256]{2,1,0:T(8,128)S(1)}, f32[16,256]{1,0:T(8,128)S(1)}, f32[16,256]{1,0:T(8,128)S(1)}, f32[16,256]{1,0:T(8,128)S(1)}) custom-call(bf16[2,2,3,64,512]{4,3,2,1,0:T(8,128)(2,1)S(1)} %bitcast.11, f32[16,512]{1,0:T(8,128)S(1)} %copy-done, f32[16,512]{1,0:T(8,128)S(1)} %copy-done.1, f32[1,512]{1,0:T(1,128)S(1)} %bitcast.18), custom_call_target="tpu_custom_call" | custom-call | tf_op jit(solution)/shard_map/chunk/pallas_call | solution.py:194
  25.2 5.1 %all-gather.2 = f32[32,256]{1,0:T(8,128)S(1)} all-gather(f32[16,256]{1,0:T(8,128)S(1)} %get-tuple-element.12), channel_id=4, replica_groups=mesh['z'=8,'xh'=2,'xl'=2,'core'=2,'chan'=8] {'xh'}, dimensions={0}, use_global_device_ids=true | all-gather | bytes 49152 | tf_op jit(solution)/shard_map/all_gather | solution.py:212
  30.3 0.4 all-to-all-done.near_ref
  30.6 4.6 %collective-permute-start = (bf16[8,64,512]{2,1,0:T(8,128)(2,1)S(1)}, bf16[8,64,512]{2,1,0:T(8,128)(2,1)S(1)}, u32[]{:S(2)}, u32[]{:S(2)}) collective-permute-start(bf16[8,64,512]{2,1,0:T(8,128)(2,1)S(1)} %all-to-all-done.near_ref), channel_id=1, source_target_pairs={{0,32},{32,0},{1,33},{33,1},{2,34},{34,2},{3,35},{35,3},{4,36},{36... | collective-permute-start | bytes 1572872 | tf_op jit(solution)/shard_map/ppermute | solution.py:222
  35.3 13.8 %all_to_all.15.totals_ref = f32[8,16,256]{2,1,0:T(8,128)S(1)} all-to-all(f32[8,16,256]{2,1,0:T(8,128)S(1)} %total.1), channel_id=1, replica_groups=mesh['z'=8,'xh'=2,'xl'=2,'core'=2,'chan'=8] {'z'}, dimensions={0} | all-to-all | bytes 262144 | tf_op jit(solution)/shard_map/all_to_all | solution.py:179
  49.1 0.5 gate.1
  49.7 4.8 %all-gather.3 = bf16[8,64,256]{2,1,0:T(8,128)(2,1)S(1)} all-gather(bf16[4,64,256]{2,1,0:T(8,128)(2,1)S(1)} %gate.1), channel_id=5, replica_groups=mesh['z'=8,'xh'=2,'xl'=2,'core'=2,'chan'=8] {'core'}, dimensions={0}, use_global_device_ids=true | all-gather | bytes 393216 | tf_op jit(solution)/shard_map/all_gather | solution.py:232
  54.4 0.0 collective-permute-done.far_ref
  54.4 0.7 project.1
  55.1 23.4 %all_to_all.16 = bf16[32,64,128]{2,1,0:T(8,128)(2,1)S(1)} all-to-all(bf16[32,64,128]{2,1,0:T(8,128)(2,1)S(1)} %bitcast.13), channel_id=1, replica_groups=mesh['z'=8,'xh'=2,'xl'=2,'core'=2,'chan'=8] {'xl','core','chan'}, dimensions={0} | all-to-all | bytes 1048576 | tf_op jit(solution)/shard_map/all_to_all | solution.py:179
  78.6 0.8 sum_parts.1
  (5 shorter events, 0.0 us)
Async XLA Ops:
  1.7 11.0 %copy-start.3 = (bf16[64,512]{1,0:T(8,128)(2,1)S(1)}, bf16[64,512]{1,0:T(8,128)(2,1)}, u32[]{:S(2)}) copy-start(bf16[64,512]{1,0:T(8,128)(2,1)} %param.7) | copy-start | bytes 196612
  1.7 11.0 %copy-start.4 = (bf16[64,512]{1,0:T(8,128)(2,1)S(1)}, bf16[64,512]{1,0:T(8,128)(2,1)}, u32[]{:S(2)}) copy-start(bf16[64,512]{1,0:T(8,128)(2,1)} %param.9) | copy-start | bytes 196612
  1.7 11.0 %copy-start.5 = (bf16[64,512]{1,0:T(8,128)(2,1)S(1)}, bf16[64,512]{1,0:T(8,128)(2,1)}, u32[]{:S(2)}) copy-start(bf16[64,512]{1,0:T(8,128)(2,1)} %param.8) | copy-start | bytes 196612
  1.7 29.0 %all-to-all-start = ((bf16[8,64,512]{2,1,0:T(8,128)(2,1)}), bf16[8,64,512]{2,1,0:T(8,128)(2,1)S(1)}, u32[]{:S(2)}, u32[]{:S(2)}) async-start(bf16[8,64,512]{2,1,0:T(8,128)(2,1)} %broadcast_in_dim.10), calls=%async_computation | async-start | bytes 1048576 | tf_op jit(solution)/shard_map/all_to_all | solution.py:179
  18.9 4.0 %copy-start = (f32[16,512]{1,0:T(8,128)S(1)}, f32[16,512]{1,0:T(8,128)}, u32[]{:S(2)}) copy-start(f32[16,512]{1,0:T(8,128)} %rate_ref.1) | copy-start | bytes 98308
  18.9 4.0 %copy-start.1 = (f32[16,512]{1,0:T(8,128)S(1)}, f32[16,512]{1,0:T(8,128)}, u32[]{:S(2)}) copy-start(f32[16,512]{1,0:T(8,128)} %residue_ref.1) | copy-start | bytes 98308
  22.9 0.7 copy-start.2
  30.6 23.8 %collective-permute-start = (bf16[8,64,512]{2,1,0:T(8,128)(2,1)S(1)}, bf16[8,64,512]{2,1,0:T(8,128)(2,1)S(1)}, u32[]{:S(2)}, u32[]{:S(2)}) collective-permute-start(bf16[8,64,512]{2,1,0:T(8,128)(2,1)S(1)} %all-to-all-done.near_ref), channel_id=1, source_target_pairs={{0,32},{32,0},{1,33},{33,1},{2,34},{34,2},{3,35},{35,3},{4,36},{36... | collective-permute-start | bytes 1572872 | tf_op jit(solution)/shard_map/ppermute | solution.py:222

commit v16 on v15

--- a/solution.py
+++ b/solution.py
@@ -141,14 +141,15 @@
     lax.fori_loop(0, width // LANES, slab, 0)
 
 
-def project_kernel(gated_ref, near_ref, far_ref, out_ref):
+def project_kernel(gated_ref, near_ref, far_ref, last_ref, out_ref):
     cores, shared, rows, half = gated_ref.shape
     gated = [gated_ref[core].reshape(shared * rows, half) for core in range(cores)]
     for j in range(out_ref.shape[1]):
+        ref, k = (far_ref, j) if j < far_ref.shape[0] else (last_ref, j - far_ref.shape[0])
         total = 0.0
         for core in range(cores):
             depth = slice(core * half, (core + 1) * half)
-            weight = jnp.concatenate([near_ref[j, :, depth], far_ref[j, :, depth]], axis=0)
+            weight = jnp.concatenate([near_ref[j, :, depth], ref[k, :, depth]], axis=0)
             total = total + lax.dot_general(
                 gated[core], weight, (((1,), (1,)), ((), ())), preferred_element_type=F32
             )
@@ -219,7 +220,9 @@
         name="total",
     )(states, rate)
     total, near = lax.optimization_barrier((total, near))
-    far = lax.ppermute(near, "xh", [(0, 1), (1, 0)])
+    far = [
+        lax.ppermute(part, "xh", [(0, 1), (1, 0)]) for part in jnp.split(near, 2, axis=0)
+    ]
     totals = exchange(total, "z")
     gated = pl.pallas_call(
         gate_kernel,
@@ -234,11 +237,11 @@
     parts = pl.pallas_call(
         project_kernel,
         out_shape=jax.ShapeDtypeStruct((blocks, y_size) + piece, BF16),
-        in_specs=[VMEM] * 3,
+        in_specs=[VMEM] * 4,
         out_specs=VMEM,
         compiler_params=PARAMS,
         name="project",
-    )(gated, near, far)
+    )(gated, near, *far)
     parts = exchange(parts.reshape((y_size * blocks,) + piece), ("xl", "core", "chan"))
     return pl.pallas_call(
         sum_kernel,

time: 80 us -> 81.3 us (1.016)
  blocking collectives: 57.2 us -> 45.8 us
  starting transfers between devices: 15.6 us -> 24.1 us
  waiting for transfers between devices: 0.36 us -> 3.76 us
    all_to_all x2 -> x1, blocking collectives: 37.3 us -> 26 us  [exchange(): return lax.all_to_all(x, axes, 0, 0, tiled=True)]
    all_to_all x1 -> x2, starting transfers between devices: 11 us -> 17.3 us  [exchange(): return lax.all_to_all(x, axes, 0, 0, tiled=True)]
    ppermute x1 -> x2, waiting for transfers between devices: 0.01 us -> 2.67 us  [body(): lax.ppermute(part, 'xh', [(0, 1), (1, 0)])]
    ppermute x1 -> x2, starting transfers between devices: 4.64 us -> 6.79 us  [body(): lax.ppermute(part, 'xh', [(0, 1), (1, 0)])]
  transfers between devices with their start and end apart: 2 -> 4, of which waited for: 1 -> 2; matrix products, arithmetic and copies ran while one was open for 0% -> 0% of each run, Pallas kernels for 3% -> 4%
where the time goes in v16:
time: 81.3 us; the launch traced here: 80.5 us
  blocking collectives  45.8 us (56%)
  starting transfers between devices  24.1 us (30%)
  Pallas kernels  4.32 us (5%)
  waiting for transfers between devices  3.76 us (5%)
  local copies, waits for them, and re-layouts  2.41 us (3%)
    all_to_all x1, blocking collectives, exchange(): return lax.all_to_all(x, axes, 0, 0, tiled=True)  26 us
    all_to_all x2, starting transfers between devices, exchange(): return lax.all_to_all(x, axes, 0, 0, tiled=True)  17.3 us
    all_gather x2, blocking collectives, body(): inputs = lax.all_gather(lax.all_gather(inputs, 'xl'), 'core')  10.1 us
    ppermute x2, starting transfers between devices, body(): lax.ppermute(part, 'xh', [(0, 1), (1, 0)])  6.79 us
    all_gather x1, blocking collectives, body(): states = lax.all_gather(state, 'xh')  5.07 us
    all_gather x1, blocking collectives, body(): gated = lax.all_gather(gated, 'core')  4.59 us
    ppermute x2, waiting for transfers between devices, body(): lax.ppermute(part, 'xh', [(0, 1), (1, 0)])  2.67 us
    broadcast_in_dim x1, local copies, waits for them, and re-layouts, body(): own_weight = jnp.broadcast_to(out_weight.T[None], (z_size, out_cols, width))  1.68 us
  transfers between devices with their start and end apart: 4, of which 2 were waited for; matrix products, arithmetic and copies ran while one was open for 0% of the time, Pallas kernels for 4%

profile of v16, /device:TPU:1, one launch (start us, length us, event | category | flops | bytes accessed | tf_op | source)
XLA Modules:
  0.0 80.5 jit_solution(13437826691284918631)
XLA Ops:
  0.0 1.7 %broadcast_in_dim.10 = bf16[8,64,512]{2,1,0:T(8,128)(2,1)} broadcast(bf16[64,512]{1,0:T(8,128)(2,1)} %bitcast.20), dimensions={1,2} | broadcast | bytes 589824 | tf_op jit(solution)/shard_map/broadcast_in_dim | solution.py:191
  1.7 11.0 %all-to-all-start = ((bf16[8,64,512]{2,1,0:T(8,128)(2,1)}), bf16[8,64,512]{2,1,0:T(8,128)(2,1)S(1)}, u32[]{:S(2)}, u32[]{:S(2)}) async-start(bf16[8,64,512]{2,1,0:T(8,128)(2,1)} %broadcast_in_dim.10), calls=%async_computation | async-start | bytes 1048576 | tf_op jit(solution)/shard_map/all_to_all | solution.py:180
  12.7 0.0 copy-done.3
  12.7 0.0 copy-done.4
  12.7 0.0 copy-done.5
  12.7 6.1 %all-gather = bf16[6,64,512]{2,1,0:T(8,128)(2,1)S(1)} all-gather(bf16[3,64,512]{2,1,0:T(8,128)(2,1)S(1)} %pad_maximum_fusion), channel_id=2, replica_groups=mesh['z'=8,'xh'=2,'xl'=2,'core'=2,'chan'=8] {'xl'}, dimensions={0}, use_global_device_ids=true | all-gather | bytes 589824 | tf_op jit(solution)/shard_map/all_gather | solution.py:194
  18.9 4.0 %all-gather.1 = bf16[4,3,64,512]{3,2,1,0:T(8,128)(2,1)S(1)} all-gather(bf16[2,3,64,512]{3,2,1,0:T(8,128)(2,1)S(1)} %bitcast.19), channel_id=3, replica_groups=mesh['z'=8,'xh'=2,'xl'=2,'core'=2,'chan'=8] {'core'}, dimensions={0}, use_global_device_ids=true | all-gather | bytes 1179648 | tf_op jit(solution)/shard_map/all_gather | solution.py:194
  22.9 0.0 copy-done
  22.9 0.7 copy-done.2
  23.5 1.7 %chunk.1 = (f32[4,64,256]{2,1,0:T(8,128)S(1)}, f32[4,16,256]{2,1,0:T(8,128)S(1)}, f32[16,256]{1,0:T(8,128)S(1)}, f32[16,256]{1,0:T(8,128)S(1)}, f32[16,256]{1,0:T(8,128)S(1)}) custom-call(bf16[2,2,3,64,512]{4,3,2,1,0:T(8,128)(2,1)S(1)} %bitcast.11, f32[16,512]{1,0:T(8,128)S(1)} %copy-done, f32[16,512]{1,0:T(8,128)S(1)} %copy-done.1, f32[1,512]{1,0:T(1,128)S(1)} %bitcast.18), custom_call_target="tpu_custom_call" | custom-call | tf_op jit(solution)/shard_map/chunk/pallas_call | solution.py:195
  25.2 5.1 %all-gather.2 = f32[32,256]{1,0:T(8,128)S(1)} all-gather(f32[16,256]{1,0:T(8,128)S(1)} %get-tuple-element.12), channel_id=4, replica_groups=mesh['z'=8,'xh'=2,'xl'=2,'core'=2,'chan'=8] {'xh'}, dimensions={0}, use_global_device_ids=true | all-gather | bytes 49152 | tf_op jit(solution)/shard_map/all_gather | solution.py:213
  30.3 0.7 total.1
  30.9 0.0 all-to-all-done.near_ref
  30.9 6.3 %all-to-all-start.1 = ((f32[8,16,256]{2,1,0:T(8,128)}), f32[8,16,256]{2,1,0:T(8,128)S(1)}, u32[]{:S(2)}, u32[]{:S(2)}) async-start(f32[8,16,256]{2,1,0:T(8,128)} %total.1), calls=%async_computation.1 | async-start | bytes 262144 | tf_op jit(solution)/shard_map/all_to_all | solution.py:180
  37.3 4.7 %collective-permute-start.1 = (bf16[4,64,512]{2,1,0:T(8,128)(2,1)S(1)}, bf16[4,64,512]{2,1,0:T(8,128)(2,1)S(1)}, u32[]{:S(2)}, u32[]{:S(2)}) collective-permute-start(bf16[4,64,512]{2,1,0:T(8,128)(2,1)S(1)} %get-tuple-element.19), channel_id=1, source_target_pairs={{0,32},{32,0},{1,33},{33,1},{2,34},{34,2},{3,35},{35,3},{4,36},{36... | collective-permute-start | bytes 786440 | tf_op jit(solution)/shard_map/ppermute | solution.py:224
  42.0 2.1 %collective-permute-start = (bf16[4,64,512]{2,1,0:T(8,128)(2,1)S(1)}, bf16[4,64,512]{2,1,0:T(8,128)(2,1)S(1)}, u32[]{:S(2)}, u32[]{:S(2)}) collective-permute-start(bf16[4,64,512]{2,1,0:T(8,128)(2,1)S(1)} %get-tuple-element.20), channel_id=1, source_target_pairs={{0,32},{32,0},{1,33},{33,1},{2,34},{34,2},{3,35},{35,3},{4,36},{36... | collective-permute-start | bytes 786440 | tf_op jit(solution)/shard_map/ppermute | solution.py:224
  44.1 1.1 %all-to-all-done.1.totals_ref = f32[8,16,256]{2,1,0:T(8,128)S(1)} async-done(((f32[8,16,256]{2,1,0:T(8,128)}), f32[8,16,256]{2,1,0:T(8,128)S(1)}, u32[]{:S(2)}, u32[]{:S(2)}) %all-to-all-start.1) | async-done | bytes 131104 | tf_op jit(solution)/shard_map/all_to_all | solution.py:180
  45.2 0.5 gate.1
  45.7 4.6 %all-gather.3 = bf16[8,64,256]{2,1,0:T(8,128)(2,1)S(1)} all-gather(bf16[4,64,256]{2,1,0:T(8,128)(2,1)S(1)} %gate.1), channel_id=5, replica_groups=mesh['z'=8,'xh'=2,'xl'=2,'core'=2,'chan'=8] {'core'}, dimensions={0}, use_global_device_ids=true | all-gather | bytes 393216 | tf_op jit(solution)/shard_map/all_gather | solution.py:235
  50.3 0.0 collective-permute-done.1.last_ref
  50.3 2.7 %collective-permute-done.far_ref = bf16[4,64,512]{2,1,0:T(8,128)(2,1)S(1)} collective-permute-done((bf16[4,64,512]{2,1,0:T(8,128)(2,1)S(1)}, bf16[4,64,512]{2,1,0:T(8,128)(2,1)S(1)}, u32[]{:S(2)}, u32[]{:S(2)}) %collective-permute-start) | collective-permute-done | bytes 262176 | tf_op jit(solution)/shard_map/ppermute | solution.py:224
  53.0 0.7 project.1
  53.7 26.0 %all_to_all.15 = bf16[32,64,128]{2,1,0:T(8,128)(2,1)S(1)} all-to-all(bf16[32,64,128]{2,1,0:T(8,128)(2,1)S(1)} %bitcast.13), channel_id=1, replica_groups=mesh['z'=8,'xh'=2,'xl'=2,'core'=2,'chan'=8] {'xl','core','chan'}, dimensions={0} | all-to-all | bytes 1048576 | tf_op jit(solution)/shard_map/all_to_all | solution.py:180
  79.7 0.8 sum_parts.1
  (9 shorter events, 0.1 us)
Async XLA Ops:
  1.7 11.0 %copy-start.3 = (bf16[64,512]{1,0:T(8,128)(2,1)S(1)}, bf16[64,512]{1,0:T(8,128)(2,1)}, u32[]{:S(2)}) copy-start(bf16[64,512]{1,0:T(8,128)(2,1)} %param.7) | copy-start | bytes 196612
  1.7 11.0 %copy-start.4 = (bf16[64,512]{1,0:T(8,128)(2,1)S(1)}, bf16[64,512]{1,0:T(8,128)(2,1)}, u32[]{:S(2)}) copy-start(bf16[64,512]{1,0:T(8,128)(2,1)} %param.9) | copy-start | bytes 196612
  1.7 11.0 %copy-start.5 = (bf16[64,512]{1,0:T(8,128)(2,1)S(1)}, bf16[64,512]{1,0:T(8,128)(2,1)}, u32[]{:S(2)}) copy-start(bf16[64,512]{1,0:T(8,128)(2,1)} %param.8) | copy-start | bytes 196612
  1.7 29.2 %all-to-all-start = ((bf16[8,64,512]{2,1,0:T(8,128)(2,1)}), bf16[8,64,512]{2,1,0:T(8,128)(2,1)S(1)}, u32[]{:S(2)}, u32[]{:S(2)}) async-start(bf16[8,64,512]{2,1,0:T(8,128)(2,1)} %broadcast_in_dim.10), calls=%async_computation | async-start | bytes 1048576 | tf_op jit(solution)/shard_map/all_to_all | solution.py:180
  18.9 4.0 %copy-start = (f32[16,512]{1,0:T(8,128)S(1)}, f32[16,512]{1,0:T(8,128)}, u32[]{:S(2)}) copy-start(f32[16,512]{1,0:T(8,128)} %rate_ref.1) | copy-start | bytes 98308
  18.9 4.0 %copy-start.1 = (f32[16,512]{1,0:T(8,128)S(1)}, f32[16,512]{1,0:T(8,128)}, u32[]{:S(2)}) copy-start(f32[16,512]{1,0:T(8,128)} %residue_ref.1) | copy-start | bytes 98308
  22.9 0.7 copy-start.2
  30.9 14.3 %all-to-all-start.1 = ((f32[8,16,256]{2,1,0:T(8,128)}), f32[8,16,256]{2,1,0:T(8,128)S(1)}, u32[]{:S(2)}, u32[]{:S(2)}) async-start(f32[8,16,256]{2,1,0:T(8,128)} %total.1), calls=%async_computation.1 | async-start | bytes 262144 | tf_op jit(solution)/shard_map/all_to_all | solution.py:180
  37.3 13.0 %collective-permute-start.1 = (bf16[4,64,512]{2,1,0:T(8,128)(2,1)S(1)}, bf16[4,64,512]{2,1,0:T(8,128)(2,1)S(1)}, u32[]{:S(2)}, u32[]{:S(2)}) collective-permute-start(bf16[4,64,512]{2,1,0:T(8,128)(2,1)S(1)} %get-tuple-element.19), channel_id=1, source_target_pairs={{0,32},{32,0},{1,33},{33,1},{2,34},{34,2},{3,35},{35,3},{4,36},{36... | collective-permute-start | bytes 786440 | tf_op jit(solution)/shard_map/ppermute | solution.py:224
  42.0 11.0 %collective-permute-start = (bf16[4,64,512]{2,1,0:T(8,128)(2,1)S(1)}, bf16[4,64,512]{2,1,0:T(8,128)(2,1)S(1)}, u32[]{:S(2)}, u32[]{:S(2)}) collective-permute-start(bf16[4,64,512]{2,1,0:T(8,128)(2,1)S(1)} %get-tuple-element.20), channel_id=1, source_target_pairs={{0,32},{32,0},{1,33},{33,1},{2,34},{34,2},{3,35},{35,3},{4,36},{36... | collective-permute-start | bytes 786440 | tf_op jit(solution)/shard_map/ppermute | solution.py:224

commit v17 on v15

--- a/solution.py
+++ b/solution.py
@@ -19,11 +19,11 @@
 
 
 def chunk_kernel(
-    inputs_ref, rate_ref, residue_ref, skip_ref,
+    inputs_ref, filters_ref,
     base_ref, before_ref, send_ref, amp_ref, copy_ref, signal_ref, state_ref,
 ):
     blocks, rows, width = base_ref.shape
-    modes = rate_ref.shape[0]
+    modes = amp_ref.shape[0]
     tiles = rows // 8
     cores = inputs_ref.shape[0]
     first_col = lax.axis_index("core") * width
@@ -34,8 +34,8 @@
         for i in range(blocks):
             key = inputs_ref[i % cores, i // cores, 0, :, source].astype(F32)
             signal_ref[i] = key * inputs_ref[i % cores, i // cores, 1, :, source].astype(F32)
-        rate = rate_ref[:, source]
-        amp = residue_ref[:, source] * jnp.sqrt(1.0 - jnp.exp(-2.0 * rate))
+        rate = filters_ref[:modes, source]
+        amp = filters_ref[modes : 2 * modes, source] * jnp.sqrt(1.0 - jnp.exp(-2.0 * rate))
         amp_ref[:, cols] = amp
         copy_ref[:, cols] = rate
         steps = [jnp.exp(-8.0 * j * rate) for j in range(tiles)]
@@ -60,7 +60,7 @@
             running = decay * running + state_ref[i]
         send_ref[:, cols] = running
         row_ids = lax.broadcasted_iota(jnp.int32, (rows, LANES), 0)
-        skip = skip_ref[0:1, source]
+        skip = filters_ref[2 * modes : 2 * modes + 1, source]
 
         def block(i, inner):
             signal = signal_ref[i]
@@ -190,6 +190,8 @@
     own_weight = jnp.broadcast_to(out_weight.T[None], (z_size, out_cols, width))
     near = exchange(own_weight, "z")
     inputs = jnp.stack([key_input, value_input, gate_input])
+    filters = jnp.concatenate([decay_rate, residue, skip_gain[None, :]], axis=0)
+    inputs, filters = lax.optimization_barrier((inputs, filters))
     inputs = lax.all_gather(lax.all_gather(inputs, "xl"), "core")
     base, before, state, amplitude, rate = pl.pallas_call(
         chunk_kernel,
@@ -200,7 +202,7 @@
             jax.ShapeDtypeStruct((modes, half), F32),
             jax.ShapeDtypeStruct((modes, half), F32),
         ),
-        in_specs=[VMEM] * 4,
+        in_specs=[VMEM] * 2,
         out_specs=(VMEM,) * 5,
         scratch_shapes=[
             pltpu.VMEM((blocks, rows, LANES), F32),
@@ -208,7 +210,7 @@
         ],
         compiler_params=PARAMS,
         name="chunk",
-    )(inputs, decay_rate, residue, skip_gain[None, :])
+    )(inputs, filters)
     states = lax.all_gather(state, "xh")
     total = pl.pallas_call(
         lambda *refs: total_kernel(rows * blocks, *refs),

time: 80 us -> 80 us (level)
  no operation moved by 1% of the time
where the time goes in v17:
time: 80 us; the launch traced here: 79.4 us
  blocking collectives  57.1 us (71%)
  starting transfers between devices  15.6 us (20%)
  Pallas kernels  3.65 us (5%)
  local copies, waits for them, and re-layouts  2.53 us (3%)
    all_to_all x2, blocking collectives, exchange(): return lax.all_to_all(x, axes, 0, 0, tiled=True)  37.3 us
    all_to_all x1, starting transfers between devices, exchange(): return lax.all_to_all(x, axes, 0, 0, tiled=True)  11 us
    all_gather x2, blocking collectives, body(): inputs = lax.all_gather(lax.all_gather(inputs, 'xl'), 'core')  9.98 us
    all_gather x1, blocking collectives, body(): states = lax.all_gather(state, 'xh')  5.07 us
    all_gather x1, blocking collectives, body(): gated = lax.all_gather(gated, 'core')  4.77 us
    ppermute x1, starting transfers between devices, body(): far = lax.ppermute(near, 'xh', [(0, 1), (1, 0)])  4.64 us
    broadcast_in_dim x1, local copies, waits for them, and re-layouts, body(): own_weight = jnp.broadcast_to(out_weight.T[None], (z_size, out_cols, width))  1.68 us
    pallas_call x1, Pallas kernels, body(): pl.pallas_call(chunk_kernel, out_shape=(jax.ShapeDtypeStruct((blocks, row...  1.63 us
  transfers between devices with their start and end apart: 2, of which 1 were waited for; matrix products, arithmetic and copies ran while one was open for 0% of the time, Pallas kernels for 3%

profile of v17, /device:TPU:1, one launch (start us, length us, event | category | flops | bytes accessed | tf_op | source)
XLA Modules:
  0.0 79.4 jit_solution(4652885930868667630)
XLA Ops:
  0.0 1.7 %broadcast_in_dim.10 = bf16[8,64,512]{2,1,0:T(8,128)(2,1)} broadcast(bf16[64,512]{1,0:T(8,128)(2,1)} %bitcast.19), dimensions={1,2} | broadcast | bytes 589824 | tf_op jit(solution)/shard_map/broadcast_in_dim | solution.py:190
  1.7 0.0 copy-start.3
  1.7 11.0 %all-to-all-start = ((bf16[8,64,512]{2,1,0:T(8,128)(2,1)}), bf16[8,64,512]{2,1,0:T(8,128)(2,1)S(1)}, u32[]{:S(2)}, u32[]{:S(2)}) async-start(bf16[8,64,512]{2,1,0:T(8,128)(2,1)} %broadcast_in_dim.10), calls=%async_computation | async-start | bytes 1048576 | tf_op jit(solution)/shard_map/all_to_all | solution.py:179
  12.7 0.0 copy-done.3
  12.7 0.0 copy-done.4
  12.7 0.0 copy-done.5
  12.7 0.0 copy-start
  12.7 0.0 copy-start.1
  12.8 0.0 copy-done.2
  12.8 0.8 copy-done
  13.6 0.0 copy-done.1
  13.6 6.1 %all-gather = bf16[6,64,512]{2,1,0:T(8,128)(2,1)S(1)} all-gather(bf16[3,64,512]{2,1,0:T(8,128)(2,1)S(1)} %pad_maximum_fusion), channel_id=2, replica_groups=mesh['z'=8,'xh'=2,'xl'=2,'core'=2,'chan'=8] {'xl'}, dimensions={0}, use_global_device_ids=true | all-gather | bytes 589824 | tf_op jit(solution)/shard_map/all_gather | solution.py:195
  19.8 3.8 %all-gather.1 = bf16[4,3,64,512]{3,2,1,0:T(8,128)(2,1)S(1)} all-gather(bf16[2,3,64,512]{3,2,1,0:T(8,128)(2,1)S(1)} %bitcast.18), channel_id=3, replica_groups=mesh['z'=8,'xh'=2,'xl'=2,'core'=2,'chan'=8] {'core'}, dimensions={0}, use_global_device_ids=true | all-gather | bytes 1179648 | tf_op jit(solution)/shard_map/all_gather | solution.py:195
  23.6 1.6 %chunk.1 = (f32[4,64,256]{2,1,0:T(8,128)S(1)}, f32[4,16,256]{2,1,0:T(8,128)S(1)}, f32[16,256]{1,0:T(8,128)S(1)}, f32[16,256]{1,0:T(8,128)S(1)}, f32[16,256]{1,0:T(8,128)S(1)}) custom-call(bf16[2,2,3,64,512]{4,3,2,1,0:T(8,128)(2,1)S(1)} %bitcast.11, f32[33,512]{1,0:T(8,128)S(1)} %pad_maximum_fusion.1.filters_ref), custom_call_target="tpu_custom_call" | custom-call | tf_op jit(solution)/shard_map/chunk/pallas_call | solution.py:196
  25.2 5.1 %all-gather.2 = f32[32,256]{1,0:T(8,128)S(1)} all-gather(f32[16,256]{1,0:T(8,128)S(1)} %get-tuple-element.16), channel_id=4, replica_groups=mesh['z'=8,'xh'=2,'xl'=2,'core'=2,'chan'=8] {'xh'}, dimensions={0}, use_global_device_ids=true | all-gather | bytes 49152 | tf_op jit(solution)/shard_map/all_gather | solution.py:214
  30.3 0.3 all-to-all-done.near_ref
  30.7 4.6 %collective-permute-start = (bf16[8,64,512]{2,1,0:T(8,128)(2,1)S(1)}, bf16[8,64,512]{2,1,0:T(8,128)(2,1)S(1)}, u32[]{:S(2)}, u32[]{:S(2)}) collective-permute-start(bf16[8,64,512]{2,1,0:T(8,128)(2,1)S(1)} %all-to-all-done.near_ref), channel_id=1, source_target_pairs={{0,32},{32,0},{1,33},{33,1},{2,34},{34,2},{3,35},{35,3},{4,36},{36... | collective-permute-start | bytes 1572872 | tf_op jit(solution)/shard_map/ppermute | solution.py:224
  35.3 13.9 %all_to_all.15.totals_ref = f32[8,16,256]{2,1,0:T(8,128)S(1)} all-to-all(f32[8,16,256]{2,1,0:T(8,128)S(1)} %total.1), channel_id=1, replica_groups=mesh['z'=8,'xh'=2,'xl'=2,'core'=2,'chan'=8] {'z'}, dimensions={0} | all-to-all | bytes 262144 | tf_op jit(solution)/shard_map/all_to_all | solution.py:179
  49.2 0.5 gate.1
  49.7 4.8 %all-gather.3 = bf16[8,64,256]{2,1,0:T(8,128)(2,1)S(1)} all-gather(bf16[4,64,256]{2,1,0:T(8,128)(2,1)S(1)} %gate.1), channel_id=5, replica_groups=mesh['z'=8,'xh'=2,'xl'=2,'core'=2,'chan'=8] {'core'}, dimensions={0}, use_global_device_ids=true | all-gather | bytes 393216 | tf_op jit(solution)/shard_map/all_gather | solution.py:234
  54.5 0.0 collective-permute-done.far_ref
  54.5 0.7 project.1
  55.2 23.4 %all_to_all.16 = bf16[32,64,128]{2,1,0:T(8,128)(2,1)S(1)} all-to-all(bf16[32,64,128]{2,1,0:T(8,128)(2,1)S(1)} %bitcast.13), channel_id=1, replica_groups=mesh['z'=8,'xh'=2,'xl'=2,'core'=2,'chan'=8] {'xl','core','chan'}, dimensions={0} | all-to-all | bytes 1048576 | tf_op jit(solution)/shard_map/all_to_all | solution.py:179
  78.6 0.8 sum_parts.1
  (6 shorter events, 0.1 us)
Async XLA Ops:
  1.7 11.0 %copy-start.3 = (f32[16,512]{1,0:T(8,128)S(1)}, f32[16,512]{1,0:T(8,128)}, u32[]{:S(2)}) copy-start(f32[16,512]{1,0:T(8,128)} %param.11) | copy-start | bytes 98308
  1.7 11.0 %copy-start.4 = (f32[16,512]{1,0:T(8,128)S(1)}, f32[16,512]{1,0:T(8,128)}, u32[]{:S(2)}) copy-start(f32[16,512]{1,0:T(8,128)} %param.10) | copy-start | bytes 98308
  1.7 11.0 %copy-start.5 = (f32[512]{0:T(512)S(1)}, f32[512]{0:T(512)}, u32[]{:S(2)}) copy-start(f32[512]{0:T(512)} %param.12) | copy-start | bytes 6148
  1.7 11.1 %copy-start.2 = (bf16[64,512]{1,0:T(8,128)(2,1)S(1)}, bf16[64,512]{1,0:T(8,128)(2,1)}, u32[]{:S(2)}) copy-start(bf16[64,512]{1,0:T(8,128)(2,1)} %param.8) | copy-start | bytes 196612
  1.7 29.0 %all-to-all-start = ((bf16[8,64,512]{2,1,0:T(8,128)(2,1)}), bf16[8,64,512]{2,1,0:T(8,128)(2,1)S(1)}, u32[]{:S(2)}, u32[]{:S(2)}) async-start(bf16[8,64,512]{2,1,0:T(8,128)(2,1)} %broadcast_in_dim.10), calls=%async_computation | async-start | bytes 1048576 | tf_op jit(solution)/shard_map/all_to_all | solution.py:179
  12.7 0.8 %copy-start = (bf16[64,512]{1,0:T(8,128)(2,1)S(1)}, bf16[64,512]{1,0:T(8,128)(2,1)}, u32[]{:S(2)}) copy-start(bf16[64,512]{1,0:T(8,128)(2,1)} %param.7) | copy-start | bytes 196612
  12.7 0.9 %copy-start.1 = (bf16[64,512]{1,0:T(8,128)(2,1)S(1)}, bf16[64,512]{1,0:T(8,128)(2,1)}, u32[]{:S(2)}) copy-start(bf16[64,512]{1,0:T(8,128)(2,1)} %param.9) | copy-start | bytes 196612
  30.7 23.8 %collective-permute-start = (bf16[8,64,512]{2,1,0:T(8,128)(2,1)S(1)}, bf16[8,64,512]{2,1,0:T(8,128)(2,1)S(1)}, u32[]{:S(2)}, u32[]{:S(2)}) collective-permute-start(bf16[8,64,512]{2,1,0:T(8,128)(2,1)S(1)} %all-to-all-done.near_ref), channel_id=1, source_target_pairs={{0,32},{32,0},{1,33},{33,1},{2,34},{34,2},{3,35},{35,3},{4,36},{36... | collective-permute-start | bytes 1572872 | tf_op jit(solution)/shard_map/ppermute | solution.py:224
